TPU v7x, 32 devices: a whole 2x2x4 slice. The times are simulated.
32 devices in a mesh: track: 8 (over y, x, core), strip: 4 (over z).
Axes of the slice: x: 2, y: 2, z: 4, core: 2. Of those that a mesh axis runs over, the one named last changes fastest.
Arguments:
- rhs: float32 [4, 128, 256], P('strip', 'track'), may hold values from -6 to 6
- principal_tiles: bfloat16 [4, 128, 256, 256], P('strip', 'track')
- lower_blocks: bfloat16 [4, 128, 256, 256], P('strip', 'track')
- coupling_blocks: bfloat16 [4, 128, 256, 256], P('strip', 'track'), may hold values from -0.09375 to 0.09375
- precond_blocks: bfloat16 [4, 128, 256, 256], P('strip', 'track'), as said below
- seg_blocks: int32 [8], P('track'), may hold values from 1 to 16, 80 in all
- links: int32 [4, 128], P('strip', 'track'), may hold values 0 or 1
Outputs:
- solution: float32 [4, 128, 256], P('strip', 'track')
- residual: float32 [4, 128, 256], P('strip', 'track')
Inputs may be any that keep to these rules, and one draw needn't show every extreme that they name: `seg_blocks`: each device holds at least one live block and the counts of all devices sum to 80. `precond_blocks`: approximate inverses of the diagonal blocks.
All inputs are finite; a program needn't handle non-finite values. No bound on the sum of `links` on one device may be relied on, other than what follows from the above.
Results may differ from a plain program's by a relative error of at most 0.0004.
Values sent between devices are 32-bit elements; how exact they have to be, the bound alone decides.
No kernel may reach another device: no remote copies, remote signals or barrier semaphores. Data moves between devices by JAX's collectives and lax.ppermute only.
A program may use at most 128 MiB of HBM per device.

v0:
```python
import jax
import jax.numpy as jnp
from jax import lax
from jax.sharding import PartitionSpec as P

ITERS = 6


def carried_in(value, axis, join, neutral):
    count, mine = (lax.axis_size(axis), lax.axis_index(axis))
    pieces = jax.tree.map(lambda part: lax.all_gather(part, axis), value)
    so_far = jax.tree.map(
        lambda part, zero: jnp.full_like(part, 0) + jnp.asarray(zero, part.dtype), value, neutral
    )

    def turn(position, so_far):
        longer = join(so_far, jax.tree.map(lambda part: part[position], pieces))
        return jax.tree.map(lambda new, old: jnp.where(position < mine, new, old), longer, so_far)

    return lax.fori_loop(0, count - 1, turn, so_far)


def padded(value, sides, width):
    for axis, dim in sides:
        size, length = (lax.axis_size(axis), value.shape[dim])
        up = [(i, (i + 1) % size) for i in range(size - 1)]
        down = [(j, i) for i, j in up]
        last = lax.slice_in_dim(value, length - width, length, axis=dim)
        first = lax.slice_in_dim(value, 0, width, axis=dim)
        before = lax.ppermute(last, axis, up)
        after = lax.ppermute(first, axis, down)
        value = jnp.concatenate([before, value, after], axis=dim)
    return value


def apply_blocks(mats, vecs):
    return jnp.einsum("kab,kb->ka", mats.astype(jnp.float32), vecs, precision=lax.Precision.HIGHEST)


def apply_transposed(mats, vecs):
    return jnp.einsum("kba,kb->ka", mats.astype(jnp.float32), vecs, precision=lax.Precision.HIGHEST)


def compose(earlier, later):
    matrix = jnp.dot(later[0], earlier[0], precision=lax.Precision.HIGHEST)
    vector = jnp.dot(later[0], earlier[1], precision=lax.Precision.HIGHEST) + later[1]
    return (matrix, vector)


def body(rhs, principal_tiles, lower_blocks, coupling_blocks, precond_blocks, seg_blocks, links):
    cap = rhs.shape[1]
    width = rhs.shape[2]
    track_idx = lax.axis_index("track")
    count = seg_blocks[0]
    slots = jnp.arange(cap, dtype=jnp.int32)
    live = (slots < count).astype(jnp.float32)
    link_live = links[0].astype(jnp.float32) * live
    linked = link_live * jnp.where((slots > 0) | (track_idx > 0), 1.0, 0.0)
    diag = principal_tiles[0]
    lower = lower_blocks[0]
    coupling = coupling_blocks[0]
    precond = precond_blocks[0]
    ident = jnp.eye(width, dtype=jnp.float32)
    factors = -linked[:, None, None] * jnp.einsum(
        "kab,kbc->kac", precond, lower, preferred_element_type=jnp.float32
    )
    step_maps = jnp.where(live[:, None, None] > 0, factors, ident[None])
    level_count = (cap - 1).bit_length()
    slot_levels = []
    composed = step_maps
    for level in range(level_count):
        span = 1 << level
        slot_levels.append(composed)
        shifted_maps = jnp.concatenate(
            [jnp.broadcast_to(ident, (span, width, width)), composed[:-span]], axis=0
        )
        composed = jnp.einsum(
            "kab,kbc->kac", composed, shifted_maps, precision=lax.Precision.HIGHEST
        )
    last_map = composed[-1]
    zero_vec = jnp.zeros((width,), jnp.float32)
    solution = jnp.zeros((cap, width), jnp.float32)
    residual = rhs[0] * live[:, None]
    for step_number in range(ITERS):
        local = apply_blocks(precond, residual) * live[:, None]
        for precondition_level in range(level_count):
            precondition_span = 1 << precondition_level
            earlier = jnp.concatenate(
                [jnp.zeros((precondition_span, width), jnp.float32), local[:-precondition_span]],
                axis=0,
            )
            local = local + jnp.einsum(
                "kab,kb->ka",
                slot_levels[precondition_level],
                earlier,
                precision=lax.Precision.HIGHEST,
            )
        precondition_end_value = local[-1]
        before = carried_in((last_map, precondition_end_value), "track", compose, (ident, zero_vec))
        entry = before[1]
        carried = jnp.einsum("kab,b->ka", composed, entry, precision=lax.Precision.HIGHEST)
        direction = (local + carried) * live[:, None]
        last_value = lax.dynamic_index_in_dim(direction, count - 1, 0, keepdims=False)
        transposed = apply_transposed(lower, direction) * link_live[:, None]
        edges = jnp.stack([transposed[0], last_value])
        rims = padded(edges, (("track", 0),), 1)
        previous = jnp.concatenate([rims[0][None], direction[:-1]], axis=0)
        lowered = apply_blocks(lower, previous) * linked[:, None]
        at_end = jnp.where(slots == count - 1, 1.0, 0.0)[:, None]
        upper = (
            jnp.concatenate([transposed[1:], jnp.zeros((1, width), jnp.float32)], axis=0)
            + at_end * rims[3][None]
        )
        cross = jnp.stack([apply_transposed(coupling, direction), direction])
        strip_halo = padded(cross, (("strip", 0),), 1)
        total = (
            apply_blocks(diag, direction)
            + lowered
            + upper
            + apply_blocks(coupling, strip_halo[0])
            + strip_halo[3]
        )
        image = total * live[:, None]
        inner, energy = lax.psum(
            (jnp.sum(residual * image), jnp.sum(image * image)), ("track", "strip")
        )
        alpha = inner / (energy + 1e-06)
        solution = solution + alpha * direction
        residual = residual - alpha * image
    return (solution[None], residual[None])


def solution(mesh):
    in_specs = (
        P("strip", "track", None),
        P("strip", "track", None, None),
        P("strip", "track", None, None),
        P("strip", "track", None, None),
        P("strip", "track", None, None),
        P("track"),
        P("strip", "track"),
    )
    out_specs = (P("strip", "track", None), P("strip", "track", None))
    return jax.shard_map(body, mesh=mesh, in_specs=in_specs, out_specs=out_specs, check_vma=False)
```

profile of v0, /device:TPU:0, one launch (start us, length us, event | category | flops | bytes accessed | tf_op | source)
XLA Modules:
  0.0 704.5 jit_solution(4140964388149101801)
XLA Ops:
  13.1 5.0 fusion.24
  20.1 5.0 fusion.28
  27.1 5.3 fusion.32
  34.4 5.0 fusion.36
  42.2 3.5 fusion.112
  45.8 17.4 %fusion.203 = f32[16,1,256]{2,1,0:T(1,128)S(1)} fusion(f32[16,256,256]{2,1,0:T(8,128)} %copy-done.1, f32[16,256,1]{1,0,2:T(8,128)S(1)} %pad_bitcast_fusion.23), kind=kOutput, calls=%fused_computation.297 | convolution fusion | flops 12582912 | bytes 4227072 | tf_op jit(solution)/shard_map/kab,kb->ka/dot_general | solution.py:92
  63.2 3.6 fusion.201
  66.9 3.6 fusion.199
  70.5 3.6 fusion.197
  74.2 10.4 %all-gather = f32[8,1,256]{2,1,0:T(1,128)S(1)} all-gather(f32[1,1,256]{2,1,0:T(1,128)S(1)} %slice_bitcast_fusion.5), channel_id=1, replica_groups=mesh['track'=8,'strip'=4] {'track'}, dimensions={0}, use_global_device_ids=true | all-gather | bytes 9216 | tf_op jit(solution)/shard_map/all_gather | solution.py:11
  84.5 9.4 %while.84 = (s32[]{:T(128)}, f32[256]{0:T(256)S(1)}, s32[]{:T(128)}, f32[8,256,256]{2,1,0:T(8,128)}, f32[8,256]{1,0:T(8,128)S(1)}, /*index=5*/s32[]{:T(128)}, s32[]{:T(128)}) while((s32[]{:T(128)}, f32[256]{0:T(256)S(1)}, s32[]{:T(128)}, f32[8,256,256]{2,1,0:T(8,128)}, f32[8,256]{1,0:T(8,128)S(1)}, /*index=5*/s32[]{:T(128)}, ...), condition=%wide.region_1.2_spmd.clone, body=%wide.region_0.1_spmd.clone.sunk | while | flops 787460 | bytes 272998 | solution.py:20
  93.9 5.9 fusion.238
  106.8 4.5 collective-permute-start.2
  117.3 42.2 %all-reduce.35 = (f32[]{:T(128)}, f32[]{:T(128)}) all-reduce(f32[]{:T(128)} %get-tuple-element.691, f32[]{:T(128)} %get-tuple-element.690), channel_id=1, replica_groups=mesh['track'=8,'strip'=4] {'track','strip'}, use_global_device_ids=true, to_apply=%region_3.4 | all-reduce | flops 2 | bytes 16 | tf_op jit(solution)/shard_map/psum | solution.py:124
  160.8 3.5 fusion.109
  164.4 5.8 fusion.192
  170.3 3.6 fusion.190
  173.9 3.6 fusion.188
  177.6 3.6 fusion.186
  181.2 9.8 %all-gather.1 = f32[8,1,256]{2,1,0:T(1,128)S(1)} all-gather(f32[1,1,256]{2,1,0:T(1,128)S(1)} %slice_bitcast_fusion.4), channel_id=1, replica_groups=mesh['track'=8,'strip'=4] {'track'}, dimensions={0}, use_global_device_ids=true | all-gather | bytes 9216 | tf_op jit(solution)/shard_map/all_gather | solution.py:11
  191.0 9.4 %while.85 = (s32[]{:T(128)}, f32[256]{0:T(256)S(1)}, s32[]{:T(128)}, f32[8,256,256]{2,1,0:T(8,128)}, f32[8,256]{1,0:T(8,128)S(1)}, /*index=5*/s32[]{:T(128)}, s32[]{:T(128)}) while((s32[]{:T(128)}, f32[256]{0:T(256)S(1)}, s32[]{:T(128)}, f32[8,256,256]{2,1,0:T(8,128)}, f32[8,256]{1,0:T(8,128)S(1)}, /*index=5*/s32[]{:T(128)}, ...), condition=%wide.region_7.8_spmd.clone, body=%wide.region_6.7_spmd.clone.sunk | while | flops 787460 | bytes 272998 | solution.py:20
  200.4 5.9 fusion.239
  215.0 4.5 collective-permute-start.6
  223.8 42.8 %all-reduce.34 = (f32[]{:T(128)}, f32[]{:T(128)}) all-reduce(f32[]{:T(128)} %get-tuple-element.689, f32[]{:T(128)} %get-tuple-element.688), channel_id=1, replica_groups=mesh['track'=8,'strip'=4] {'track','strip'}, use_global_device_ids=true, to_apply=%region_9.10 | all-reduce | flops 2 | bytes 16 | tf_op jit(solution)/shard_map/psum | solution.py:124
  267.8 3.5 fusion.107
  271.4 5.8 fusion.181
  277.2 3.6 fusion.179
  280.9 3.6 fusion.177
  284.5 3.6 fusion.175
  288.2 10.1 %all-gather.2 = f32[8,1,256]{2,1,0:T(1,128)S(1)} all-gather(f32[1,1,256]{2,1,0:T(1,128)S(1)} %slice_bitcast_fusion.3), channel_id=1, replica_groups=mesh['track'=8,'strip'=4] {'track'}, dimensions={0}, use_global_device_ids=true | all-gather | bytes 9216 | tf_op jit(solution)/shard_map/all_gather | solution.py:11
  298.2 9.4 %while.86 = (s32[]{:T(128)}, f32[256]{0:T(256)S(1)}, s32[]{:T(128)}, f32[8,256,256]{2,1,0:T(8,128)}, f32[8,256]{1,0:T(8,128)S(1)}, /*index=5*/s32[]{:T(128)}, s32[]{:T(128)}) while((s32[]{:T(128)}, f32[256]{0:T(256)S(1)}, s32[]{:T(128)}, f32[8,256,256]{2,1,0:T(8,128)}, f32[8,256]{1,0:T(8,128)S(1)}, /*index=5*/s32[]{:T(128)}, ...), condition=%wide.region_13.14_spmd.clone, body=%wide.region_12.13_spmd.clone.sunk | while | flops 787460 | bytes 272998 | solution.py:20
  307.6 5.9 fusion.240
  322.2 4.5 collective-permute-start.10
  331.0 42.7 %all-reduce.33 = (f32[]{:T(128)}, f32[]{:T(128)}) all-reduce(f32[]{:T(128)} %get-tuple-element.687, f32[]{:T(128)} %get-tuple-element.686), channel_id=1, replica_groups=mesh['track'=8,'strip'=4] {'track','strip'}, use_global_device_ids=true, to_apply=%region_15.16 | all-reduce | flops 2 | bytes 16 | tf_op jit(solution)/shard_map/psum | solution.py:124
  374.9 3.5 fusion.105
  378.5 5.8 fusion.170
  384.4 3.6 fusion.168
  388.0 3.6 fusion.166
  391.7 3.6 fusion.164
  395.3 9.9 %all-gather.3 = f32[8,1,256]{2,1,0:T(1,128)S(1)} all-gather(f32[1,1,256]{2,1,0:T(1,128)S(1)} %slice_bitcast_fusion.2), channel_id=1, replica_groups=mesh['track'=8,'strip'=4] {'track'}, dimensions={0}, use_global_device_ids=true | all-gather | bytes 9216 | tf_op jit(solution)/shard_map/all_gather | solution.py:11
  405.2 9.4 %while.87 = (s32[]{:T(128)}, f32[256]{0:T(256)S(1)}, s32[]{:T(128)}, f32[8,256,256]{2,1,0:T(8,128)}, f32[8,256]{1,0:T(8,128)S(1)}, /*index=5*/s32[]{:T(128)}, s32[]{:T(128)}) while((s32[]{:T(128)}, f32[256]{0:T(256)S(1)}, s32[]{:T(128)}, f32[8,256,256]{2,1,0:T(8,128)}, f32[8,256]{1,0:T(8,128)S(1)}, /*index=5*/s32[]{:T(128)}, ...), condition=%wide.region_19.20_spmd.clone, body=%wide.region_18.19_spmd.clone.sunk | while | flops 787460 | bytes 272998 | solution.py:20
  414.6 5.9 fusion.241
  429.2 4.5 collective-permute-start.14
  438.0 42.9 %all-reduce.32 = (f32[]{:T(128)}, f32[]{:T(128)}) all-reduce(f32[]{:T(128)} %get-tuple-element.685, f32[]{:T(128)} %get-tuple-element.684), channel_id=1, replica_groups=mesh['track'=8,'strip'=4] {'track','strip'}, use_global_device_ids=true, to_apply=%region_21.22 | all-reduce | flops 2 | bytes 16 | tf_op jit(solution)/shard_map/psum | solution.py:124
  482.2 3.5 fusion.103
  485.7 5.8 fusion.159
  491.6 3.6 fusion.157
  495.2 3.6 fusion.155
  498.9 3.6 fusion.153
  502.5 9.8 %all-gather.4 = f32[8,1,256]{2,1,0:T(1,128)S(1)} all-gather(f32[1,1,256]{2,1,0:T(1,128)S(1)} %slice_bitcast_fusion.1), channel_id=1, replica_groups=mesh['track'=8,'strip'=4] {'track'}, dimensions={0}, use_global_device_ids=true | all-gather | bytes 9216 | tf_op jit(solution)/shard_map/all_gather | solution.py:11
  512.4 9.4 %while.88 = (s32[]{:T(128)}, f32[256]{0:T(256)S(1)}, s32[]{:T(128)}, f32[8,256,256]{2,1,0:T(8,128)}, f32[8,256]{1,0:T(8,128)S(1)}, /*index=5*/s32[]{:T(128)}, s32[]{:T(128)}) while((s32[]{:T(128)}, f32[256]{0:T(256)S(1)}, s32[]{:T(128)}, f32[8,256,256]{2,1,0:T(8,128)}, f32[8,256]{1,0:T(8,128)S(1)}, /*index=5*/s32[]{:T(128)}, ...), condition=%wide.region_25.26_spmd.clone, body=%wide.region_24.25_spmd.clone.sunk | while | flops 787460 | bytes 272998 | solution.py:20
  521.7 5.9 fusion.242
  536.3 4.5 collective-permute-start.18
  545.1 42.8 %all-reduce.31 = (f32[]{:T(128)}, f32[]{:T(128)}) all-reduce(f32[]{:T(128)} %get-tuple-element.683, f32[]{:T(128)} %get-tuple-element.682), channel_id=1, replica_groups=mesh['track'=8,'strip'=4] {'track','strip'}, use_global_device_ids=true, to_apply=%region_27.28 | all-reduce | flops 2 | bytes 16 | tf_op jit(solution)/shard_map/psum | solution.py:124
  589.1 3.5 fusion.101
  592.7 5.8 fusion.148
  598.6 3.6 fusion.146
  602.2 3.6 fusion.144
  605.9 3.6 fusion.142
  609.5 9.9 %all-gather.5 = f32[8,1,256]{2,1,0:T(1,128)S(1)} all-gather(f32[1,1,256]{2,1,0:T(1,128)S(1)} %slice_bitcast_fusion), channel_id=1, replica_groups=mesh['track'=8,'strip'=4] {'track'}, dimensions={0}, use_global_device_ids=true | all-gather | bytes 9216 | tf_op jit(solution)/shard_map/all_gather | solution.py:11
  619.4 9.4 %while.89 = (s32[]{:T(128)}, f32[256]{0:T(256)S(1)}, s32[]{:T(128)}, f32[8,256,256]{2,1,0:T(8,128)}, f32[8,256]{1,0:T(8,128)S(1)}, /*index=5*/s32[]{:T(128)}, s32[]{:T(128)}) while((s32[]{:T(128)}, f32[256]{0:T(256)S(1)}, s32[]{:T(128)}, f32[8,256,256]{2,1,0:T(8,128)}, f32[8,256]{1,0:T(8,128)S(1)}, /*index=5*/s32[]{:T(128)}, ...), condition=%wide.region_31.32_spmd.clone, body=%wide.region_30.31_spmd.clone.sunk | while | flops 787460 | bytes 272998 | solution.py:20
  628.8 5.9 fusion.243
  643.3 4.5 collective-permute-start.22
  652.1 42.6 %all-reduce.30 = (f32[]{:T(128)}, f32[]{:T(128)}) all-reduce(f32[]{:T(128)} %get-tuple-element.681, f32[]{:T(128)} %get-tuple-element.680), channel_id=1, replica_groups=mesh['track'=8,'strip'=4] {'track','strip'}, use_global_device_ids=true, to_apply=%region_33.34 | all-reduce | flops 2 | bytes 16 | tf_op jit(solution)/shard_map/psum | solution.py:124
  (465 shorter events, 148.1 us)
Async XLA Ops:
  7.2 1.6 copy-start
  7.2 77.4 %all-gather.8.cloned.1.call-start = ((), (), s32[]{:S(2)}) async-start(), calls=%async_computation | async-start | bytes 2359296 | tf_op jit(solution)/shard_map/all_gather | solution.py:11
  11.1 2.0 copy-start.1
  18.1 2.0 copy-start.2
  25.2 2.0 copy-start.9
  32.4 2.0 copy-start.16
  34.4 7.8 %copy-start.36 = (f32[1,16,256]{2,1,0:T(8,128)S(1)}, f32[1,16,256]{2,1,0:T(8,128)}, u32[]{:S(2)}) copy-start(f32[1,16,256]{2,1,0:T(8,128)} %param.19) | copy-start | bytes 49156
  39.4 2.0 copy-start.29
  42.2 21.0 %copy-start.3 = (f32[16,256,256]{2,1,0:T(8,128)S(1)}, f32[16,256,256]{2,1,0:T(8,128)}, u32[]{:S(2)}) copy-start(f32[16,256,256]{2,1,0:T(8,128)} %copy-done.2) | copy-start | bytes 12582916
  63.1 3.8 copy-start.10
  66.8 3.7 copy-start.17
  93.9 9.3 %copy-start.23 = (bf16[1,16,256,256]{3,2,1,0:T(8,128)(2,1)S(1)}, bf16[1,16,256,256]{3,2,1,0:T(8,128)(2,1)}, u32[]{:S(2)}) copy-start(bf16[1,16,256,256]{3,2,1,0:T(8,128)(2,1)} %param.22) | copy-start | bytes 6291460
  99.8 11.5 %copy-start.30 = (bf16[1,16,256,256]{3,2,1,0:T(8,128)(2,1)S(1)}, bf16[1,16,256,256]{3,2,1,0:T(8,128)(2,1)}, u32[]{:S(2)}) copy-start(bf16[1,16,256,256]{3,2,1,0:T(8,128)(2,1)} %param.20) | copy-start | bytes 6291460
  101.0 12.1 %collective-permute-start = (f32[1,256]{1,0:T(1,128)S(1)}, f32[1,256]{1,0:T(1,128)S(1)}, u32[]{:S(2)}, u32[]{:S(2)}) collective-permute-start(f32[1,256]{1,0:T(1,128)S(1)} %constant_dynamic-slice_fusion.11), channel_id=1, source_target_pairs={{0,4},{4,8},{8,12},{12,16},{16,20},{20,24},{24,28},{1,5},{5,9},{9,... | collective-permute-start | bytes 3080 | tf_op jit(solution)/shard_map/ppermute | solution.py:30
  104.2 12.4 %collective-permute-start.3 = (f32[1,16,256]{2,1,0:T(8,128)S(1)}, f32[1,16,256]{2,1,0:T(8,128)S(1)}, u32[]{:S(2)}, u32[]{:S(2)}) collective-permute-start(f32[1,16,256]{2,1,0:T(8,128)S(1)} %bitcast.752), channel_id=1, source_target_pairs={{1,0},{2,1},{3,2},{5,4},{6,5},{7,6},{9,8},{10,9},{11,10},{13,12},{... | collective-permute-start | bytes 49160 | tf_op jit(solution)/shard_map/ppermute | solution.py:31
  105.5 11.1 %collective-permute-start.1 = (f32[1,256]{1,0:T(1,128)S(1)}, f32[1,256]{1,0:T(1,128)S(1)}, u32[]{:S(2)}, u32[]{:S(2)}) collective-permute-start(f32[1,256]{1,0:T(1,128)S(1)} %slice.224), channel_id=1, source_target_pairs={{4,0},{8,4},{12,8},{16,12},{20,16},{24,20},{28,24},{5,1},{9,5},{13... | collective-permute-start | bytes 3080 | tf_op jit(solution)/shard_map/ppermute | solution.py:31
  106.8 8.0 %collective-permute-start.2 = (f32[1,16,256]{2,1,0:T(8,128)S(1)}, f32[1,16,256]{2,1,0:T(8,128)S(1)}, u32[]{:S(2)}, u32[]{:S(2)}) collective-permute-start(f32[1,16,256]{2,1,0:T(8,128)S(1)} %bitcast.665), channel_id=1, source_target_pairs={{0,1},{1,2},{2,3},{4,5},{5,6},{6,7},{8,9},{9,10},{10,11},{12,13},{... | collective-permute-start | bytes 49160 | tf_op jit(solution)/shard_map/ppermute | solution.py:30
  160.8 9.4 %copy-start.4 = (f32[16,256,256]{2,1,0:T(8,128)S(1)}, f32[16,256,256]{2,1,0:T(8,128)}, u32[]{:S(2)}) copy-start(f32[16,256,256]{2,1,0:T(8,128)} %copy-done.2) | copy-start | bytes 12582916
  170.2 3.8 copy-start.11
  173.9 3.7 copy-start.18
  200.4 6.0 copy-start.24
  206.3 2.0 copy-start.31
  210.0 9.5 %collective-permute-start.4 = (f32[1,256]{1,0:T(1,128)S(1)}, f32[1,256]{1,0:T(1,128)S(1)}, u32[]{:S(2)}, u32[]{:S(2)}) collective-permute-start(f32[1,256]{1,0:T(1,128)S(1)} %constant_dynamic-slice_fusion.10), channel_id=1, source_target_pairs={{0,4},{4,8},{8,12},{12,16},{16,20},{20,24},{24,28},{1,5},{5,9},{9,... | collective-permute-start | bytes 3080 | tf_op jit(solution)/shard_map/ppermute | solution.py:30
  212.4 10.6 %collective-permute-start.7 = (f32[1,16,256]{2,1,0:T(8,128)S(1)}, f32[1,16,256]{2,1,0:T(8,128)S(1)}, u32[]{:S(2)}, u32[]{:S(2)}) collective-permute-start(f32[1,16,256]{2,1,0:T(8,128)S(1)} %bitcast.753), channel_id=1, source_target_pairs={{1,0},{2,1},{3,2},{5,4},{6,5},{7,6},{9,8},{10,9},{11,10},{13,12},{... | collective-permute-start | bytes 49160 | tf_op jit(solution)/shard_map/ppermute | solution.py:31
  213.7 9.3 %collective-permute-start.5 = (f32[1,256]{1,0:T(1,128)S(1)}, f32[1,256]{1,0:T(1,128)S(1)}, u32[]{:S(2)}, u32[]{:S(2)}) collective-permute-start(f32[1,256]{1,0:T(1,128)S(1)} %slice.232), channel_id=1, source_target_pairs={{4,0},{8,4},{12,8},{16,12},{20,16},{24,20},{28,24},{5,1},{9,5},{13... | collective-permute-start | bytes 3080 | tf_op jit(solution)/shard_map/ppermute | solution.py:31
  215.0 6.3 collective-permute-start.6
  267.8 9.4 %copy-start.5 = (f32[16,256,256]{2,1,0:T(8,128)S(1)}, f32[16,256,256]{2,1,0:T(8,128)}, u32[]{:S(2)}) copy-start(f32[16,256,256]{2,1,0:T(8,128)} %copy-done.2) | copy-start | bytes 12582916
  277.1 3.8 copy-start.12
  280.8 3.7 copy-start.19
  307.6 6.0 copy-start.25
  313.5 2.0 copy-start.32
  317.2 9.5 %collective-permute-start.8 = (f32[1,256]{1,0:T(1,128)S(1)}, f32[1,256]{1,0:T(1,128)S(1)}, u32[]{:S(2)}, u32[]{:S(2)}) collective-permute-start(f32[1,256]{1,0:T(1,128)S(1)} %constant_dynamic-slice_fusion.9), channel_id=1, source_target_pairs={{0,4},{4,8},{8,12},{12,16},{16,20},{20,24},{24,28},{1,5},{5,9},{9,... | collective-permute-start | bytes 3080 | tf_op jit(solution)/shard_map/ppermute | solution.py:30
  319.6 10.6 %collective-permute-start.11 = (f32[1,16,256]{2,1,0:T(8,128)S(1)}, f32[1,16,256]{2,1,0:T(8,128)S(1)}, u32[]{:S(2)}, u32[]{:S(2)}) collective-permute-start(f32[1,16,256]{2,1,0:T(8,128)S(1)} %bitcast.754), channel_id=1, source_target_pairs={{1,0},{2,1},{3,2},{5,4},{6,5},{7,6},{9,8},{10,9},{11,10},{13,12},{... | collective-permute-start | bytes 49160 | tf_op jit(solution)/shard_map/ppermute | solution.py:31
  320.9 9.3 %collective-permute-start.9 = (f32[1,256]{1,0:T(1,128)S(1)}, f32[1,256]{1,0:T(1,128)S(1)}, u32[]{:S(2)}, u32[]{:S(2)}) collective-permute-start(f32[1,256]{1,0:T(1,128)S(1)} %slice.240), channel_id=1, source_target_pairs={{4,0},{8,4},{12,8},{16,12},{20,16},{24,20},{28,24},{5,1},{9,5},{13... | collective-permute-start | bytes 3080 | tf_op jit(solution)/shard_map/ppermute | solution.py:31
  322.2 6.3 collective-permute-start.10
  374.9 9.4 %copy-start.6 = (f32[16,256,256]{2,1,0:T(8,128)S(1)}, f32[16,256,256]{2,1,0:T(8,128)}, u32[]{:S(2)}) copy-start(f32[16,256,256]{2,1,0:T(8,128)} %copy-done.2) | copy-start | bytes 12582916
  384.3 3.8 copy-start.13
  388.0 3.7 copy-start.20
  414.6 6.0 copy-start.26
  420.5 2.0 copy-start.33
  424.2 9.5 %collective-permute-start.12 = (f32[1,256]{1,0:T(1,128)S(1)}, f32[1,256]{1,0:T(1,128)S(1)}, u32[]{:S(2)}, u32[]{:S(2)}) collective-permute-start(f32[1,256]{1,0:T(1,128)S(1)} %constant_dynamic-slice_fusion.8), channel_id=1, source_target_pairs={{0,4},{4,8},{8,12},{12,16},{16,20},{20,24},{24,28},{1,5},{5,9},{9,... | collective-permute-start | bytes 3080 | tf_op jit(solution)/shard_map/ppermute | solution.py:30
  426.6 10.6 %collective-permute-start.15 = (f32[1,16,256]{2,1,0:T(8,128)S(1)}, f32[1,16,256]{2,1,0:T(8,128)S(1)}, u32[]{:S(2)}, u32[]{:S(2)}) collective-permute-start(f32[1,16,256]{2,1,0:T(8,128)S(1)} %bitcast.755), channel_id=1, source_target_pairs={{1,0},{2,1},{3,2},{5,4},{6,5},{7,6},{9,8},{10,9},{11,10},{13,12},{... | collective-permute-start | bytes 49160 | tf_op jit(solution)/shard_map/ppermute | solution.py:31
  427.9 9.3 %collective-permute-start.13 = (f32[1,256]{1,0:T(1,128)S(1)}, f32[1,256]{1,0:T(1,128)S(1)}, u32[]{:S(2)}, u32[]{:S(2)}) collective-permute-start(f32[1,256]{1,0:T(1,128)S(1)} %slice.248), channel_id=1, source_target_pairs={{4,0},{8,4},{12,8},{16,12},{20,16},{24,20},{28,24},{5,1},{9,5},{13... | collective-permute-start | bytes 3080 | tf_op jit(solution)/shard_map/ppermute | solution.py:31
  429.2 6.3 collective-permute-start.14
  482.1 9.4 %copy-start.7 = (f32[16,256,256]{2,1,0:T(8,128)S(1)}, f32[16,256,256]{2,1,0:T(8,128)}, u32[]{:S(2)}) copy-start(f32[16,256,256]{2,1,0:T(8,128)} %copy-done.2) | copy-start | bytes 12582916
  491.5 3.8 copy-start.14
  495.2 3.7 copy-start.21
  521.7 6.0 copy-start.27
  527.7 2.0 copy-start.34
  531.4 9.5 %collective-permute-start.16 = (f32[1,256]{1,0:T(1,128)S(1)}, f32[1,256]{1,0:T(1,128)S(1)}, u32[]{:S(2)}, u32[]{:S(2)}) collective-permute-start(f32[1,256]{1,0:T(1,128)S(1)} %constant_dynamic-slice_fusion.7), channel_id=1, source_target_pairs={{0,4},{4,8},{8,12},{12,16},{16,20},{20,24},{24,28},{1,5},{5,9},{9,... | collective-permute-start | bytes 3080 | tf_op jit(solution)/shard_map/ppermute | solution.py:30
  533.7 10.6 %collective-permute-start.19 = (f32[1,16,256]{2,1,0:T(8,128)S(1)}, f32[1,16,256]{2,1,0:T(8,128)S(1)}, u32[]{:S(2)}, u32[]{:S(2)}) collective-permute-start(f32[1,16,256]{2,1,0:T(8,128)S(1)} %bitcast.756), channel_id=1, source_target_pairs={{1,0},{2,1},{3,2},{5,4},{6,5},{7,6},{9,8},{10,9},{11,10},{13,12},{... | collective-permute-start | bytes 49160 | tf_op jit(solution)/shard_map/ppermute | solution.py:31
  535.0 9.3 %collective-permute-start.17 = (f32[1,256]{1,0:T(1,128)S(1)}, f32[1,256]{1,0:T(1,128)S(1)}, u32[]{:S(2)}, u32[]{:S(2)}) collective-permute-start(f32[1,256]{1,0:T(1,128)S(1)} %slice.256), channel_id=1, source_target_pairs={{4,0},{8,4},{12,8},{16,12},{20,16},{24,20},{28,24},{5,1},{9,5},{13... | collective-permute-start | bytes 3080 | tf_op jit(solution)/shard_map/ppermute | solution.py:31
  536.3 6.3 collective-permute-start.18
  589.1 9.4 %copy-start.8 = (f32[16,256,256]{2,1,0:T(8,128)S(1)}, f32[16,256,256]{2,1,0:T(8,128)}, u32[]{:S(2)}) copy-start(f32[16,256,256]{2,1,0:T(8,128)} %copy-done.2) | copy-start | bytes 12582916
  598.4 3.8 copy-start.15
  602.2 3.7 copy-start.22
  628.8 6.0 copy-start.28
  634.7 2.0 copy-start.35
  638.4 9.5 %collective-permute-start.20 = (f32[1,256]{1,0:T(1,128)S(1)}, f32[1,256]{1,0:T(1,128)S(1)}, u32[]{:S(2)}, u32[]{:S(2)}) collective-permute-start(f32[1,256]{1,0:T(1,128)S(1)} %constant_dynamic-slice_fusion.6), channel_id=1, source_target_pairs={{0,4},{4,8},{8,12},{12,16},{16,20},{20,24},{24,28},{1,5},{5,9},{9,... | collective-permute-start | bytes 3080 | tf_op jit(solution)/shard_map/ppermute | solution.py:30
  640.7 10.6 %collective-permute-start.23 = (f32[1,16,256]{2,1,0:T(8,128)S(1)}, f32[1,16,256]{2,1,0:T(8,128)S(1)}, u32[]{:S(2)}, u32[]{:S(2)}) collective-permute-start(f32[1,16,256]{2,1,0:T(8,128)S(1)} %bitcast.757), channel_id=1, source_target_pairs={{1,0},{2,1},{3,2},{5,4},{6,5},{7,6},{9,8},{10,9},{11,10},{13,12},{... | collective-permute-start | bytes 49160 | tf_op jit(solution)/shard_map/ppermute | solution.py:31
  642.0 9.3 %collective-permute-start.21 = (f32[1,256]{1,0:T(1,128)S(1)}, f32[1,256]{1,0:T(1,128)S(1)}, u32[]{:S(2)}, u32[]{:S(2)}) collective-permute-start(f32[1,256]{1,0:T(1,128)S(1)} %slice.264), channel_id=1, source_target_pairs={{4,0},{8,4},{12,8},{16,12},{20,16},{24,20},{28,24},{5,1},{9,5},{13... | collective-permute-start | bytes 3080 | tf_op jit(solution)/shard_map/ppermute | solution.py:31
  643.3 6.3 collective-permute-start.22
Sparse Core Ops, SparseCore 0:
  42.2 30.5 all-gather.7
where the time goes:
time: 716 us; the launch traced here: 704 us
  blocking collectives  316 us (44%)
  matrix products  284 us (40%)
  starting transfers between devices  56.3 us (8%)
  between operations  24.1 us (3%)
  local copies, waits for them, and re-layouts  13.8 us (2%)
  other arithmetic  9.32 us (1%)
    psum x6, blocking collectives, body(): lax.psum((jnp.sum(residual * image), jnp.sum(image * image)), ('track', '...  256 us
    dot_general x24, matrix products, body(): jnp.einsum('kab,kb->ka', slot_levels[precondition_level], earlier, precis...  111 us
    all_gather x6, blocking collectives, carried_in(): pieces = jax.tree.map(lambda part: lax.all_gather(part, axis), value)  59.9 us
    dot_general x24, matrix products, apply_blocks(): jnp.einsum('kab,kb->ka', mats.astype(jnp.float32), vecs, precision=lax.Pr...  51.9 us
    dot_general x42, matrix products, compose(): jnp.dot(later[0], earlier[1], precision=lax.Precision.HIGHEST) + later[1]  51.4 us
    ppermute x12, starting transfers between devices, padded(): before = lax.ppermute(last, axis, up)  40.7 us
    dot_general x6, matrix products, body(): jnp.einsum('kab,b->ka', composed, entry, precision=lax.Precision.HIGHEST)  35.5 us
    dot_general x4, matrix products, body(): jnp.einsum('kab,kbc->kac', composed, shifted_maps, precision=lax.Precisio...  20.3 us
  transfers between devices with their start and end apart: 25, of which 0 were waited for; matrix products, arithmetic and copies ran while one was open for 8% of the time, Pallas kernels for 0%

commit v1 on v0

v1 whole, which is shorter than its diff:
```python
import functools

import jax
import jax.numpy as jnp
from jax import lax
from jax.experimental import pallas as pl
from jax.experimental.pallas import tpu as pltpu
from jax.sharding import PartitionSpec as P

ITERS = 6
CHAINS = 2
ROWS = 8
NT = (((1,), (1,)), ((), ()))
NN = (((1,), (0,)), ((), ()))
VMEM = pl.BlockSpec(memory_space=pltpu.VMEM)
SMEM = pl.BlockSpec(memory_space=pltpu.SMEM)
F32 = jnp.float32


def pieces(value):
    high = value.astype(jnp.bfloat16).astype(F32)
    rest = value - high
    middle = rest.astype(jnp.bfloat16).astype(F32)
    low = rest - middle
    return high, middle, low


def split_row(row):
    high, middle, low = pieces(row)
    return jnp.concatenate([high, middle, low, jnp.zeros_like(low)], axis=0).astype(jnp.bfloat16)


def times(lhs, matrix, dims):
    out = lax.dot_general(lhs, matrix, dims, preferred_element_type=F32)
    return out[:ROWS] + out[ROWS : 2 * ROWS] + out[2 * ROWS : 3 * ROWS]


def times_matrix(value, matrix, dims):
    high, middle, low = pieces(value)
    lhs = jnp.concatenate([high, middle, low], axis=0).astype(jnp.bfloat16)
    out = lax.dot_general(lhs, matrix, dims, preferred_element_type=F32)
    n = value.shape[0]
    return out[:n] + out[n : 2 * n] + out[2 * n :]


def spread(row):
    return jnp.transpose(jnp.broadcast_to(row, (128, row.shape[1])))


def times_f32(column, matrix):
    wide = jnp.concatenate([column] * (matrix.shape[1] // 128), axis=1)
    return jnp.sum(matrix * wide, axis=0, keepdims=True)


def wide_row(ref, j):
    return jnp.broadcast_to(ref[j : j + 1, :], (ROWS, ref.shape[1]))


def sweep(x_ref, lower_ref, precond_ref, on_ref, live_ref, local_ref, cap):
    length = cap // CHAINS
    state = [None] * CHAINS
    first = None
    for t in range(length):
        for q in range(CHAINS):
            j = q * length + t
            inner = wide_row(x_ref, j)
            if t > 0:
                inner = inner - on_ref[j] * times(split_row(state[q]), lower_ref[j], NT)
            value = times(split_row(inner), precond_ref[j], NT)
            before = state[q] if t > 0 else jnp.zeros_like(value)
            state[q] = jnp.where(live_ref[j] > 0, value, before)
            local_ref[j : j + 1, :] = state[q][:1]
            if j == 0:
                first = on_ref[0] * times(split_row(state[q]), lower_ref[0], NN)
    return state, first


def send_ends(state, first, maps_ref, residual, image, track, n_track, length, out_ref):
    end = state[0][:1]
    for q in range(1, CHAINS):
        end = state[q][:1] + times_f32(spread(end), maps_ref[q * length + length - 1])
    if residual is None:
        dots = [jnp.zeros((1, 128), F32)] * 2
    else:
        dots = []
        for left in (residual, image):
            partial = jnp.sum(left * image, axis=0, keepdims=True)
            dots.append(sum(partial[:, i : i + 128] for i in range(0, partial.shape[1], 128)))
    half = end.shape[1] // 128
    to_later = jnp.concatenate([end[:, 128 * i : 128 * i + 128] for i in range(half)] + dots, axis=0)
    to_earlier = jnp.concatenate(
        [first[:1, 128 * i : 128 * i + 128] for i in range(half)] + dots, axis=0
    )
    for i in range(out_ref.shape[0]):
        out_ref[i] = jnp.where(i % n_track > track, to_later, to_earlier)


def maps_kernel(cap, lower_ref, precond_ref, on_ref, live_ref, maps_ref, total_ref, edge_ref):
    width = lower_ref.shape[-1]
    length = cap // CHAINS
    rows = lax.broadcasted_iota(jnp.int32, (width, width), 0)
    cols = lax.broadcasted_iota(jnp.int32, (width, width), 1)
    ident = jnp.where(rows == cols, 1.0, 0.0).astype(F32)
    state = [ident] * CHAINS
    for t in range(length):
        for q in range(CHAINS):
            j = q * length + t
            if t == 0:
                inner = lax.dot_general(
                    ident.astype(jnp.bfloat16), lower_ref[j], NT, preferred_element_type=F32
                )
                value = lax.dot_general(
                    inner.astype(jnp.bfloat16), precond_ref[j], NT, preferred_element_type=F32
                )
            else:
                inner = times_matrix(state[q], lower_ref[j], NT)
                value = times_matrix(inner, precond_ref[j], NT)
            state[q] = jnp.where(live_ref[j] > 0, -on_ref[j] * value, state[q])
            maps_ref[j] = state[q]
            if j == 0:
                edge_ref[...] = times_matrix(state[q], lower_ref[0], NN)
    total = state[0]
    for q in range(1, CHAINS):
        total = jnp.dot(total, state[q], precision=lax.Precision.HIGHEST)
    total_ref[...] = total


def entry_kernel(n_track, pos_ref, totals_ref, out_ref):
    track = pos_ref[0]
    value = None
    for i in range(1, n_track - 1):
        index = jnp.bitwise_xor(jnp.maximum(track - i, 0), track)
        nearer = totals_ref[index]
        value = nearer if value is None else jnp.dot(nearer, value, precision=lax.Precision.HIGHEST)
        out_ref[i - 1] = value


def start_kernel(cap, n_track, rhs_ref, lower_ref, precond_ref, maps_ref, on_ref, live_ref, pos_ref, local_ref, send_ref):
    state, first = sweep(rhs_ref, lower_ref, precond_ref, on_ref, live_ref, local_ref, cap)
    send_ends(state, first, maps_ref, None, None, pos_ref[0], n_track, cap // CHAINS, send_ref)


def direction_kernel(
    cap, n_track, recv_ref, local_ref, maps_ref, entry_ref, edge_map_ref, coupling_ref, live_ref, pos_ref,
    value_ref, first_ref, second_ref, rims_ref,
):
    track, strip = pos_ref[0], pos_ref[1]
    width = local_ref.shape[1]
    length = cap // CHAINS
    half = width // 128
    base = strip * n_track

    def end_of(i):
        got = recv_ref[base + jnp.maximum(track - i, 0)]
        got = jnp.where(track - i >= 0, got, 0.0)
        return [got[h : h + 1] for h in range(half)]

    entry = jnp.concatenate(end_of(1), axis=1)
    for i in range(2, n_track):
        column = jnp.concatenate([spread(part) for part in end_of(i)], axis=0)
        entry = entry + times_f32(column, entry_ref[i - 2])
    rims_ref[0:1, :] = entry
    columns = [spread(entry)]
    for q in range(1, CHAINS):
        last = q * length - 1
        begin = local_ref[last : last + 1, :] + times_f32(columns[-1], maps_ref[last])
        columns.append(spread(begin))
    even = strip % 2 == 0
    for j in range(cap):
        value = local_ref[j : j + 1, :] + times_f32(columns[j // length], maps_ref[j])
        masked = jnp.where(live_ref[j] > 0, value, 0.0)
        value_ref[j : j + 1, :] = masked
        crossed = times(split_row(jnp.broadcast_to(masked, (ROWS, width))), coupling_ref[j], NN)[:1]
        first_ref[j : j + 1, :] = jnp.where(even, masked, crossed)
        second_ref[j : j + 1, :] = jnp.where(even, crossed, masked)
    ahead = recv_ref[base + jnp.minimum(track + 1, n_track - 1)]
    ahead = jnp.concatenate([ahead[h : h + 1] for h in range(half)], axis=1)
    ahead = ahead + times_f32(spread(value), edge_map_ref[...])
    rims_ref[1:2, :] = jnp.where(track < n_track - 1, ahead, 0.0)


def local_kernel(cap, value_ref, rims_ref, diag_ref, lower_ref, on_ref, pos_ref, base_ref):
    count = pos_ref[2]
    lowered = on_ref[0] * times(split_row(wide_row(rims_ref, 0)), lower_ref[0], NT)
    edge = wide_row(rims_ref, 1)
    held = None
    for j in range(cap):
        lhs = split_row(wide_row(value_ref, j))
        own = times(lhs, diag_ref[j], NT) + lowered
        if j > 0:
            held = held + on_ref[j] * times(lhs, lower_ref[j], NN)
            base_ref[j - 1 : j, :] = held[:1]
        if j < cap - 1:
            lowered = on_ref[j + 1] * times(lhs, lower_ref[j + 1], NT)
        held = own + jnp.where(count - 1 == j, edge, 0.0)
    base_ref[cap - 1 : cap, :] = held[:1]


def alpha_of(recv_ref, half):
    total = jnp.sum(recv_ref[...], axis=0)
    inner = jnp.sum(total[half : half + 1], axis=1, keepdims=True)
    energy = jnp.sum(total[half + 1 : half + 2], axis=1, keepdims=True)
    return inner / (energy + 1e-6)


def update_kernel(
    cap, n_track, first, last, base_ref, first_ref, second_ref, recv_ref, value_ref, state_ref, mask_ref,
    coupling_ref, lower_ref, precond_ref, maps_ref, on_ref, live_ref, pos_ref, next_ref, local_ref, send_ref,
):
    track, strip = pos_ref[0], pos_ref[1]
    width = base_ref.shape[1]
    odd = strip % 2 == 1
    image_ref = next_ref.at[1]
    one, two = first_ref[...], second_ref[...]
    below = jnp.where(odd, one, two)
    above = jnp.where(odd, two, one)
    image_ref[...] = base_ref[...] + above
    for j in range(cap):
        row = jnp.broadcast_to(below[j : j + 1, :], (ROWS, width))
        crossed = times(split_row(row), coupling_ref[j], NT)
        image_ref[j : j + 1, :] = image_ref[j : j + 1, :] + crossed[:1]
    image = image_ref[...] * mask_ref[...]
    if first:
        next_ref[0] = state_ref[0]
        next_ref[2] = value_ref[...]
        next_ref[3] = jnp.zeros_like(image)
        next_ref[1] = image
    else:
        alpha = alpha_of(recv_ref, width // 128)
        next_ref[0] = state_ref[0] - alpha * state_ref[1]
        next_ref[3] = state_ref[3] + alpha * state_ref[2]
        next_ref[2] = state_ref[2] - alpha * value_ref[...]
        next_ref[1] = state_ref[1] - alpha * image
    residual, image = next_ref[0], next_ref[1]
    if last:
        state, edge = [jnp.zeros((1, width), F32)], jnp.zeros((1, width), F32)
        local_ref[...] = jnp.zeros_like(image)
        dots = []
        for left in (residual, image):
            partial = jnp.sum(left * image, axis=0, keepdims=True)
            dots.append(sum(partial[:, i : i + 128] for i in range(0, width, 128)))
        packed = jnp.concatenate([jnp.zeros((width // 128, 128), F32)] + dots, axis=0)
        for i in range(send_ref.shape[0]):
            send_ref[i] = packed
    else:
        state, edge = sweep(image_ref, lower_ref, precond_ref, on_ref, live_ref, local_ref, cap)
        send_ends(state, edge, maps_ref, residual, image, track, n_track, cap // CHAINS, send_ref)


def final_kernel(recv_ref, state_ref, solution_ref, residual_ref):
    alpha = alpha_of(recv_ref, state_ref.shape[2] // 128)
    solution_ref[...] = state_ref[3] + alpha * state_ref[2]
    residual_ref[...] = state_ref[0] - alpha * state_ref[1]


def call(kernel, outs, specs, *args):
    return pl.pallas_call(
        kernel,
        out_shape=[jax.ShapeDtypeStruct(shape, F32) for shape in outs],
        in_specs=specs,
        out_specs=[VMEM] * len(outs),
        compiler_params=pltpu.CompilerParams(vmem_limit_bytes=40 * 1024 * 1024),
    )(*args)


def body(rhs, principal_tiles, lower_blocks, coupling_blocks, precond_blocks, seg_blocks, links):
    cap, width = rhs.shape[1:]
    n_track, n_strip = lax.axis_size("track"), lax.axis_size("strip")
    track, strip = lax.axis_index("track"), lax.axis_index("strip")
    count = seg_blocks[0]
    slots = jnp.arange(cap, dtype=jnp.int32)
    live = (slots < count).astype(F32)
    on = links[0].astype(F32) * live * jnp.where((slots > 0) | (track > 0), 1.0, 0.0)
    mask = jnp.broadcast_to(live[:, None], (cap, width))
    pos = jnp.stack([track, strip, count]).astype(jnp.int32)
    diag, lower, coupling, precond = (
        principal_tiles[0], lower_blocks[0], coupling_blocks[0], precond_blocks[0],
    )
    whole = n_track * n_strip
    block = (cap, width)
    chunk = (whole, width // 128 + 2, 128)

    maps, total, edge_map = call(
        functools.partial(maps_kernel, cap),
        [(cap, width, width), (width, width), (width, width)],
        [VMEM, VMEM, SMEM, SMEM],
        lower, precond, on, live,
    )
    gathered = [total]
    for m in range(2, n_track, 2):
        gathered.append(lax.ppermute(total, "track", [(i, i ^ m) for i in range(n_track)]))
    gathered = jnp.stack(gathered)
    other = lax.ppermute(gathered, "track", [(i, i ^ 1) for i in range(n_track)])
    totals = jnp.stack([gathered, other], axis=1).reshape(n_track, width, width)
    edge_map = lax.ppermute(edge_map, "track", [(i + 1, i) for i in range(n_track - 1)])
    entries, = call(
        functools.partial(entry_kernel, n_track),
        [(n_track - 2, width, width)],
        [SMEM, VMEM],
        pos, totals,
    )

    residual = rhs[0] * mask
    local, send = call(
        functools.partial(start_kernel, cap, n_track),
        [block, chunk],
        [VMEM] * 4 + [SMEM] * 3,
        residual, lower, precond, maps, on, live, pos,
    )
    state = jnp.broadcast_to(residual[None], (4,) + block)
    pairs = [(i, i ^ 1) for i in range(n_strip) if i ^ 1 < n_strip]
    cross = [(i, j) for k in range(1, n_strip - 1, 2) for i, j in ((k, k + 1), (k + 1, k))]
    for step_number in range(ITERS):
        recv = lax.all_to_all(send, ("strip", "track"), 0, 0)
        value, first, second, rims = call(
            functools.partial(direction_kernel, cap, n_track),
            [block, block, block, (2, width)],
            [VMEM] * 6 + [SMEM] * 2,
            recv, local, maps, entries, edge_map, coupling, live, pos,
        )
        first = lax.ppermute(first, "strip", pairs)
        second = lax.ppermute(second, "strip", cross)
        base, = call(
            functools.partial(local_kernel, cap),
            [block],
            [VMEM] * 4 + [SMEM] * 2,
            value, rims, diag, lower, on, pos,
        )
        state, local, send = call(
            functools.partial(update_kernel, cap, n_track, step_number == 0, step_number == ITERS - 1),
            [(4,) + block, block, chunk],
            [VMEM] * 11 + [SMEM] * 3,
            base, first, second, recv, value, state, mask, coupling, lower, precond, maps, on, live, pos,
        )
    recv = lax.all_to_all(send, ("strip", "track"), 0, 0)
    solution, residual = call(final_kernel, [block, block], [VMEM] * 2, recv, state)
    return (solution[None], residual[None])


def solution(mesh):
    in_specs = (
        P("strip", "track", None),
        P("strip", "track", None, None),
        P("strip", "track", None, None),
        P("strip", "track", None, None),
        P("strip", "track", None, None),
        P("track"),
        P("strip", "track"),
    )
    out_specs = (P("strip", "track", None), P("strip", "track", None))
    return jax.shard_map(body, mesh=mesh, in_specs=in_specs, out_specs=out_specs, check_vma=False)
```

time: 716 us -> 184 us (0.26); the launches traced: 704 us -> 183 us
  matrix products: 284 us -> 0 us
  blocking collectives: 316 us -> 71 us
  Pallas kernels: 0 us -> 53.7 us
  starting transfers between devices: 56.3 us -> 22.9 us
  between operations: 24.1 us -> 1.59 us
  waiting for transfers between devices: 0.08 us -> 14.1 us
    dot_general x113 -> x0, matrix products: 284 us -> none  [the longest x24 111 us: body(): jnp.einsum('kab,kb->ka', slot_levels[precondition_level], earlier, precis...]
    psum x6 -> x0, blocking collectives: 256 us -> none  [body(): lax.psum((jnp.sum(residual * image), jnp.sum(image * image)), ('track', '...]
    all_to_all x0 -> x6, blocking collectives: none -> 71 us  [body(): recv = lax.all_to_all(send, ('strip', 'track'), 0, 0)]
    all_gather x6 -> x0, blocking collectives: 59.9 us -> none  [carried_in(): pieces = jax.tree.map(lambda part: lax.all_gather(part, axis), value)]
    pallas_call x0 -> x22, Pallas kernels: none -> 53.7 us  [call(): pl.pallas_call(kernel, out_shape=[jax.ShapeDtypeStruct(shape, F32) for sh...]
    ppermute x24 -> x17, starting transfers between devices: 56.2 us -> 15.8 us  [the longest x6 5.91 us: body(): first = lax.ppermute(first, 'strip', pairs)]
    ppermute x24 -> x17, waiting for transfers between devices: 0.06 us -> 12.7 us  [the longest x3 11.7 us: body(): lax.ppermute(total, 'track', [(i, i ^ m) for i in range(n_track)])]
    unnamed x86 -> x32, local copies, waits for them, and re-layouts: 8.72 us -> 15.3 us
  transfers between devices with their start and end apart: 25 -> 18, of which waited for: 0 -> 8; matrix products, arithmetic and copies ran while one was open for 8% -> 1% of each run, Pallas kernels for 0% -> 11%
where the time goes in v1:
time: 184 us; the launch traced here: 183 us
  blocking collectives  71 us (39%)
  Pallas kernels  53.7 us (29%)
  starting transfers between devices  22.9 us (12%)
  local copies, waits for them, and re-layouts  15.5 us (8%)
  waiting for transfers between devices  14.1 us (8%)
  other arithmetic  4.11 us (2%)
    all_to_all x6, blocking collectives, body(): recv = lax.all_to_all(send, ('strip', 'track'), 0, 0)  71 us
    pallas_call x22, Pallas kernels, call(): pl.pallas_call(kernel, out_shape=[jax.ShapeDtypeStruct(shape, F32) for sh...  53.7 us
    unnamed x32, local copies, waits for them, and re-layouts  15.3 us
    ppermute x3, waiting for transfers between devices, body(): lax.ppermute(total, 'track', [(i, i ^ m) for i in range(n_track)])  11.7 us
    all_to_all x1, starting transfers between devices, body(): recv = lax.all_to_all(send, ('strip', 'track'), 0, 0)  7.08 us
    ppermute x6, starting transfers between devices, body(): first = lax.ppermute(first, 'strip', pairs)  5.91 us
    ppermute x3, starting transfers between devices, body(): lax.ppermute(total, 'track', [(i, i ^ m) for i in range(n_track)])  4.46 us
    ppermute x6, starting transfers between devices, body(): second = lax.ppermute(second, 'strip', cross)  4.13 us
  transfers between devices with their start and end apart: 18, of which 8 were waited for; matrix products, arithmetic and copies ran while one was open for 1% of the time, Pallas kernels for 11%

profile of v1, /device:TPU:0, one launch (start us, length us, event | category | flops | bytes accessed | tf_op | source)
XLA Modules:
  0.0 182.9 jit_solution(2285066521799443700)
XLA Ops:
  1.3 0.7 fusion.on_ref
  2.0 1.6 copy-done.4
  3.6 1.6 copy-done.8
  5.1 5.7 %shard_map.86 = (f32[16,256,256]{2,1,0:T(8,128)S(1)}, f32[256,256]{1,0:T(8,128)S(1)}, f32[256,256]{1,0:T(8,128)S(1)}) custom-call(bf16[16,256,256]{2,1,0:T(8,128)(2,1)S(1)} %bitcast.25, bf16[16,256,256]{2,1,0:T(8,128)(2,1)S(1)} %bitcast.51, f32[16]{0:T(128)S(1)} %fusion.on_ref, f32[16]{0:T(128)S(1)} %compare_convert_fusion.live_ref), custom_call_target="tpu_custom_call" | custom-call | tf_op jit(solution)/shard_map/pallas_call | solution.py:257
  10.8 1.9 %copy-done = f32[16,256,256]{2,1,0:T(8,128)} copy-done((f32[16,256,256]{2,1,0:T(8,128)}, f32[16,256,256]{2,1,0:T(8,128)S(1)}, u32[]{:S(2)}) %copy-start) | copy-done | bytes 4194328
  12.8 3.9 %collective-permute-start.2 = (f32[256,256]{1,0:T(8,128)S(1)}, f32[256,256]{1,0:T(8,128)S(1)}, u32[]{:S(2)}, u32[]{:S(2)}) collective-permute-start(f32[256,256]{1,0:T(8,128)S(1)} %get-tuple-element.53), channel_id=1, source_target_pairs={{0,24},{4,28},{8,16},{12,20},{16,8},{20,12},{24,0},{28,4},{1,25},{... | collective-permute-start | bytes 786440 | tf_op jit(solution)/shard_map/ppermute | solution.py:291
  16.7 0.5 collective-permute-start
  17.2 6.6 %collective-permute-done.2 = f32[256,256]{1,0:T(8,128)S(1)} collective-permute-done((f32[256,256]{1,0:T(8,128)S(1)}, f32[256,256]{1,0:T(8,128)S(1)}, u32[]{:S(2)}, u32[]{:S(2)}) %collective-permute-start.2) | collective-permute-done | bytes 262176 | tf_op jit(solution)/shard_map/ppermute | solution.py:291
  23.8 5.0 %collective-permute-done = f32[256,256]{1,0:T(8,128)S(1)} collective-permute-done((f32[256,256]{1,0:T(8,128)S(1)}, f32[256,256]{1,0:T(8,128)S(1)}, u32[]{:S(2)}, u32[]{:S(2)}) %collective-permute-start) | collective-permute-done | bytes 262176 | tf_op jit(solution)/shard_map/ppermute | solution.py:291
  28.9 1.5 fusion.1
  30.4 1.3 collective-permute-start.4
  31.9 2.2 %copy-done.1 = f32[16,256,256]{2,1,0:T(8,128)S(1)} copy-done((f32[16,256,256]{2,1,0:T(8,128)S(1)}, f32[16,256,256]{2,1,0:T(8,128)}, u32[]{:S(2)}) %copy-start.1) | copy-done | bytes 4194328
  34.1 1.6 copy-done.9
  35.7 3.3 %shard_map.87 = (f32[16,256]{1,0:T(8,128)S(1)}, f32[32,4,128]{2,1,0:T(4,128)}) custom-call(f32[16,256]{1,0:T(8,128)S(1)} %bitcast_multiply_fusion.rhs_ref, bf16[16,256,256]{2,1,0:T(8,128)(2,1)S(1)} %bitcast.26, bf16[16,256,256]{2,1,0:T(8,128)(2,1)S(1)} %bitcast.52, f32[16,256,256]{2,1,0:T(8,128)S(1)} %copy-done.1, f32[16]{0:T(128)S(1)} %fusion.on_ref, ...), custom_call_target="tpu_custom_call" | custom-call | tf_op jit(solution)/shard_map/pallas_call | solution.py:257
  39.0 7.1 %all-to-all-start = ((f32[32,4,128]{2,1,0:T(4,128)}), f32[32,4,128]{2,1,0:T(4,128)S(1)}, u32[]{:S(2)}, u32[]{:S(2)}) async-start(f32[32,4,128]{2,1,0:T(4,128)} %get-tuple-element.51), calls=%async_computation | async-start | bytes 131072 | tf_op jit(solution)/shard_map/all_to_all | solution.py:314
  46.1 1.7 pad_maximum_fusion
  47.8 0.1 copy.9
  47.9 3.0 %shard_map.88.entry_ref = f32[6,256,256]{2,1,0:T(8,128)S(1)} custom-call(s32[3]{0:T(128)S(1)} %pad_add_fusion.pos_ref, f32[8,256,256]{2,1,0:T(8,128)S(1)} %bitcast.65), custom_call_target="tpu_custom_call" | custom-call | tf_op jit(solution)/shard_map/pallas_call | solution.py:257
  51.0 1.2 copy-done.11
  52.2 1.3 all-to-all-done.recv_ref
  53.5 2.2 %copy-done.2 = f32[16,256,256]{2,1,0:T(8,128)S(1)} copy-done((f32[16,256,256]{2,1,0:T(8,128)S(1)}, f32[16,256,256]{2,1,0:T(8,128)}, u32[]{:S(2)}) %copy-start.2) | copy-done | bytes 4194328
  55.7 1.6 copy-done.6
  57.3 1.4 copy-done.12
  58.7 1.7 shard_map.89
  60.4 0.7 collective-permute-start.5
  61.1 0.7 collective-permute-start.6
  61.8 2.2 %shard_map.90.base_ref = f32[16,256]{1,0:T(8,128)S(1)} custom-call(f32[16,256]{1,0:T(8,128)S(1)} %get-tuple-element.55.value_ref, f32[2,256]{1,0:T(2,128)S(1)} %get-tuple-element.56.rims_ref, bf16[16,256,256]{2,1,0:T(8,128)(2,1)S(1)} %bitcast.59, bf16[16,256,256]{2,1,0:T(8,128)(2,1)S(1)} %bitcast.27, f32[16]{0:T(128)S(1)} %fusion.on_ref, ...), custom_call_target="tpu_custom_call" | custom-call | tf_op jit(solution)/shard_map/pallas_call | solution.py:257
  64.0 0.2 collective-permute-done.5.first_ref
  64.3 3.3 %shard_map.91 = (f32[4,16,256]{2,1,0:T(8,128)S(1)}, f32[16,256]{1,0:T(8,128)S(1)}, f32[32,4,128]{2,1,0:T(4,128)S(1)}) custom-call(f32[16,256]{1,0:T(8,128)S(1)} %shard_map.90.base_ref, f32[16,256]{1,0:T(8,128)S(1)} %collective-permute-done.5.first_ref, f32[16,256]{1,0:T(8,128)S(1)} %collective-permute-done.6.second_ref, ...), custom_call_target="tpu_custom_call" | custom-call | tf_op jit(solution)/shard_map/pallas_call | solution.py:257
  67.6 14.2 %all_to_all.35.recv_ref = f32[32,4,128]{2,1,0:T(4,128)S(1)} all-to-all(f32[32,4,128]{2,1,0:T(4,128)S(1)} %get-tuple-element.59), channel_id=1, replica_groups=mesh['track'=8,'strip'=4] {'strip','track'}, dimensions={0} | all-to-all | bytes 131072 | tf_op jit(solution)/shard_map/all_to_all | solution.py:314
  81.8 1.6 shard_map.92
  83.4 0.7 collective-permute-start.7
  84.1 0.7 collective-permute-start.8
  84.8 2.2 %shard_map.93.base_ref = f32[16,256]{1,0:T(8,128)S(1)} custom-call(f32[16,256]{1,0:T(8,128)S(1)} %get-tuple-element.61.value_ref, f32[2,256]{1,0:T(2,128)S(1)} %get-tuple-element.62.rims_ref, bf16[16,256,256]{2,1,0:T(8,128)(2,1)S(1)} %bitcast.60, bf16[16,256,256]{2,1,0:T(8,128)(2,1)S(1)} %bitcast.29, f32[16]{0:T(128)S(1)} %fusion.on_ref, ...), custom_call_target="tpu_custom_call" | custom-call | tf_op jit(solution)/shard_map/pallas_call | solution.py:257
  87.0 0.3 collective-permute-done.7.first_ref
  87.3 3.3 %shard_map.94 = (f32[4,16,256]{2,1,0:T(8,128)S(1)}, f32[16,256]{1,0:T(8,128)S(1)}, f32[32,4,128]{2,1,0:T(4,128)S(1)}) custom-call(f32[16,256]{1,0:T(8,128)S(1)} %shard_map.93.base_ref, f32[16,256]{1,0:T(8,128)S(1)} %collective-permute-done.7.first_ref, f32[16,256]{1,0:T(8,128)S(1)} %collective-permute-done.8.second_ref, ...), custom_call_target="tpu_custom_call" | custom-call | tf_op jit(solution)/shard_map/pallas_call | solution.py:257
  90.6 11.6 %all_to_all.36.recv_ref = f32[32,4,128]{2,1,0:T(4,128)S(1)} all-to-all(f32[32,4,128]{2,1,0:T(4,128)S(1)} %get-tuple-element.66), channel_id=1, replica_groups=mesh['track'=8,'strip'=4] {'strip','track'}, dimensions={0} | all-to-all | bytes 131072 | tf_op jit(solution)/shard_map/all_to_all | solution.py:314
  102.2 1.6 shard_map.95
  103.9 0.7 collective-permute-start.10
  104.5 2.5 %collective-permute-start.9 = (f32[16,256]{1,0:T(8,128)S(1)}, f32[16,256]{1,0:T(8,128)S(1)}, u32[]{:S(2)}, u32[]{:S(2)}) collective-permute-start(f32[16,256]{1,0:T(8,128)S(1)} %get-tuple-element.70), channel_id=1, source_target_pairs={{0,1},{1,0},{2,3},{3,2},{4,5},{5,4},{6,7},{7,6},{8,9},{9,8},{10,11... | collective-permute-start | bytes 49160 | tf_op jit(solution)/shard_map/ppermute | solution.py:321
  107.1 2.2 %shard_map.96.base_ref = f32[16,256]{1,0:T(8,128)S(1)} custom-call(f32[16,256]{1,0:T(8,128)S(1)} %get-tuple-element.68.value_ref, f32[2,256]{1,0:T(2,128)S(1)} %get-tuple-element.69.rims_ref, bf16[16,256,256]{2,1,0:T(8,128)(2,1)S(1)} %bitcast.61, bf16[16,256,256]{2,1,0:T(8,128)(2,1)S(1)} %bitcast.31, f32[16]{0:T(128)S(1)} %fusion.on_ref, ...), custom_call_target="tpu_custom_call" | custom-call | tf_op jit(solution)/shard_map/pallas_call | solution.py:257
  109.3 3.3 %shard_map.97 = (f32[4,16,256]{2,1,0:T(8,128)S(1)}, f32[16,256]{1,0:T(8,128)S(1)}, f32[32,4,128]{2,1,0:T(4,128)S(1)}) custom-call(f32[16,256]{1,0:T(8,128)S(1)} %shard_map.96.base_ref, f32[16,256]{1,0:T(8,128)S(1)} %collective-permute-done.9.first_ref, f32[16,256]{1,0:T(8,128)S(1)} %collective-permute-done.10.second_ref, ...), custom_call_target="tpu_custom_call" | custom-call | tf_op jit(solution)/shard_map/pallas_call | solution.py:257
  112.6 10.1 %all_to_all.37.recv_ref = f32[32,4,128]{2,1,0:T(4,128)S(1)} all-to-all(f32[32,4,128]{2,1,0:T(4,128)S(1)} %get-tuple-element.73), channel_id=1, replica_groups=mesh['track'=8,'strip'=4] {'strip','track'}, dimensions={0} | all-to-all | bytes 131072 | tf_op jit(solution)/shard_map/all_to_all | solution.py:314
  122.7 1.6 shard_map.98
  124.4 0.7 collective-permute-start.11
  125.0 0.7 collective-permute-start.12
  125.7 2.2 %shard_map.99.base_ref = f32[16,256]{1,0:T(8,128)S(1)} custom-call(f32[16,256]{1,0:T(8,128)S(1)} %get-tuple-element.75.value_ref, f32[2,256]{1,0:T(2,128)S(1)} %get-tuple-element.76.rims_ref, bf16[16,256,256]{2,1,0:T(8,128)(2,1)S(1)} %bitcast.62, bf16[16,256,256]{2,1,0:T(8,128)(2,1)S(1)} %bitcast.33, f32[16]{0:T(128)S(1)} %fusion.on_ref, ...), custom_call_target="tpu_custom_call" | custom-call | tf_op jit(solution)/shard_map/pallas_call | solution.py:257
  127.9 0.3 collective-permute-done.11.first_ref
  128.2 3.3 %shard_map.100 = (f32[4,16,256]{2,1,0:T(8,128)S(1)}, f32[16,256]{1,0:T(8,128)S(1)}, f32[32,4,128]{2,1,0:T(4,128)S(1)}) custom-call(f32[16,256]{1,0:T(8,128)S(1)} %shard_map.99.base_ref, f32[16,256]{1,0:T(8,128)S(1)} %collective-permute-done.11.first_ref, f32[16,256]{1,0:T(8,128)S(1)} %collective-permute-done.12.second_ref, ...), custom_call_target="tpu_custom_call" | custom-call | tf_op jit(solution)/shard_map/pallas_call | solution.py:257
  131.5 11.6 %all_to_all.38.recv_ref = f32[32,4,128]{2,1,0:T(4,128)S(1)} all-to-all(f32[32,4,128]{2,1,0:T(4,128)S(1)} %get-tuple-element.80), channel_id=1, replica_groups=mesh['track'=8,'strip'=4] {'strip','track'}, dimensions={0} | all-to-all | bytes 131072 | tf_op jit(solution)/shard_map/all_to_all | solution.py:314
  143.2 1.6 shard_map.101
  144.8 0.7 collective-permute-start.13
  145.5 0.9 collective-permute-start.14
  146.3 2.2 %shard_map.102.base_ref = f32[16,256]{1,0:T(8,128)S(1)} custom-call(f32[16,256]{1,0:T(8,128)S(1)} %get-tuple-element.82.value_ref, f32[2,256]{1,0:T(2,128)S(1)} %get-tuple-element.83.rims_ref, bf16[16,256,256]{2,1,0:T(8,128)(2,1)S(1)} %bitcast.63, bf16[16,256,256]{2,1,0:T(8,128)(2,1)S(1)} %bitcast.35, f32[16]{0:T(128)S(1)} %fusion.on_ref, ...), custom_call_target="tpu_custom_call" | custom-call | tf_op jit(solution)/shard_map/pallas_call | solution.py:257
  148.6 3.3 %shard_map.103 = (f32[4,16,256]{2,1,0:T(8,128)S(1)}, f32[16,256]{1,0:T(8,128)S(1)}, f32[32,4,128]{2,1,0:T(4,128)S(1)}) custom-call(f32[16,256]{1,0:T(8,128)S(1)} %shard_map.102.base_ref, f32[16,256]{1,0:T(8,128)S(1)} %collective-permute-done.13.first_ref, f32[16,256]{1,0:T(8,128)S(1)} %collective-permute-done.14.second_ref, ...), custom_call_target="tpu_custom_call" | custom-call | tf_op jit(solution)/shard_map/pallas_call | solution.py:257
  151.9 11.8 %all_to_all.39.recv_ref = f32[32,4,128]{2,1,0:T(4,128)S(1)} all-to-all(f32[32,4,128]{2,1,0:T(4,128)S(1)} %get-tuple-element.87), channel_id=1, replica_groups=mesh['track'=8,'strip'=4] {'strip','track'}, dimensions={0} | all-to-all | bytes 131072 | tf_op jit(solution)/shard_map/all_to_all | solution.py:314
  163.8 1.6 shard_map.104
  165.4 0.7 collective-permute-start.15
  166.1 0.7 collective-permute-start.16
  166.7 2.2 %shard_map.105.base_ref = f32[16,256]{1,0:T(8,128)S(1)} custom-call(f32[16,256]{1,0:T(8,128)S(1)} %get-tuple-element.89.value_ref, f32[2,256]{1,0:T(2,128)S(1)} %get-tuple-element.90.rims_ref, bf16[16,256,256]{2,1,0:T(8,128)(2,1)S(1)} %bitcast.64, bf16[16,256,256]{2,1,0:T(8,128)(2,1)S(1)} %bitcast.37, f32[16]{0:T(128)S(1)} %fusion.on_ref, ...), custom_call_target="tpu_custom_call" | custom-call | tf_op jit(solution)/shard_map/pallas_call | solution.py:257
  168.9 0.3 collective-permute-done.15.first_ref
  169.2 1.3 shard_map.106
  170.5 11.6 %all_to_all.40.recv_ref = f32[32,4,128]{2,1,0:T(4,128)S(1)} all-to-all(f32[32,4,128]{2,1,0:T(4,128)S(1)} %get-tuple-element.94), channel_id=1, replica_groups=mesh['track'=8,'strip'=4] {'strip','track'}, dimensions={0} | all-to-all | bytes 131072 | tf_op jit(solution)/shard_map/all_to_all | solution.py:335
  182.2 0.8 shard_map.107
  (42 shorter events, 0.5 us)
Async XLA Ops:
  2.0 1.6 copy-start.4
  3.6 1.6 copy-start.8
  10.8 2.0 %copy-start = (f32[16,256,256]{2,1,0:T(8,128)}, f32[16,256,256]{2,1,0:T(8,128)S(1)}, u32[]{:S(2)}) copy-start(f32[16,256,256]{2,1,0:T(8,128)S(1)} %get-tuple-element.50.maps_ref) | copy-start | bytes 12582916
  12.8 19.0 %copy-start.15 = (f32[1,16,256]{2,1,0:T(8,128)S(1)}, f32[1,16,256]{2,1,0:T(8,128)}, u32[]{:S(2)}) copy-start(f32[1,16,256]{2,1,0:T(8,128)} %param.7) | copy-start | bytes 49156
  12.8 19.1 %copy-start.5 = (bf16[1,16,256,256]{3,2,1,0:T(8,128)(2,1)S(1)}, bf16[1,16,256,256]{3,2,1,0:T(8,128)(2,1)}, u32[]{:S(2)}) copy-start(bf16[1,16,256,256]{3,2,1,0:T(8,128)(2,1)} %param.9) | copy-start | bytes 6291460
  12.8 11.1 %collective-permute-start.2 = (f32[256,256]{1,0:T(8,128)S(1)}, f32[256,256]{1,0:T(8,128)S(1)}, u32[]{:S(2)}, u32[]{:S(2)}) collective-permute-start(f32[256,256]{1,0:T(8,128)S(1)} %get-tuple-element.53), channel_id=1, source_target_pairs={{0,24},{4,28},{8,16},{12,20},{16,8},{20,12},{24,0},{28,4},{1,25},{... | collective-permute-start | bytes 786440 | tf_op jit(solution)/shard_map/ppermute | solution.py:291
  16.7 12.2 %collective-permute-start = (f32[256,256]{1,0:T(8,128)S(1)}, f32[256,256]{1,0:T(8,128)S(1)}, u32[]{:S(2)}, u32[]{:S(2)}) collective-permute-start(f32[256,256]{1,0:T(8,128)S(1)} %get-tuple-element.53), channel_id=1, source_target_pairs={{0,8},{4,12},{8,0},{12,4},{16,24},{20,28},{24,16},{28,20},{1,9},{5... | collective-permute-start | bytes 786440 | tf_op jit(solution)/shard_map/ppermute | solution.py:291
  17.2 11.7 %collective-permute-start.1 = (f32[256,256]{1,0:T(8,128)S(1)}, f32[256,256]{1,0:T(8,128)S(1)}, u32[]{:S(2)}, u32[]{:S(2)}) collective-permute-start(f32[256,256]{1,0:T(8,128)S(1)} %get-tuple-element.53), channel_id=1, source_target_pairs={{0,16},{4,20},{8,24},{12,28},{16,0},{20,4},{24,8},{28,12},{1,17},{... | collective-permute-start | bytes 786440 | tf_op jit(solution)/shard_map/ppermute | solution.py:291
  30.4 15.7 %collective-permute-start.3 = (f32[4,256,256]{2,1,0:T(8,128)}, f32[4,256,256]{2,1,0:T(8,128)}, u32[]{:S(2)}, u32[]{:S(2)}) collective-permute-start(f32[4,256,256]{2,1,0:T(8,128)} %get-tuple-element.99), channel_id=1, source_target_pairs={{0,4},{4,0},{8,12},{12,8},{16,20},{20,16},{24,28},{28,24},{1,5},{5... | collective-permute-start | bytes 3145736 | tf_op jit(solution)/shard_map/ppermute | solution.py:293
  30.4 23.1 %collective-permute-start.4 = (f32[256,256]{1,0:T(8,128)S(1)}, f32[256,256]{1,0:T(8,128)S(1)}, u32[]{:S(2)}, u32[]{:S(2)}) collective-permute-start(f32[256,256]{1,0:T(8,128)S(1)} %get-tuple-element.54), channel_id=1, source_target_pairs={{4,0},{8,4},{12,8},{16,12},{20,16},{24,20},{28,24},{5,1},{9,5},{13... | collective-permute-start | bytes 786440 | tf_op jit(solution)/shard_map/ppermute | solution.py:295
  31.9 2.2 %copy-start.1 = (f32[16,256,256]{2,1,0:T(8,128)S(1)}, f32[16,256,256]{2,1,0:T(8,128)}, u32[]{:S(2)}) copy-start(f32[16,256,256]{2,1,0:T(8,128)} %copy-done) | copy-start | bytes 12582916
  34.1 1.6 copy-start.9
  39.0 14.5 %all-to-all-start = ((f32[32,4,128]{2,1,0:T(4,128)}), f32[32,4,128]{2,1,0:T(4,128)S(1)}, u32[]{:S(2)}, u32[]{:S(2)}) async-start(f32[32,4,128]{2,1,0:T(4,128)} %get-tuple-element.51), calls=%async_computation | async-start | bytes 131072 | tf_op jit(solution)/shard_map/all_to_all | solution.py:314
  50.9 1.2 copy-start.11
  53.5 2.2 %copy-start.2 = (f32[16,256,256]{2,1,0:T(8,128)S(1)}, f32[16,256,256]{2,1,0:T(8,128)}, u32[]{:S(2)}) copy-start(f32[16,256,256]{2,1,0:T(8,128)} %copy-done) | copy-start | bytes 12582916
  55.7 1.6 copy-start.6
  57.3 1.4 copy-start.12
  58.7 3.1 %copy-start.14 = (bf16[1,16,256,256]{3,2,1,0:T(8,128)(2,1)S(1)}, bf16[1,16,256,256]{3,2,1,0:T(8,128)(2,1)}, u32[]{:S(2)}) copy-start(bf16[1,16,256,256]{3,2,1,0:T(8,128)(2,1)} %param.8) | copy-start | bytes 6291460
  58.7 5.6 %copy-start.10 = (bf16[1,16,256,256]{3,2,1,0:T(8,128)(2,1)S(1)}, bf16[1,16,256,256]{3,2,1,0:T(8,128)(2,1)}, u32[]{:S(2)}) copy-start(bf16[1,16,256,256]{3,2,1,0:T(8,128)(2,1)} %param.11) | copy-start | bytes 6291460
  60.4 3.8 %collective-permute-start.5 = (f32[16,256]{1,0:T(8,128)S(1)}, f32[16,256]{1,0:T(8,128)S(1)}, u32[]{:S(2)}, u32[]{:S(2)}) collective-permute-start(f32[16,256]{1,0:T(8,128)S(1)} %get-tuple-element.57), channel_id=1, source_target_pairs={{0,1},{1,0},{2,3},{3,2},{4,5},{5,4},{6,7},{7,6},{8,9},{9,8},{10,11... | collective-permute-start | bytes 49160 | tf_op jit(solution)/shard_map/ppermute | solution.py:321
  61.1 3.1 %collective-permute-start.6 = (f32[16,256]{1,0:T(8,128)S(1)}, f32[16,256]{1,0:T(8,128)S(1)}, u32[]{:S(2)}, u32[]{:S(2)}) collective-permute-start(f32[16,256]{1,0:T(8,128)S(1)} %get-tuple-element.58), channel_id=1, source_target_pairs={{1,2},{2,1},{5,6},{6,5},{9,10},{10,9},{13,14},{14,13},{17,18},{18,... | collective-permute-start | bytes 49160 | tf_op jit(solution)/shard_map/ppermute | solution.py:322
  61.8 2.5 %copy-start.3 = (f32[16,256,256]{2,1,0:T(8,128)S(1)}, f32[16,256,256]{2,1,0:T(8,128)}, u32[]{:S(2)}) copy-start(f32[16,256,256]{2,1,0:T(8,128)} %copy-done) | copy-start | bytes 12582916
  64.3 17.5 %copy-start.7 = (bf16[1,16,256,256]{3,2,1,0:T(8,128)(2,1)S(1)}, bf16[1,16,256,256]{3,2,1,0:T(8,128)(2,1)}, u32[]{:S(2)}) copy-start(bf16[1,16,256,256]{3,2,1,0:T(8,128)(2,1)} %param.10) | copy-start | bytes 6291460
  64.3 17.5 %copy-start.13 = (f32[6,256,256]{2,1,0:T(8,128)S(1)}, f32[6,256,256]{2,1,0:T(8,128)}, u32[]{:S(2)}) copy-start(f32[6,256,256]{2,1,0:T(8,128)} %copy-done.11) | copy-start | bytes 4718596
  83.4 3.8 %collective-permute-start.7 = (f32[16,256]{1,0:T(8,128)S(1)}, f32[16,256]{1,0:T(8,128)S(1)}, u32[]{:S(2)}, u32[]{:S(2)}) collective-permute-start(f32[16,256]{1,0:T(8,128)S(1)} %get-tuple-element.63), channel_id=1, source_target_pairs={{0,1},{1,0},{2,3},{3,2},{4,5},{5,4},{6,7},{7,6},{8,9},{9,8},{10,11... | collective-permute-start | bytes 49160 | tf_op jit(solution)/shard_map/ppermute | solution.py:321
  84.1 3.1 %collective-permute-start.8 = (f32[16,256]{1,0:T(8,128)S(1)}, f32[16,256]{1,0:T(8,128)S(1)}, u32[]{:S(2)}, u32[]{:S(2)}) collective-permute-start(f32[16,256]{1,0:T(8,128)S(1)} %get-tuple-element.64), channel_id=1, source_target_pairs={{1,2},{2,1},{5,6},{6,5},{9,10},{10,9},{13,14},{14,13},{17,18},{18,... | collective-permute-start | bytes 49160 | tf_op jit(solution)/shard_map/ppermute | solution.py:322
  103.9 5.4 %collective-permute-start.10 = (f32[16,256]{1,0:T(8,128)S(1)}, f32[16,256]{1,0:T(8,128)S(1)}, u32[]{:S(2)}, u32[]{:S(2)}) collective-permute-start(f32[16,256]{1,0:T(8,128)S(1)} %get-tuple-element.71), channel_id=1, source_target_pairs={{1,2},{2,1},{5,6},{6,5},{9,10},{10,9},{13,14},{14,13},{17,18},{18,... | collective-permute-start | bytes 49160 | tf_op jit(solution)/shard_map/ppermute | solution.py:322
  104.5 4.8 %collective-permute-start.9 = (f32[16,256]{1,0:T(8,128)S(1)}, f32[16,256]{1,0:T(8,128)S(1)}, u32[]{:S(2)}, u32[]{:S(2)}) collective-permute-start(f32[16,256]{1,0:T(8,128)S(1)} %get-tuple-element.70), channel_id=1, source_target_pairs={{0,1},{1,0},{2,3},{3,2},{4,5},{5,4},{6,7},{7,6},{8,9},{9,8},{10,11... | collective-permute-start | bytes 49160 | tf_op jit(solution)/shard_map/ppermute | solution.py:321
  124.4 3.8 %collective-permute-start.11 = (f32[16,256]{1,0:T(8,128)S(1)}, f32[16,256]{1,0:T(8,128)S(1)}, u32[]{:S(2)}, u32[]{:S(2)}) collective-permute-start(f32[16,256]{1,0:T(8,128)S(1)} %get-tuple-element.77), channel_id=1, source_target_pairs={{0,1},{1,0},{2,3},{3,2},{4,5},{5,4},{6,7},{7,6},{8,9},{9,8},{10,11... | collective-permute-start | bytes 49160 | tf_op jit(solution)/shard_map/ppermute | solution.py:321
  125.0 3.1 %collective-permute-start.12 = (f32[16,256]{1,0:T(8,128)S(1)}, f32[16,256]{1,0:T(8,128)S(1)}, u32[]{:S(2)}, u32[]{:S(2)}) collective-permute-start(f32[16,256]{1,0:T(8,128)S(1)} %get-tuple-element.78), channel_id=1, source_target_pairs={{1,2},{2,1},{5,6},{6,5},{9,10},{10,9},{13,14},{14,13},{17,18},{18,... | collective-permute-start | bytes 49160 | tf_op jit(solution)/shard_map/ppermute | solution.py:322
  144.8 3.8 %collective-permute-start.13 = (f32[16,256]{1,0:T(8,128)S(1)}, f32[16,256]{1,0:T(8,128)S(1)}, u32[]{:S(2)}, u32[]{:S(2)}) collective-permute-start(f32[16,256]{1,0:T(8,128)S(1)} %get-tuple-element.84), channel_id=1, source_target_pairs={{0,1},{1,0},{2,3},{3,2},{4,5},{5,4},{6,7},{7,6},{8,9},{9,8},{10,11... | collective-permute-start | bytes 49160 | tf_op jit(solution)/shard_map/ppermute | solution.py:321
  145.5 3.1 %collective-permute-start.14 = (f32[16,256]{1,0:T(8,128)S(1)}, f32[16,256]{1,0:T(8,128)S(1)}, u32[]{:S(2)}, u32[]{:S(2)}) collective-permute-start(f32[16,256]{1,0:T(8,128)S(1)} %get-tuple-element.85), channel_id=1, source_target_pairs={{1,2},{2,1},{5,6},{6,5},{9,10},{10,9},{13,14},{14,13},{17,18},{18,... | collective-permute-start | bytes 49160 | tf_op jit(solution)/shard_map/ppermute | solution.py:322
  165.4 3.8 %collective-permute-start.15 = (f32[16,256]{1,0:T(8,128)S(1)}, f32[16,256]{1,0:T(8,128)S(1)}, u32[]{:S(2)}, u32[]{:S(2)}) collective-permute-start(f32[16,256]{1,0:T(8,128)S(1)} %get-tuple-element.91), channel_id=1, source_target_pairs={{0,1},{1,0},{2,3},{3,2},{4,5},{5,4},{6,7},{7,6},{8,9},{9,8},{10,11... | collective-permute-start | bytes 49160 | tf_op jit(solution)/shard_map/ppermute | solution.py:321
  166.1 3.1 %collective-permute-start.16 = (f32[16,256]{1,0:T(8,128)S(1)}, f32[16,256]{1,0:T(8,128)S(1)}, u32[]{:S(2)}, u32[]{:S(2)}) collective-permute-start(f32[16,256]{1,0:T(8,128)S(1)} %get-tuple-element.92), channel_id=1, source_target_pairs={{1,2},{2,1},{5,6},{6,5},{9,10},{10,9},{13,14},{14,13},{17,18},{18,... | collective-permute-start | bytes 49160 | tf_op jit(solution)/shard_map/ppermute | solution.py:322

commit v2 on v1

v2 whole, which is shorter than its diff:
```python
import functools
import math

import jax
import jax.numpy as jnp
from jax import lax
from jax.experimental import pallas as pl
from jax.experimental.pallas import tpu as pltpu
from jax.sharding import PartitionSpec as P

ITERS = 6
CHAINS = 4
ROWS = 8
EARLY = 2
VMEM_BYTES = 16 * 1024 * 1024
PINNED = 1 << 19
NT = (((1,), (1,)), ((), ()))
NN = (((1,), (0,)), ((), ()))
VMEM = pl.BlockSpec(memory_space=pltpu.VMEM)
HBM = pl.BlockSpec(memory_space=pltpu.MemorySpace.HBM)
SMEM = pl.BlockSpec(memory_space=pltpu.SMEM)
F32 = jnp.float32


def pieces(value):
    high = value.astype(jnp.bfloat16)
    rest = value - high.astype(F32)
    middle = rest.astype(jnp.bfloat16)
    low = (rest - middle.astype(F32)).astype(jnp.bfloat16)
    return jnp.concatenate([high, middle, low], axis=0)


def split_row(row):
    return pieces(jnp.concatenate([row, row], axis=0))


def times(lhs, matrix, dims):
    out = lax.dot_general(lhs, matrix, dims, preferred_element_type=F32)
    return out[:ROWS] + out[2 * ROWS : 3 * ROWS] + out[4 * ROWS : 5 * ROWS]


def times_matrix(value, matrix, dims):
    out = lax.dot_general(pieces(value), matrix, dims, preferred_element_type=F32)
    n = value.shape[0]
    return out[:n] + out[n : 2 * n] + out[2 * n :]


def spread(row):
    return jnp.transpose(jnp.broadcast_to(row, (128, row.shape[1])))


def times_f32(column, matrix):
    wide = jnp.concatenate([column] * (matrix.shape[1] // 128), axis=1)
    return jnp.sum(matrix * wide, axis=0, keepdims=True)


def wide_row(ref, j):
    return jnp.broadcast_to(ref[j : j + 1, :], (ROWS, ref.shape[1]))


def is_live(pos_ref, j):
    return j < pos_ref[2]


def link(links_ref, pos_ref, j):
    joined = links_ref[0, j] if j else jnp.where(pos_ref[0] > 0, links_ref[0, 0], 0)
    return jnp.where(is_live(pos_ref, j), joined, 0).astype(F32)


def live_mask(pos_ref, shape):
    return lax.broadcasted_iota(jnp.int32, shape, 0) < pos_ref[2]


def dot_parts(residual, image):
    parts = []
    for left in (residual, image):
        partial = jnp.sum(left * image, axis=0, keepdims=True)
        parts.append(sum(partial[:, i : i + 128] for i in range(0, partial.shape[1], 128)))
    return parts


def halves(row):
    return [row[:, i : i + 128] for i in range(0, row.shape[1], 128)]


def send_ends(end, first, dots, other_ref, pos_ref, n_track, out_ref):
    track = pos_ref[0]
    carried = jnp.where(track % 2 == 0, times_f32(spread(end), other_ref[...]), end)
    near = jnp.concatenate(halves(end) + dots, axis=0)
    far = jnp.concatenate(halves(carried) + dots, axis=0)
    back = jnp.concatenate(halves(first) + dots, axis=0)
    for i in range(out_ref.shape[0]):
        ahead = i % n_track - track
        out_ref[i] = jnp.where(ahead > 1, far, jnp.where(ahead == 1, near, back))


def chain_end(state, maps_ref, length):
    end = state[0][:1]
    for q in range(1, CHAINS):
        end = state[q][:1] + times_f32(spread(end), maps_ref[q * length + length - 1])
    return end


def maps_kernel(
    cap, rhs_hbm, lower_hbm, precond_hbm, diag_hbm, coupling_hbm, links_ref, pos_ref,
    maps_ref, total_ref, edge_ref, local_ref, ends_ref, lower_ref, precond_ref, diag_ref, coupling_ref,
    rhs_ref, sems,
):
    width = lower_ref.shape[-1]
    length = cap // CHAINS
    copies = [pltpu.make_async_copy(rhs_hbm, rhs_ref, sems.at[0])]

    def load(source, target, start, count):
        rows = pl.ds(start, count)
        copies.append(pltpu.make_async_copy(source.at[rows], target.at[rows], sems.at[len(copies)]))

    for begin, end in ((0, EARLY), (EARLY, length)):
        for source, target in ((lower_hbm, lower_ref), (precond_hbm, precond_ref)):
            for q in range(CHAINS):
                load(source, target, q * length + begin, end - begin)
    load(diag_hbm, diag_ref, 0, cap)
    load(coupling_hbm, coupling_ref, 0, cap)
    for copy in copies:
        copy.start()
    early = 1 + 2 * CHAINS
    for copy in copies[:early]:
        copy.wait()
    rows = lax.broadcasted_iota(jnp.int32, (width, width), 0)
    cols = lax.broadcasted_iota(jnp.int32, (width, width), 1)
    ident = jnp.where(rows == cols, 1.0, 0.0).astype(F32)
    state = [ident] * CHAINS
    local = [None] * CHAINS
    for t in range(length):
        if t == EARLY:
            for copy in copies[early:-2]:
                copy.wait()
        for q in range(CHAINS):
            j = q * length + t
            live, on = is_live(pos_ref, j), link(links_ref, pos_ref, j)
            if t == 0:
                inner = lax.dot_general(
                    ident.astype(jnp.bfloat16), lower_ref[j], NT, preferred_element_type=F32
                )
                value = lax.dot_general(
                    inner.astype(jnp.bfloat16), precond_ref[j], NT, preferred_element_type=F32
                )
            else:
                inner = times_matrix(state[q], lower_ref[j], NT)
                value = times_matrix(inner, precond_ref[j], NT)
            state[q] = jnp.where(live, -on * value, state[q])
            maps_ref[j] = state[q]
            inner = wide_row(rhs_ref, j)
            if t > 0:
                inner = inner - on * times(split_row(local[q]), lower_ref[j], NT)
            value = times(split_row(inner), precond_ref[j], NT)
            local[q] = jnp.where(live, value, local[q] if t > 0 else 0.0)
            local_ref[j : j + 1, :] = local[q][:1]
            if j == 0:
                edge_ref[...] = times_matrix(state[q], lower_ref[0], NN)
                ends_ref[1:2, :] = (on * times(split_row(local[q]), lower_ref[0], NN))[:1]
    while len(state) > 1:
        pairs = zip(state[::2], state[1::2])
        state = [jnp.dot(a, b, precision=lax.Precision.HIGHEST) for a, b in pairs]
    total_ref[...] = state[0]
    ends_ref[0:1, :] = chain_end(local, maps_ref, length)
    for copy in copies[-2:]:
        copy.wait()


def pair_kernel(n_track, total_ref, other_ref, ends_ref, pos_ref, *refs):
    chip_ref, send_ref = refs[-2:]
    first_core = pos_ref[0] % 2 == 0
    own, other = total_ref[...], other_ref[...]
    half = own.shape[0] // 2
    early = jnp.where(first_core, own[:half], other[half:])
    late = jnp.where(first_core, other, own)
    chip_ref[...] = jnp.dot(early, late, precision=lax.Precision.HIGHEST)
    dots = [jnp.zeros((1, 128), F32)] * 2
    send_ends(ends_ref[0:1, :], ends_ref[1:2, :], dots, other_ref, pos_ref, n_track, send_ref)


def direction_kernel(cap, n_track, recv_ref, local_ref, maps_ref, other_ref, coupling_ref, *refs):
    chip_refs, (pos_ref, value_ref, first_ref, second_ref, entry_ref) = refs[:-5], refs[-5:]
    track, strip = pos_ref[0], pos_ref[1]
    width = local_ref.shape[1]
    length = cap // CHAINS
    half = width // 128
    base = strip * n_track
    chip = track // 2

    def chunk(index, valid):
        got = recv_ref[base + jnp.clip(index, 0, n_track - 1)]
        got = jnp.where(valid, got, 0.0)
        return jnp.concatenate([got[h : h + 1] for h in range(half)], axis=1)

    def chip_end(i):
        valid = chip - i >= 0
        return chunk(2 * (chip - i), valid) + chunk(2 * (chip - i) + 1, valid)

    def chip_map(i):
        mine, paired = chip_refs[i][...], chip_refs[i + len(chip_refs) // 2][...]
        first_core = track % 2 == 0
        top, bottom = jnp.where(first_core, mine, paired), jnp.where(first_core, paired, mine)
        return jnp.concatenate([top, bottom], axis=0)

    furthest = n_track // 2 - 1
    entry = chip_end(furthest)
    for i in range(furthest - 1, 0, -1):
        entry = chip_end(i) + times_f32(spread(entry), chip_map(i - 1))
    inside = chunk(track - 1, track > 0) + times_f32(spread(entry), other_ref[...])
    entry = jnp.where(track % 2 == 1, inside, entry)
    entry_ref[...] = entry
    columns = [spread(entry)]
    for q in range(1, CHAINS):
        last = q * length - 1
        begin = local_ref[last : last + 1, :] + times_f32(columns[-1], maps_ref[last])
        columns.append(spread(begin))
    even = strip % 2 == 0
    for j in range(cap):
        value = local_ref[j : j + 1, :] + times_f32(columns[j // length], maps_ref[j])
        masked = jnp.where(is_live(pos_ref, j), value, 0.0)
        value_ref[j : j + 1, :] = masked
        crossed = times(split_row(jnp.broadcast_to(masked, (ROWS, width))), coupling_ref[j], NN)[:1]
        first_ref[j : j + 1, :] = jnp.where(even, masked, crossed)
        second_ref[j : j + 1, :] = jnp.where(even, crossed, masked)


def local_kernel(cap, value_ref, entry_ref, diag_ref, lower_ref, links_ref, pos_ref, base_ref):
    lowered = link(links_ref, pos_ref, 0) * times(split_row(wide_row(entry_ref, 0)), lower_ref[0], NT)
    held = None
    for j in range(cap):
        lhs = split_row(wide_row(value_ref, j))
        own = times(lhs, diag_ref[j], NT) + lowered
        if j > 0:
            held = held + link(links_ref, pos_ref, j) * times(lhs, lower_ref[j], NN)
            base_ref[j - 1 : j, :] = held[:1]
        if j < cap - 1:
            lowered = link(links_ref, pos_ref, j + 1) * times(lhs, lower_ref[j + 1], NT)
        held = own
    base_ref[cap - 1 : cap, :] = held[:1]


def alpha_of(recv_ref, half):
    total = jnp.sum(recv_ref[...], axis=0)
    inner = jnp.sum(total[half : half + 1], axis=1, keepdims=True)
    energy = jnp.sum(total[half + 1 : half + 2], axis=1, keepdims=True)
    return inner / (energy + 1e-6)


def update_kernel(
    cap, n_track, first, base_ref, first_ref, second_ref, recv_ref, value_ref, state_ref, edge_map_ref, coupling_ref,
    lower_ref, precond_ref, maps_ref, other_ref, links_ref, pos_ref, next_ref, local_ref, send_ref,
):
    track, strip, count = pos_ref[0], pos_ref[1], pos_ref[2]
    width = base_ref.shape[1]
    length = cap // CHAINS
    odd = strip % 2 == 1
    image_ref = next_ref.at[1]
    one, two = first_ref[...], second_ref[...]
    below = jnp.where(odd, one, two)
    above = jnp.where(odd, two, one)
    ahead = recv_ref[strip * n_track + jnp.minimum(track + 1, n_track - 1)]
    ahead = jnp.concatenate([ahead[h : h + 1] for h in range(width // 128)], axis=1)
    ahead = ahead + times_f32(spread(value_ref[pl.ds(count - 1, 1), :]), edge_map_ref[...])
    ahead = jnp.where(track < n_track - 1, ahead, 0.0)
    at_end = lax.broadcasted_iota(jnp.int32, (cap, width), 0) == count - 1
    image_ref[...] = base_ref[...] + above + jnp.where(at_end, ahead, 0.0)
    for j in range(cap):
        row = jnp.broadcast_to(below[j : j + 1, :], (ROWS, width))
        crossed = times(split_row(row), coupling_ref[j], NT)
        image_ref[j : j + 1, :] = image_ref[j : j + 1, :] + crossed[:1]
    mask = live_mask(pos_ref, (cap, width))
    image = jnp.where(mask, image_ref[...], 0.0)
    if first:
        next_ref[0] = jnp.where(mask, state_ref[...], 0.0)
        next_ref[2] = value_ref[...]
        next_ref[3] = jnp.zeros_like(image)
        next_ref[1] = image
    else:
        alpha = alpha_of(recv_ref, width // 128)
        next_ref[0] = state_ref[0] - alpha * state_ref[1]
        next_ref[3] = state_ref[3] + alpha * state_ref[2]
        next_ref[2] = state_ref[2] - alpha * value_ref[...]
        next_ref[1] = state_ref[1] - alpha * image
    dots = dot_parts(next_ref[0], next_ref[1])
    if local_ref is None:
        packed = jnp.concatenate([jnp.zeros((width // 128, 128), F32)] + dots, axis=0)
        for i in range(send_ref.shape[0]):
            send_ref[i] = packed
        return
    state = [None] * CHAINS
    for t in range(length):
        for q in range(CHAINS):
            j = q * length + t
            inner = wide_row(image_ref, j)
            if t > 0:
                lowered = times(split_row(state[q]), lower_ref[j], NT)
                inner = inner - link(links_ref, pos_ref, j) * lowered
            value = times(split_row(inner), precond_ref[j], NT)
            state[q] = jnp.where(is_live(pos_ref, j), value, state[q] if t > 0 else 0.0)
            local_ref[j : j + 1, :] = state[q][:1]
            if j == 0:
                edge = link(links_ref, pos_ref, 0) * times(split_row(state[q]), lower_ref[0], NN)
    send_ends(chain_end(state, maps_ref, length), edge[:1], dots, other_ref, pos_ref, n_track, send_ref)


def last_update_kernel(cap, n_track, *refs):
    update_kernel(cap, n_track, False, *refs[:-1], None, refs[-1])


def final_kernel(recv_ref, state_ref, solution_ref, residual_ref):
    alpha = alpha_of(recv_ref, state_ref.shape[2] // 128)
    solution_ref[...] = state_ref[3] + alpha * state_ref[2]
    residual_ref[...] = state_ref[0] - alpha * state_ref[1]


def call(kernel, outs, specs, *args, scratch=(), vmem=VMEM_BYTES):
    outs = [out if len(out) == 2 and isinstance(out[0], tuple) else (out, F32) for out in outs]
    args = [
        pltpu.with_memory_space_constraint(arg, spec.memory_space) if arg.size >= PINNED or spec is HBM else arg
        for arg, spec in zip(args, specs)
    ]
    return pl.pallas_call(
        kernel,
        out_shape=[
            pltpu.VMEM(shape, dtype) if math.prod(shape) >= PINNED else jax.ShapeDtypeStruct(shape, dtype)
            for shape, dtype in outs
        ],
        in_specs=specs,
        out_specs=[VMEM] * len(outs),
        scratch_shapes=scratch,
        compiler_params=pltpu.CompilerParams(vmem_limit_bytes=vmem),
    )(*args)


def body(rhs, principal_tiles, lower_blocks, coupling_blocks, precond_blocks, seg_blocks, links):
    cap, width = rhs.shape[1:]
    n_track, n_strip = lax.axis_size("track"), lax.axis_size("strip")
    track, strip = lax.axis_index("track"), lax.axis_index("strip")
    pos = jnp.stack([track, strip, seg_blocks[0]]).astype(jnp.int32)
    rhs = rhs[0]
    whole = n_track * n_strip
    chips = n_track // 2
    block = (cap, width)
    square = (width, width)
    stack = (cap, width, width)
    chunk = (whole, width // 128 + 2, 128)
    swap = [(i, i ^ 1) for i in range(n_track)]

    maps, total, edge_map, local, ends, lower, precond, diag, coupling = call(
        functools.partial(maps_kernel, cap),
        [stack, square, square, block, (2, width)] + [(stack, jnp.bfloat16)] * 4,
        [HBM] * 5 + [SMEM] * 2,
        rhs, lower_blocks[0], precond_blocks[0], principal_tiles[0], coupling_blocks[0], links, pos,
        scratch=[pltpu.VMEM(block, F32), pltpu.SemaphoreType.DMA((4 * CHAINS + 3,))],
    )
    other = lax.ppermute(total, "track", swap)
    chip, send = call(
        functools.partial(pair_kernel, n_track),
        [(width // 2, width), chunk],
        [VMEM] * 3 + [SMEM] + [VMEM] * 5,
        total, other, ends, pos, maps, lower, precond, diag, coupling,
    )
    nearer = [
        lax.ppermute(chip, "track", [(i, i + 2 * k) for i in range(2, n_track - 2 * k)])
        for k in range(1, chips - 1)
    ]
    state = rhs
    pairs = [(i, i ^ 1) for i in range(n_strip) if i ^ 1 < n_strip]
    cross = [(i, j) for k in range(1, n_strip - 1, 2) for i, j in ((k, k + 1), (k + 1, k))]
    for step_number in range(ITERS):
        recv = lax.all_to_all(send, ("strip", "track"), 0, 0)
        if step_number == 0:
            recv, *nearer = lax.optimization_barrier((recv, *nearer))
            nearer += [lax.ppermute(part, "track", swap) for part in nearer]
        value, first, second, entry = call(
            functools.partial(direction_kernel, cap, n_track),
            [block, block, block, (1, width)],
            [VMEM] * (5 + len(nearer)) + [SMEM],
            recv, local, maps, other, coupling, *nearer, pos,
        )
        if step_number == 0:
            edge_map, entry = lax.optimization_barrier((edge_map, entry))
            edge_map = lax.ppermute(edge_map, "track", [(i + 1, i) for i in range(n_track - 1)])
        first = lax.ppermute(first, "strip", pairs)
        second = lax.ppermute(second, "strip", cross)
        base, = call(
            functools.partial(local_kernel, cap),
            [block],
            [VMEM] * 4 + [SMEM] * 2,
            value, entry, diag, lower, links, pos,
        )
        args = (base, first, second, recv, value, state, edge_map, coupling, lower, precond, maps, other, links, pos)
        specs = [VMEM] * 12 + [SMEM] * 2
        if step_number < ITERS - 1:
            kernel = functools.partial(update_kernel, cap, n_track, step_number == 0)
            state, local, send = call(kernel, [(4,) + block, block, chunk], specs, *args)
        else:
            kernel = functools.partial(last_update_kernel, cap, n_track)
            state, send = call(kernel, [(4,) + block, chunk], specs, *args)
    recv = lax.all_to_all(send, ("strip", "track"), 0, 0)
    solution, residual = call(final_kernel, [block, block], [VMEM] * 2, recv, state)
    return (solution[None], residual[None])


def solution(mesh):
    in_specs = (
        P("strip", "track", None),
        P("strip", "track", None, None),
        P("strip", "track", None, None),
        P("strip", "track", None, None),
        P("strip", "track", None, None),
        P("track"),
        P("strip", "track"),
    )
    out_specs = (P("strip", "track", None), P("strip", "track", None))
    return jax.shard_map(body, mesh=mesh, in_specs=in_specs, out_specs=out_specs, check_vma=False)
```

time: 184 us -> 156 us (0.85)
  blocking collectives: 71 us -> 88.9 us
  local copies, waits for them, and re-layouts: 15.5 us -> 0.67 us
  starting transfers between devices: 22.9 us -> 11.9 us
  waiting for transfers between devices: 14.1 us -> 3.58 us
  Pallas kernels: 53.7 us -> 49.1 us
  other arithmetic: 4.11 us -> 0.08 us
    all_to_all x6 -> x7, blocking collectives: 71 us -> 88.9 us  [body(): recv = lax.all_to_all(send, ('strip', 'track'), 0, 0)]
    unnamed x32 -> x6, local copies, waits for them, and re-layouts: 15.3 us -> 0.67 us
    ppermute x4 -> x5, waiting for transfers between devices: 11.7 us -> 2.19 us  [the longest x1 1.16 us: body(): other = lax.ppermute(total, 'track', swap)]
    all_to_all x1 -> x0, starting transfers between devices: 7.08 us -> none  [body(): recv = lax.all_to_all(send, ('strip', 'track'), 0, 0)]
    pallas_call x22 -> x21, Pallas kernels: 53.7 us -> 49.1 us  [call(): pl.pallas_call(kernel, out_shape=[pltpu.VMEM(shape, dtype) if math.prod(s...]
    another operation x3 -> x1, other arithmetic: 3.3 us -> 0.08 us  [body(): pos = jnp.stack([track, strip, seg_blocks[0]]).astype(jnp.int32)]
    ppermute x4 -> x5, starting transfers between devices: 4.46 us -> 2.38 us  [the longest x2 1.34 us: body(): lax.ppermute(chip, 'track', [(i, i + 2 * k) for i in range(2, n_track - 2...]
    ppermute x6, starting transfers between devices: 5.91 us -> 3.98 us  [body(): first = lax.ppermute(first, 'strip', pairs)]
  transfers between devices with their start and end apart: 18 -> 18, of which waited for: 8 -> 9; matrix products, arithmetic and copies ran while one was open for 1% -> 0% of each run, Pallas kernels for 11% -> 8%
where the time goes in v2:
time: 156 us
  blocking collectives  88.9 us (57%)
  Pallas kernels  49.1 us (31%)
  starting transfers between devices  11.9 us (8%)
  waiting for transfers between devices  3.58 us (2%)
    all_to_all x7, blocking collectives, body(): recv = lax.all_to_all(send, ('strip', 'track'), 0, 0)  88.9 us
    pallas_call x21, Pallas kernels, call(): pl.pallas_call(kernel, out_shape=[pltpu.VMEM(shape, dtype) if math.prod(s...  49.1 us
    ppermute x6, starting transfers between devices, body(): second = lax.ppermute(second, 'strip', cross)  4.3 us
    ppermute x6, starting transfers between devices, body(): first = lax.ppermute(first, 'strip', pairs)  3.98 us
  transfers between devices with their start and end apart: 18, of which 9 were waited for; matrix products, arithmetic and copies ran while one was open for 0% of the time, Pallas kernels for 8%

profile of v2, /device:TPU:0, one launch (start us, length us, event | category | flops | bytes accessed | tf_op | source)
XLA Modules:
  0.0 155.7 jit_solution(10871939809548432245)
XLA Ops:
  1.3 0.1 pad_add_fusion.pos_ref.refs_4_.refs_13_
  1.4 0.7 copy-done
  2.0 8.4 %shard_map.86 = (f32[16,256,256]{2,1,0:T(8,128)S(1)}, f32[256,256]{1,0:T(8,128)S(1)}, f32[256,256]{1,0:T(8,128)S(1)}, f32[16,256]{1,0:T(8,128)S(1)}, f32[2,256]{...) custom-call(f32[16,256]{1,0:T(8,128)} %bitcast.9, ...), custom_call_target="tpu_custom_call" | custom-call | tf_op jit(solution)/shard_map/pallas_call | solution.py:323
  10.4 0.5 collective-permute-start
  10.9 1.2 collective-permute-done.other_ref.refs_11_
  12.1 0.8 shard_map.87
  13.0 0.7 collective-permute-start.1
  13.6 0.7 collective-permute-start.2
  14.3 16.9 %all_to_all.35.recv_ref = f32[32,4,128]{2,1,0:T(4,128)S(1)} all-to-all(f32[32,4,128]{2,1,0:T(4,128)S(1)} %get-tuple-element.68), channel_id=1, replica_groups=mesh['track'=8,'strip'=4] {'strip','track'}, dimensions={0} | all-to-all | bytes 131072 | tf_op jit(solution)/shard_map/all_to_all | solution.py:372
  31.2 0.0 collective-permute-done.1.refs_0_
  31.2 0.1 collective-permute-start.3
  31.3 0.4 collective-permute-start.4
  31.7 0.8 collective-permute-done.3.refs_2_
  32.5 0.2 collective-permute-done.4.refs_3_
  32.7 1.7 %shard_map.88 = (f32[16,256]{1,0:T(8,128)S(1)}, f32[16,256]{1,0:T(8,128)S(1)}, f32[16,256]{1,0:T(8,128)S(1)}, f32[1,256]{1,0:T(1,128)S(1)}) custom-call(f32[32,4,128]{2,1,0:T(4,128)S(1)} %all_to_all.35.recv_ref, f32[16,256]{1,0:T(8,128)S(1)} %get-tuple-element.71.local_ref, f32[16,256,256]{2,1,0:T(8,128)S(1)} %get-tuple-element.63.refs_0_.maps_ref.refs_10_, ...), custom_call_target="tpu_custom_call" | custom-call | tf_op jit(solution)/shard_map/pallas_call | solution.py:323
  34.4 1.3 collective-permute-start.7
  35.8 0.7 collective-permute-start.5
  36.4 0.7 collective-permute-start.6
  37.1 0.0 copy-start.1
  37.1 0.0 copy-start.2
  37.1 2.2 %shard_map.89.base_ref = f32[16,256]{1,0:T(8,128)S(1)} custom-call(f32[16,256]{1,0:T(8,128)S(1)} %get-tuple-element.74.value_ref, f32[1,256]{1,0:T(1,128)S(1)} %get-tuple-element.77.entry_ref, bf16[16,256,256]{2,1,0:T(8,128)(2,1)S(1)} %get-tuple-element.66.refs_3_.diag_ref, bf16[16,256,256]{2,1,0:T(8,128)(2,1)S(1)} %get-tuple-element.64.refs_1_.lower_ref.refs_8_, ...), custom_call_target="tpu_custom_call" | custom-call | tf_op jit(solution)/shard_map/pallas_call | solution.py:323
  39.3 0.3 collective-permute-done.5.first_ref
  39.6 0.0 collective-permute-done.6.second_ref
  39.6 2.9 %shard_map.90 = (f32[4,16,256]{2,1,0:T(8,128)S(1)}, f32[16,256]{1,0:T(8,128)S(1)}, f32[32,4,128]{2,1,0:T(4,128)S(1)}) custom-call(f32[16,256]{1,0:T(8,128)S(1)} %shard_map.89.base_ref, f32[16,256]{1,0:T(8,128)S(1)} %collective-permute-done.5.first_ref, f32[16,256]{1,0:T(8,128)S(1)} %collective-permute-done.6.second_ref, ...), custom_call_target="tpu_custom_call" | custom-call | tf_op jit(solution)/shard_map/pallas_call | solution.py:323
  42.5 13.5 %all_to_all.36.recv_ref = f32[32,4,128]{2,1,0:T(4,128)S(1)} all-to-all(f32[32,4,128]{2,1,0:T(4,128)S(1)} %get-tuple-element.81), channel_id=1, replica_groups=mesh['track'=8,'strip'=4] {'strip','track'}, dimensions={0} | all-to-all | bytes 131072 | tf_op jit(solution)/shard_map/all_to_all | solution.py:372
  56.0 1.7 %shard_map.91 = (f32[16,256]{1,0:T(8,128)S(1)}, f32[16,256]{1,0:T(8,128)S(1)}, f32[16,256]{1,0:T(8,128)S(1)}, f32[1,256]{1,0:T(1,128)S(1)}) custom-call(f32[32,4,128]{2,1,0:T(4,128)S(1)} %all_to_all.36.recv_ref, f32[16,256]{1,0:T(8,128)S(1)} %get-tuple-element.82.local_ref, f32[16,256,256]{2,1,0:T(8,128)S(1)} %get-tuple-element.63.refs_0_.maps_ref.refs_10_, ...), custom_call_target="tpu_custom_call" | custom-call | tf_op jit(solution)/shard_map/pallas_call | solution.py:323
  57.7 0.7 collective-permute-start.8
  58.4 0.8 collective-permute-start.9
  59.2 2.2 %shard_map.92.base_ref = f32[16,256]{1,0:T(8,128)S(1)} custom-call(f32[16,256]{1,0:T(8,128)S(1)} %get-tuple-element.83.value_ref, f32[1,256]{1,0:T(1,128)S(1)} %get-tuple-element.84.entry_ref, bf16[16,256,256]{2,1,0:T(8,128)(2,1)S(1)} %get-tuple-element.66.refs_3_.diag_ref, bf16[16,256,256]{2,1,0:T(8,128)(2,1)S(1)} %get-tuple-element.64.refs_1_.lower_ref.refs_8_, ...), custom_call_target="tpu_custom_call" | custom-call | tf_op jit(solution)/shard_map/pallas_call | solution.py:323
  61.4 0.1 collective-permute-done.8.first_ref
  61.5 2.9 %shard_map.93 = (f32[4,16,256]{2,1,0:T(8,128)S(1)}, f32[16,256]{1,0:T(8,128)S(1)}, f32[32,4,128]{2,1,0:T(4,128)S(1)}) custom-call(f32[16,256]{1,0:T(8,128)S(1)} %shard_map.92.base_ref, f32[16,256]{1,0:T(8,128)S(1)} %collective-permute-done.8.first_ref, f32[16,256]{1,0:T(8,128)S(1)} %collective-permute-done.9.second_ref, ...), custom_call_target="tpu_custom_call" | custom-call | tf_op jit(solution)/shard_map/pallas_call | solution.py:323
  64.3 11.8 %all_to_all.37.recv_ref = f32[32,4,128]{2,1,0:T(4,128)S(1)} all-to-all(f32[32,4,128]{2,1,0:T(4,128)S(1)} %get-tuple-element.88), channel_id=1, replica_groups=mesh['track'=8,'strip'=4] {'strip','track'}, dimensions={0} | all-to-all | bytes 131072 | tf_op jit(solution)/shard_map/all_to_all | solution.py:372
  76.1 1.7 %shard_map.94 = (f32[16,256]{1,0:T(8,128)S(1)}, f32[16,256]{1,0:T(8,128)S(1)}, f32[16,256]{1,0:T(8,128)S(1)}, f32[1,256]{1,0:T(1,128)S(1)}) custom-call(f32[32,4,128]{2,1,0:T(4,128)S(1)} %all_to_all.37.recv_ref, f32[16,256]{1,0:T(8,128)S(1)} %get-tuple-element.89.local_ref, f32[16,256,256]{2,1,0:T(8,128)S(1)} %get-tuple-element.63.refs_0_.maps_ref.refs_10_, ...), custom_call_target="tpu_custom_call" | custom-call | tf_op jit(solution)/shard_map/pallas_call | solution.py:323
  77.9 0.7 collective-permute-start.10
  78.5 0.7 collective-permute-start.11
  79.2 2.2 %shard_map.95.base_ref = f32[16,256]{1,0:T(8,128)S(1)} custom-call(f32[16,256]{1,0:T(8,128)S(1)} %get-tuple-element.90.value_ref, f32[1,256]{1,0:T(1,128)S(1)} %get-tuple-element.91.entry_ref, bf16[16,256,256]{2,1,0:T(8,128)(2,1)S(1)} %get-tuple-element.66.refs_3_.diag_ref, bf16[16,256,256]{2,1,0:T(8,128)(2,1)S(1)} %get-tuple-element.64.refs_1_.lower_ref.refs_8_, ...), custom_call_target="tpu_custom_call" | custom-call | tf_op jit(solution)/shard_map/pallas_call | solution.py:323
  81.4 0.3 collective-permute-done.10.first_ref
  81.7 2.9 %shard_map.96 = (f32[4,16,256]{2,1,0:T(8,128)S(1)}, f32[16,256]{1,0:T(8,128)S(1)}, f32[32,4,128]{2,1,0:T(4,128)S(1)}) custom-call(f32[16,256]{1,0:T(8,128)S(1)} %shard_map.95.base_ref, f32[16,256]{1,0:T(8,128)S(1)} %collective-permute-done.10.first_ref, f32[16,256]{1,0:T(8,128)S(1)} %collective-permute-done.11.second_ref, ...), custom_call_target="tpu_custom_call" | custom-call | tf_op jit(solution)/shard_map/pallas_call | solution.py:323
  84.5 11.6 %all_to_all.38.recv_ref = f32[32,4,128]{2,1,0:T(4,128)S(1)} all-to-all(f32[32,4,128]{2,1,0:T(4,128)S(1)} %get-tuple-element.95), channel_id=1, replica_groups=mesh['track'=8,'strip'=4] {'strip','track'}, dimensions={0} | all-to-all | bytes 131072 | tf_op jit(solution)/shard_map/all_to_all | solution.py:372
  96.2 1.7 %shard_map.97 = (f32[16,256]{1,0:T(8,128)S(1)}, f32[16,256]{1,0:T(8,128)S(1)}, f32[16,256]{1,0:T(8,128)S(1)}, f32[1,256]{1,0:T(1,128)S(1)}) custom-call(f32[32,4,128]{2,1,0:T(4,128)S(1)} %all_to_all.38.recv_ref, f32[16,256]{1,0:T(8,128)S(1)} %get-tuple-element.96.local_ref, f32[16,256,256]{2,1,0:T(8,128)S(1)} %get-tuple-element.63.refs_0_.maps_ref.refs_10_, ...), custom_call_target="tpu_custom_call" | custom-call | tf_op jit(solution)/shard_map/pallas_call | solution.py:323
  97.9 0.7 collective-permute-start.12
  98.6 0.7 collective-permute-start.13
  99.2 2.2 %shard_map.98.base_ref = f32[16,256]{1,0:T(8,128)S(1)} custom-call(f32[16,256]{1,0:T(8,128)S(1)} %get-tuple-element.97.value_ref, f32[1,256]{1,0:T(1,128)S(1)} %get-tuple-element.98.entry_ref, bf16[16,256,256]{2,1,0:T(8,128)(2,1)S(1)} %get-tuple-element.66.refs_3_.diag_ref, bf16[16,256,256]{2,1,0:T(8,128)(2,1)S(1)} %get-tuple-element.64.refs_1_.lower_ref.refs_8_, ...), custom_call_target="tpu_custom_call" | custom-call | tf_op jit(solution)/shard_map/pallas_call | solution.py:323
  101.4 0.3 collective-permute-done.12.first_ref
  101.7 0.0 collective-permute-done.13.second_ref
  101.7 2.9 %shard_map.99 = (f32[4,16,256]{2,1,0:T(8,128)S(1)}, f32[16,256]{1,0:T(8,128)S(1)}, f32[32,4,128]{2,1,0:T(4,128)S(1)}) custom-call(f32[16,256]{1,0:T(8,128)S(1)} %shard_map.98.base_ref, f32[16,256]{1,0:T(8,128)S(1)} %collective-permute-done.12.first_ref, f32[16,256]{1,0:T(8,128)S(1)} %collective-permute-done.13.second_ref, ...), custom_call_target="tpu_custom_call" | custom-call | tf_op jit(solution)/shard_map/pallas_call | solution.py:323
  104.5 11.6 %all_to_all.39.recv_ref = f32[32,4,128]{2,1,0:T(4,128)S(1)} all-to-all(f32[32,4,128]{2,1,0:T(4,128)S(1)} %get-tuple-element.102), channel_id=1, replica_groups=mesh['track'=8,'strip'=4] {'strip','track'}, dimensions={0} | all-to-all | bytes 131072 | tf_op jit(solution)/shard_map/all_to_all | solution.py:372
  116.2 1.7 %shard_map.100 = (f32[16,256]{1,0:T(8,128)S(1)}, f32[16,256]{1,0:T(8,128)S(1)}, f32[16,256]{1,0:T(8,128)S(1)}, f32[1,256]{1,0:T(1,128)S(1)}) custom-call(f32[32,4,128]{2,1,0:T(4,128)S(1)} %all_to_all.39.recv_ref, f32[16,256]{1,0:T(8,128)S(1)} %get-tuple-element.103.local_ref, f32[16,256,256]{2,1,0:T(8,128)S(1)} %get-tuple-element.63.refs_0_.maps_ref.refs_10_, ...), custom_call_target="tpu_custom_call" | custom-call | tf_op jit(solution)/shard_map/pallas_call | solution.py:323
  117.9 0.7 collective-permute-start.14
  118.6 0.9 collective-permute-start.15
  119.5 2.2 %shard_map.101.base_ref = f32[16,256]{1,0:T(8,128)S(1)} custom-call(f32[16,256]{1,0:T(8,128)S(1)} %get-tuple-element.104.value_ref, f32[1,256]{1,0:T(1,128)S(1)} %get-tuple-element.105.entry_ref, bf16[16,256,256]{2,1,0:T(8,128)(2,1)S(1)} %get-tuple-element.66.refs_3_.diag_ref, bf16[16,256,256]{2,1,0:T(8,128)(2,1)S(1)} %get-tuple-element.64.refs_1_.lower_ref.refs_8_, ...), custom_call_target="tpu_custom_call" | custom-call | tf_op jit(solution)/shard_map/pallas_call | solution.py:323
  121.6 0.1 collective-permute-done.14.first_ref
  121.7 0.0 collective-permute-done.15.second_ref
  121.7 2.9 %shard_map.102 = (f32[4,16,256]{2,1,0:T(8,128)S(1)}, f32[16,256]{1,0:T(8,128)S(1)}, f32[32,4,128]{2,1,0:T(4,128)S(1)}) custom-call(f32[16,256]{1,0:T(8,128)S(1)} %shard_map.101.base_ref, f32[16,256]{1,0:T(8,128)S(1)} %collective-permute-done.14.first_ref, f32[16,256]{1,0:T(8,128)S(1)} %collective-permute-done.15.second_ref, ...), custom_call_target="tpu_custom_call" | custom-call | tf_op jit(solution)/shard_map/pallas_call | solution.py:323
  124.6 11.8 %all_to_all.40.recv_ref.refs_3_ = f32[32,4,128]{2,1,0:T(4,128)S(1)} all-to-all(f32[32,4,128]{2,1,0:T(4,128)S(1)} %get-tuple-element.109), channel_id=1, replica_groups=mesh['track'=8,'strip'=4] {'strip','track'}, dimensions={0} | all-to-all | bytes 131072 | tf_op jit(solution)/shard_map/all_to_all | solution.py:372
  136.4 1.7 %shard_map.103 = (f32[16,256]{1,0:T(8,128)S(1)}, f32[16,256]{1,0:T(8,128)S(1)}, f32[16,256]{1,0:T(8,128)S(1)}, f32[1,256]{1,0:T(1,128)S(1)}) custom-call(f32[32,4,128]{2,1,0:T(4,128)S(1)} %all_to_all.40.recv_ref.refs_3_, f32[16,256]{1,0:T(8,128)S(1)} %get-tuple-element.110.local_ref, f32[16,256,256]{2,1,0:T(8,128)S(1)} %get-tuple-element.63.refs_0_.maps_ref.refs_10_, ...), custom_call_target="tpu_custom_call" | custom-call | tf_op jit(solution)/shard_map/pallas_call | solution.py:323
  138.1 0.7 collective-permute-start.16
  138.8 0.7 collective-permute-start.17
  139.5 2.2 %shard_map.104.refs_0_ = f32[16,256]{1,0:T(8,128)S(1)} custom-call(f32[16,256]{1,0:T(8,128)S(1)} %get-tuple-element.111.value_ref.refs_4_, f32[1,256]{1,0:T(1,128)S(1)} %get-tuple-element.112.entry_ref, bf16[16,256,256]{2,1,0:T(8,128)(2,1)S(1)} %get-tuple-element.66.refs_3_.diag_ref, bf16[16,256,256]{2,1,0:T(8,128)(2,1)S(1)} %get-tuple-element.64.refs_1_.lower_ref.refs_8_, ...), custom_call_target="tpu_custom_call" | custom-call | tf_op jit(solution)/shard_map/pallas_call | solution.py:323
  141.6 0.3 collective-permute-done.16.refs_1_
  141.9 0.0 collective-permute-done.17.refs_2_
  141.9 1.3 shard_map.105
  143.2 11.6 %all_to_all.41.recv_ref = f32[32,4,128]{2,1,0:T(4,128)S(1)} all-to-all(f32[32,4,128]{2,1,0:T(4,128)S(1)} %get-tuple-element.116), channel_id=1, replica_groups=mesh['track'=8,'strip'=4] {'strip','track'}, dimensions={0} | all-to-all | bytes 131072 | tf_op jit(solution)/shard_map/all_to_all | solution.py:401
  154.9 0.8 shard_map.106
  (7 shorter events, 0.0 us)
Async XLA Ops:
  1.4 0.7 copy-start
  10.4 1.7 %collective-permute-start = (f32[256,256]{1,0:T(8,128)S(1)}, f32[256,256]{1,0:T(8,128)S(1)}, u32[]{:S(2)}, u32[]{:S(2)}) collective-permute-start(f32[256,256]{1,0:T(8,128)S(1)} %get-tuple-element.61.total_ref), channel_id=1, source_target_pairs={{0,4},{4,0},{8,12},{12,8},{16,20},{20,16},{24,28},{28,24},{1,5},{5... | collective-permute-start | bytes 786440 | tf_op jit(solution)/shard_map/ppermute | solution.py:357
  13.0 18.2 %collective-permute-start.1 = (f32[128,256]{1,0:T(8,128)S(1)}, f32[128,256]{1,0:T(8,128)S(1)}, u32[]{:S(2)}, u32[]{:S(2)}) collective-permute-start(f32[128,256]{1,0:T(8,128)S(1)} %get-tuple-element.69), channel_id=1, source_target_pairs={{8,16},{12,20},{16,24},{20,28},{9,17},{13,21},{17,25},{21,29},{10,... | collective-permute-start | bytes 393224 | tf_op jit(solution)/shard_map/ppermute | solution.py:365
  13.6 17.5 %collective-permute-start.2 = (f32[128,256]{1,0:T(8,128)S(1)}, f32[128,256]{1,0:T(8,128)S(1)}, u32[]{:S(2)}, u32[]{:S(2)}) collective-permute-start(f32[128,256]{1,0:T(8,128)S(1)} %get-tuple-element.69), channel_id=1, source_target_pairs={{8,24},{12,28},{9,25},{13,29},{10,26},{14,30},{11,27},{15,31}} | collective-permute-start | bytes 393224 | tf_op jit(solution)/shard_map/ppermute | solution.py:365
  31.2 1.4 collective-permute-start.3
  31.3 1.4 collective-permute-start.4
  34.4 5.1 %collective-permute-start.7 = (f32[256,256]{1,0:T(8,128)S(1)}, f32[256,256]{1,0:T(8,128)S(1)}, u32[]{:S(2)}, u32[]{:S(2)}) collective-permute-start(f32[256,256]{1,0:T(8,128)S(1)} %get-tuple-element.80), channel_id=1, source_target_pairs={{4,0},{8,4},{12,8},{16,12},{20,16},{24,20},{28,24},{5,1},{9,5},{13... | collective-permute-start | bytes 786440 | tf_op jit(solution)/shard_map/ppermute | solution.py:384
  35.8 3.8 %collective-permute-start.5 = (f32[16,256]{1,0:T(8,128)S(1)}, f32[16,256]{1,0:T(8,128)S(1)}, u32[]{:S(2)}, u32[]{:S(2)}) collective-permute-start(f32[16,256]{1,0:T(8,128)S(1)} %get-tuple-element.78), channel_id=1, source_target_pairs={{0,1},{1,0},{2,3},{3,2},{4,5},{5,4},{6,7},{7,6},{8,9},{9,8},{10,11... | collective-permute-start | bytes 49160 | tf_op jit(solution)/shard_map/ppermute | solution.py:385
  36.4 3.1 %collective-permute-start.6 = (f32[16,256]{1,0:T(8,128)S(1)}, f32[16,256]{1,0:T(8,128)S(1)}, u32[]{:S(2)}, u32[]{:S(2)}) collective-permute-start(f32[16,256]{1,0:T(8,128)S(1)} %get-tuple-element.79), channel_id=1, source_target_pairs={{1,2},{2,1},{5,6},{6,5},{9,10},{10,9},{13,14},{14,13},{17,18},{18,... | collective-permute-start | bytes 49160 | tf_op jit(solution)/shard_map/ppermute | solution.py:386
  37.1 2.5 %copy-start.1 = (s32[1,16]{1,0:T(1,128)S(1)}, s32[1,16]{1,0:T(1,128)}, u32[]{:S(2)}) copy-start(s32[1,16]{1,0:T(1,128)} %refs_12_.1) | copy-start | bytes 196
  37.1 2.5 %copy-start.2 = (f32[1,16,256]{2,1,0:T(8,128)S(1)}, f32[1,16,256]{2,1,0:T(8,128)}, u32[]{:S(2)}) copy-start(f32[1,16,256]{2,1,0:T(8,128)} %param.7) | copy-start | bytes 49156
  57.7 3.8 %collective-permute-start.8 = (f32[16,256]{1,0:T(8,128)S(1)}, f32[16,256]{1,0:T(8,128)S(1)}, u32[]{:S(2)}, u32[]{:S(2)}) collective-permute-start(f32[16,256]{1,0:T(8,128)S(1)} %get-tuple-element.85), channel_id=1, source_target_pairs={{0,1},{1,0},{2,3},{3,2},{4,5},{5,4},{6,7},{7,6},{8,9},{9,8},{10,11... | collective-permute-start | bytes 49160 | tf_op jit(solution)/shard_map/ppermute | solution.py:385
  58.4 3.1 %collective-permute-start.9 = (f32[16,256]{1,0:T(8,128)S(1)}, f32[16,256]{1,0:T(8,128)S(1)}, u32[]{:S(2)}, u32[]{:S(2)}) collective-permute-start(f32[16,256]{1,0:T(8,128)S(1)} %get-tuple-element.86), channel_id=1, source_target_pairs={{1,2},{2,1},{5,6},{6,5},{9,10},{10,9},{13,14},{14,13},{17,18},{18,... | collective-permute-start | bytes 49160 | tf_op jit(solution)/shard_map/ppermute | solution.py:386
  77.9 3.8 %collective-permute-start.10 = (f32[16,256]{1,0:T(8,128)S(1)}, f32[16,256]{1,0:T(8,128)S(1)}, u32[]{:S(2)}, u32[]{:S(2)}) collective-permute-start(f32[16,256]{1,0:T(8,128)S(1)} %get-tuple-element.92), channel_id=1, source_target_pairs={{0,1},{1,0},{2,3},{3,2},{4,5},{5,4},{6,7},{7,6},{8,9},{9,8},{10,11... | collective-permute-start | bytes 49160 | tf_op jit(solution)/shard_map/ppermute | solution.py:385
  78.5 3.1 %collective-permute-start.11 = (f32[16,256]{1,0:T(8,128)S(1)}, f32[16,256]{1,0:T(8,128)S(1)}, u32[]{:S(2)}, u32[]{:S(2)}) collective-permute-start(f32[16,256]{1,0:T(8,128)S(1)} %get-tuple-element.93), channel_id=1, source_target_pairs={{1,2},{2,1},{5,6},{6,5},{9,10},{10,9},{13,14},{14,13},{17,18},{18,... | collective-permute-start | bytes 49160 | tf_op jit(solution)/shard_map/ppermute | solution.py:386
  97.9 3.8 %collective-permute-start.12 = (f32[16,256]{1,0:T(8,128)S(1)}, f32[16,256]{1,0:T(8,128)S(1)}, u32[]{:S(2)}, u32[]{:S(2)}) collective-permute-start(f32[16,256]{1,0:T(8,128)S(1)} %get-tuple-element.99), channel_id=1, source_target_pairs={{0,1},{1,0},{2,3},{3,2},{4,5},{5,4},{6,7},{7,6},{8,9},{9,8},{10,11... | collective-permute-start | bytes 49160 | tf_op jit(solution)/shard_map/ppermute | solution.py:385
  98.6 3.1 %collective-permute-start.13 = (f32[16,256]{1,0:T(8,128)S(1)}, f32[16,256]{1,0:T(8,128)S(1)}, u32[]{:S(2)}, u32[]{:S(2)}) collective-permute-start(f32[16,256]{1,0:T(8,128)S(1)} %get-tuple-element.100), channel_id=1, source_target_pairs={{1,2},{2,1},{5,6},{6,5},{9,10},{10,9},{13,14},{14,13},{17,18},{18,... | collective-permute-start | bytes 49160 | tf_op jit(solution)/shard_map/ppermute | solution.py:386
  117.9 3.8 %collective-permute-start.14 = (f32[16,256]{1,0:T(8,128)S(1)}, f32[16,256]{1,0:T(8,128)S(1)}, u32[]{:S(2)}, u32[]{:S(2)}) collective-permute-start(f32[16,256]{1,0:T(8,128)S(1)} %get-tuple-element.106), channel_id=1, source_target_pairs={{0,1},{1,0},{2,3},{3,2},{4,5},{5,4},{6,7},{7,6},{8,9},{9,8},{10,11... | collective-permute-start | bytes 49160 | tf_op jit(solution)/shard_map/ppermute | solution.py:385
  118.6 3.1 %collective-permute-start.15 = (f32[16,256]{1,0:T(8,128)S(1)}, f32[16,256]{1,0:T(8,128)S(1)}, u32[]{:S(2)}, u32[]{:S(2)}) collective-permute-start(f32[16,256]{1,0:T(8,128)S(1)} %get-tuple-element.107), channel_id=1, source_target_pairs={{1,2},{2,1},{5,6},{6,5},{9,10},{10,9},{13,14},{14,13},{17,18},{18,... | collective-permute-start | bytes 49160 | tf_op jit(solution)/shard_map/ppermute | solution.py:386
  138.1 3.8 %collective-permute-start.16 = (f32[16,256]{1,0:T(8,128)S(1)}, f32[16,256]{1,0:T(8,128)S(1)}, u32[]{:S(2)}, u32[]{:S(2)}) collective-permute-start(f32[16,256]{1,0:T(8,128)S(1)} %get-tuple-element.113), channel_id=1, source_target_pairs={{0,1},{1,0},{2,3},{3,2},{4,5},{5,4},{6,7},{7,6},{8,9},{9,8},{10,11... | collective-permute-start | bytes 49160 | tf_op jit(solution)/shard_map/ppermute | solution.py:385
  138.8 3.1 %collective-permute-start.17 = (f32[16,256]{1,0:T(8,128)S(1)}, f32[16,256]{1,0:T(8,128)S(1)}, u32[]{:S(2)}, u32[]{:S(2)}) collective-permute-start(f32[16,256]{1,0:T(8,128)S(1)} %get-tuple-element.114), channel_id=1, source_target_pairs={{1,2},{2,1},{5,6},{6,5},{9,10},{10,9},{13,14},{14,13},{17,18},{18,... | collective-permute-start | bytes 49160 | tf_op jit(solution)/shard_map/ppermute | solution.py:386

commit v3 on v2

--- a/solution.py
+++ b/solution.py
@@ -11,7 +11,7 @@
 ITERS = 6
 CHAINS = 4
 ROWS = 8
-EARLY = 2
+EARLY = 1
 VMEM_BYTES = 16 * 1024 * 1024
 PINNED = 1 << 19
 NT = (((1,), (1,)), ((), ()))
@@ -94,21 +94,25 @@
         out_ref[i] = jnp.where(ahead > 1, far, jnp.where(ahead == 1, near, back))
 
 
-def chain_end(state, maps_ref, length):
-    end = state[0][:1]
+def chain_ends(state, maps_ref, length):
+    ends = [state[0][:1]]
     for q in range(1, CHAINS):
-        end = state[q][:1] + times_f32(spread(end), maps_ref[q * length + length - 1])
-    return end
+        ends.append(state[q][:1] + times_f32(spread(ends[-1]), maps_ref[q * length + length - 1]))
+    return ends
 
 
 def maps_kernel(
-    cap, rhs_hbm, lower_hbm, precond_hbm, diag_hbm, coupling_hbm, links_ref, pos_ref,
-    maps_ref, total_ref, edge_ref, local_ref, ends_ref, lower_ref, precond_ref, diag_ref, coupling_ref,
-    rhs_ref, sems,
+    cap, rhs_hbm, links_hbm, lower_hbm, precond_hbm, diag_hbm, coupling_hbm, pos_ref,
+    maps_ref, total_ref, edge_ref, local_ref, ends_ref, begins_ref, through_ref,
+    lower_ref, precond_ref, diag_ref, coupling_ref,
+    rhs_ref, links_ref, sems,
 ):
     width = lower_ref.shape[-1]
     length = cap // CHAINS
-    copies = [pltpu.make_async_copy(rhs_hbm, rhs_ref, sems.at[0])]
+    copies = [
+        pltpu.make_async_copy(rhs_hbm, rhs_ref, sems.at[0]),
+        pltpu.make_async_copy(links_hbm, links_ref, sems.at[1]),
+    ]
 
     def load(source, target, start, count):
         rows = pl.ds(start, count)
@@ -122,7 +126,7 @@
     load(coupling_hbm, coupling_ref, 0, cap)
     for copy in copies:
         copy.start()
-    early = 1 + 2 * CHAINS
+    early = 2 + 2 * CHAINS
     for copy in copies[:early]:
         copy.wait()
     rows = lax.broadcasted_iota(jnp.int32, (width, width), 0)
@@ -158,11 +162,19 @@
             if j == 0:
                 edge_ref[...] = times_matrix(state[q], lower_ref[0], NN)
                 ends_ref[1:2, :] = (on * times(split_row(local[q]), lower_ref[0], NN))[:1]
-    while len(state) > 1:
-        pairs = zip(state[::2], state[1::2])
-        state = [jnp.dot(a, b, precision=lax.Precision.HIGHEST) for a, b in pairs]
-    total_ref[...] = state[0]
-    ends_ref[0:1, :] = chain_end(local, maps_ref, length)
+    span = 1
+    while span < CHAINS:
+        state = [
+            state[q] if q < span else jnp.dot(state[q - span], state[q], precision=lax.Precision.HIGHEST)
+            for q in range(CHAINS)
+        ]
+        span *= 2
+    for q in range(CHAINS - 1):
+        through_ref[q] = state[q]
+    total_ref[...] = state[-1]
+    ends = chain_ends(local, maps_ref, length)
+    ends_ref[0:1, :] = ends[-1]
+    begins_ref[...] = jnp.concatenate(ends, axis=0)
     for copy in copies[-2:]:
         copy.wait()
 
@@ -179,7 +191,7 @@
     send_ends(ends_ref[0:1, :], ends_ref[1:2, :], dots, other_ref, pos_ref, n_track, send_ref)
 
 
-def direction_kernel(cap, n_track, recv_ref, local_ref, maps_ref, other_ref, coupling_ref, *refs):
+def direction_kernel(cap, n_track, recv_ref, local_ref, begins_ref, maps_ref, through_ref, other_ref, coupling_ref, *refs):
     chip_refs, (pos_ref, value_ref, first_ref, second_ref, entry_ref) = refs[:-5], refs[-5:]
     track, strip = pos_ref[0], pos_ref[1]
     width = local_ref.shape[1]
@@ -212,8 +224,7 @@
     entry_ref[...] = entry
     columns = [spread(entry)]
     for q in range(1, CHAINS):
-        last = q * length - 1
-        begin = local_ref[last : last + 1, :] + times_f32(columns[-1], maps_ref[last])
+        begin = begins_ref[q - 1 : q, :] + times_f32(columns[0], through_ref[q - 1])
         columns.append(spread(begin))
     even = strip % 2 == 0
     for j in range(cap):
@@ -248,8 +259,8 @@
 
 
 def update_kernel(
-    cap, n_track, first, base_ref, first_ref, second_ref, recv_ref, value_ref, state_ref, edge_map_ref, coupling_ref,
-    lower_ref, precond_ref, maps_ref, other_ref, links_ref, pos_ref, next_ref, local_ref, send_ref,
+    cap, n_track, n_strip, first, base_ref, first_ref, second_ref, recv_ref, value_ref, state_ref, edge_map_ref, coupling_ref,
+    lower_ref, precond_ref, maps_ref, other_ref, links_ref, pos_ref, next_ref, local_ref, begins_ref, send_ref,
 ):
     track, strip, count = pos_ref[0], pos_ref[1], pos_ref[2]
     width = base_ref.shape[1]
@@ -257,8 +268,8 @@
     odd = strip % 2 == 1
     image_ref = next_ref.at[1]
     one, two = first_ref[...], second_ref[...]
-    below = jnp.where(odd, one, two)
-    above = jnp.where(odd, two, one)
+    below = jnp.where(strip > 0, jnp.where(odd, one, two), 0.0)
+    above = jnp.where(strip < n_strip - 1, jnp.where(odd, two, one), 0.0)
     ahead = recv_ref[strip * n_track + jnp.minimum(track + 1, n_track - 1)]
     ahead = jnp.concatenate([ahead[h : h + 1] for h in range(width // 128)], axis=1)
     ahead = ahead + times_f32(spread(value_ref[pl.ds(count - 1, 1), :]), edge_map_ref[...])
@@ -301,11 +312,13 @@
             local_ref[j : j + 1, :] = state[q][:1]
             if j == 0:
                 edge = link(links_ref, pos_ref, 0) * times(split_row(state[q]), lower_ref[0], NN)
-    send_ends(chain_end(state, maps_ref, length), edge[:1], dots, other_ref, pos_ref, n_track, send_ref)
-
-
-def last_update_kernel(cap, n_track, *refs):
-    update_kernel(cap, n_track, False, *refs[:-1], None, refs[-1])
+    ends = chain_ends(state, maps_ref, length)
+    begins_ref[...] = jnp.concatenate(ends, axis=0)
+    send_ends(ends[-1], edge[:1], dots, other_ref, pos_ref, n_track, send_ref)
+
+
+def last_update_kernel(cap, n_track, n_strip, *refs):
+    update_kernel(cap, n_track, n_strip, False, *refs[:-1], None, None, refs[-1])
 
 
 def final_kernel(recv_ref, state_ref, solution_ref, residual_ref):
@@ -345,14 +358,18 @@
     square = (width, width)
     stack = (cap, width, width)
     chunk = (whole, width // 128 + 2, 128)
+    chain = (CHAINS, width)
     swap = [(i, i ^ 1) for i in range(n_track)]
 
-    maps, total, edge_map, local, ends, lower, precond, diag, coupling = call(
+    maps, total, edge_map, local, ends, begins, through, lower, precond, diag, coupling = call(
         functools.partial(maps_kernel, cap),
-        [stack, square, square, block, (2, width)] + [(stack, jnp.bfloat16)] * 4,
-        [HBM] * 5 + [SMEM] * 2,
-        rhs, lower_blocks[0], precond_blocks[0], principal_tiles[0], coupling_blocks[0], links, pos,
-        scratch=[pltpu.VMEM(block, F32), pltpu.SemaphoreType.DMA((4 * CHAINS + 3,))],
+        [stack, square, square, block, (2, width), chain, (CHAINS - 1,) + square] + [(stack, jnp.bfloat16)] * 4,
+        [HBM] * 6 + [SMEM],
+        rhs, links, lower_blocks[0], precond_blocks[0], principal_tiles[0], coupling_blocks[0], pos,
+        scratch=[
+            pltpu.VMEM(block, F32), pltpu.SMEM(links.shape, jnp.int32),
+            pltpu.SemaphoreType.DMA((4 * CHAINS + 4,)),
+        ],
     )
     other = lax.ppermute(total, "track", swap)
     chip, send = call(
@@ -367,7 +384,7 @@
     ]
     state = rhs
     pairs = [(i, i ^ 1) for i in range(n_strip) if i ^ 1 < n_strip]
-    cross = [(i, j) for k in range(1, n_strip - 1, 2) for i, j in ((k, k + 1), (k + 1, k))]
+    cross = [(i, (i + 1 if i % 2 else i - 1) % n_strip) for i in range(n_strip)]
     for step_number in range(ITERS):
         recv = lax.all_to_all(send, ("strip", "track"), 0, 0)
         if step_number == 0:
@@ -376,12 +393,12 @@
         value, first, second, entry = call(
             functools.partial(direction_kernel, cap, n_track),
             [block, block, block, (1, width)],
-            [VMEM] * (5 + len(nearer)) + [SMEM],
-            recv, local, maps, other, coupling, *nearer, pos,
+            [VMEM] * (7 + len(nearer)) + [SMEM],
+            recv, local, begins, maps, through, other, coupling, *nearer, pos,
         )
         if step_number == 0:
             edge_map, entry = lax.optimization_barrier((edge_map, entry))
-            edge_map = lax.ppermute(edge_map, "track", [(i + 1, i) for i in range(n_track - 1)])
+            edge_map = lax.ppermute(edge_map, "track", [((i + 1) % n_track, i) for i in range(n_track)])
         first = lax.ppermute(first, "strip", pairs)
         second = lax.ppermute(second, "strip", cross)
         base, = call(
@@ -393,10 +410,10 @@
         args = (base, first, second, recv, value, state, edge_map, coupling, lower, precond, maps, other, links, pos)
         specs = [VMEM] * 12 + [SMEM] * 2
         if step_number < ITERS - 1:
-            kernel = functools.partial(update_kernel, cap, n_track, step_number == 0)
-            state, local, send = call(kernel, [(4,) + block, block, chunk], specs, *args)
+            kernel = functools.partial(update_kernel, cap, n_track, n_strip, step_number == 0)
+            state, local, begins, send = call(kernel, [(4,) + block, block, chain, chunk], specs, *args)
         else:
-            kernel = functools.partial(last_update_kernel, cap, n_track)
+            kernel = functools.partial(last_update_kernel, cap, n_track, n_strip)
             state, send = call(kernel, [(4,) + block, chunk], specs, *args)
     recv = lax.all_to_all(send, ("strip", "track"), 0, 0)
     solution, residual = call(final_kernel, [block, block], [VMEM] * 2, recv, state)

time: 156 us -> 152 us (0.974)
  blocking collectives: 88.9 us -> 72.4 us
  waiting for transfers between devices: 3.58 us -> 13.3 us
  starting transfers between devices: 11.9 us -> 16 us
    all_to_all x7, blocking collectives: 88.9 us -> 72.4 us  [body(): recv = lax.all_to_all(send, ('strip', 'track'), 0, 0)]
    ppermute x6, waiting for transfers between devices: 0.02 us -> 11 us  [body(): second = lax.ppermute(second, 'strip', cross)]
    ppermute x6, starting transfers between devices: 4.3 us -> 9.02 us  [body(): second = lax.ppermute(second, 'strip', cross)]
  transfers between devices with their start and end apart: 18 -> 18, of which waited for: 9 -> 9; matrix products, arithmetic and copies ran while one was open for 0% -> 0% of each run, Pallas kernels for 8% -> 9%
where the time goes in v3:
time: 152 us
  blocking collectives  72.4 us (48%)
  Pallas kernels  48.4 us (32%)
  starting transfers between devices  16 us (11%)
  waiting for transfers between devices  13.3 us (9%)
    all_to_all x7, blocking collectives, body(): recv = lax.all_to_all(send, ('strip', 'track'), 0, 0)  72.4 us
    pallas_call x21, Pallas kernels, call(): pl.pallas_call(kernel, out_shape=[pltpu.VMEM(shape, dtype) if math.prod(s...  48.4 us
    ppermute x6, waiting for transfers between devices, body(): second = lax.ppermute(second, 'strip', cross)  11 us
    ppermute x6, starting transfers between devices, body(): second = lax.ppermute(second, 'strip', cross)  9.02 us
    ppermute x6, starting transfers between devices, body(): first = lax.ppermute(first, 'strip', pairs)  3.96 us
  transfers between devices with their start and end apart: 18, of which 9 were waited for; matrix products, arithmetic and copies ran while one was open for 0% of the time, Pallas kernels for 9%

profile of v3, /device:TPU:0, one launch (start us, length us, event | category | flops | bytes accessed | tf_op | source)
XLA Modules:
  0.0 151.7 jit_solution(11884846459590465418)
XLA Ops:
  1.3 0.1 pad_add_fusion.pos_ref.refs_4_.refs_13_
  1.4 8.1 %shard_map.86 = (f32[16,256,256]{2,1,0:T(8,128)S(1)}, f32[256,256]{1,0:T(8,128)S(1)}, f32[256,256]{1,0:T(8,128)S(1)}, f32[16,256]{1,0:T(8,128)S(1)}, f32[2,256]{...) custom-call(f32[16,256]{1,0:T(8,128)} %bitcast.9, ...), custom_call_target="tpu_custom_call" | custom-call | tf_op jit(solution)/shard_map/pallas_call | solution.py:336
  9.5 0.5 collective-permute-start
  10.0 1.2 collective-permute-done.other_ref.refs_11_
  11.1 0.8 shard_map.87
  12.0 0.7 collective-permute-start.1
  12.7 0.7 collective-permute-start.2
  13.3 16.9 %all_to_all.35.recv_ref = f32[32,4,128]{2,1,0:T(4,128)S(1)} all-to-all(f32[32,4,128]{2,1,0:T(4,128)S(1)} %get-tuple-element.75), channel_id=1, replica_groups=mesh['track'=8,'strip'=4] {'strip','track'}, dimensions={0} | all-to-all | bytes 131072 | tf_op jit(solution)/shard_map/all_to_all | solution.py:389
  30.2 0.0 collective-permute-done.1.refs_0_
  30.2 0.1 collective-permute-start.3
  30.3 0.4 collective-permute-start.4
  30.7 0.8 collective-permute-done.3.refs_2_
  31.6 0.2 collective-permute-done.4.refs_3_
  31.7 1.7 %shard_map.88 = (f32[16,256]{1,0:T(8,128)S(1)}, f32[16,256]{1,0:T(8,128)S(1)}, f32[16,256]{1,0:T(8,128)S(1)}, f32[1,256]{1,0:T(1,128)S(1)}) custom-call(f32[32,4,128]{2,1,0:T(4,128)S(1)} %all_to_all.35.recv_ref, f32[16,256]{1,0:T(8,128)S(1)} %get-tuple-element.78.local_ref, f32[4,256]{1,0:T(4,128)S(1)} %get-tuple-element.79.begins_ref, ...), custom_call_target="tpu_custom_call" | custom-call | tf_op jit(solution)/shard_map/pallas_call | solution.py:336
  33.4 0.7 collective-permute-start.7
  34.1 0.6 collective-permute-start.5
  34.8 1.4 collective-permute-start.6
  36.1 2.2 %shard_map.89.base_ref = f32[16,256]{1,0:T(8,128)S(1)} custom-call(f32[16,256]{1,0:T(8,128)S(1)} %get-tuple-element.83.value_ref, f32[1,256]{1,0:T(1,128)S(1)} %get-tuple-element.86.entry_ref, bf16[16,256,256]{2,1,0:T(8,128)(2,1)S(1)} %get-tuple-element.73.refs_3_.diag_ref, bf16[16,256,256]{2,1,0:T(8,128)(2,1)S(1)} %get-tuple-element.71.refs_1_.lower_ref.refs_8_, ...), custom_call_target="tpu_custom_call" | custom-call | tf_op jit(solution)/shard_map/pallas_call | solution.py:336
  38.3 0.0 collective-permute-done.5.first_ref
  38.3 2.0 %collective-permute-done.6.second_ref = f32[16,256]{1,0:T(8,128)S(1)} collective-permute-done((f32[16,256]{1,0:T(8,128)S(1)}, f32[16,256]{1,0:T(8,128)S(1)}, u32[]{:S(2)}, u32[]{:S(2)}) %collective-permute-start.6) | collective-permute-done | bytes 16416 | tf_op jit(solution)/shard_map/ppermute | solution.py:403
  40.3 0.0 collective-permute-done.7.edge_map_ref.refs_6_
  40.3 2.9 %shard_map.90 = (f32[4,16,256]{2,1,0:T(8,128)S(1)}, f32[16,256]{1,0:T(8,128)S(1)}, f32[4,256]{1,0:T(4,128)S(1)}, f32[32,4,128]{2,1,0:T(4,128)S(1)}) custom-call(f32[16,256]{1,0:T(8,128)S(1)} %shard_map.89.base_ref, f32[16,256]{1,0:T(8,128)S(1)} %collective-permute-done.5.first_ref, f32[16,256]{1,0:T(8,128)S(1)} %collective-permute-done.6.second_ref, ...), custom_call_target="tpu_custom_call" | custom-call | tf_op jit(solution)/shard_map/pallas_call | solution.py:336
  43.2 9.8 %all_to_all.36.recv_ref = f32[32,4,128]{2,1,0:T(4,128)S(1)} all-to-all(f32[32,4,128]{2,1,0:T(4,128)S(1)} %get-tuple-element.90), channel_id=1, replica_groups=mesh['track'=8,'strip'=4] {'strip','track'}, dimensions={0} | all-to-all | bytes 131072 | tf_op jit(solution)/shard_map/all_to_all | solution.py:389
  53.0 1.7 %shard_map.91 = (f32[16,256]{1,0:T(8,128)S(1)}, f32[16,256]{1,0:T(8,128)S(1)}, f32[16,256]{1,0:T(8,128)S(1)}, f32[1,256]{1,0:T(1,128)S(1)}) custom-call(f32[32,4,128]{2,1,0:T(4,128)S(1)} %all_to_all.36.recv_ref, f32[16,256]{1,0:T(8,128)S(1)} %get-tuple-element.91.local_ref, f32[4,256]{1,0:T(4,128)S(1)} %get-tuple-element.92.begins_ref, ...), custom_call_target="tpu_custom_call" | custom-call | tf_op jit(solution)/shard_map/pallas_call | solution.py:336
  54.7 0.7 collective-permute-start.8
  55.4 1.5 %collective-permute-start.9 = (f32[16,256]{1,0:T(8,128)S(1)}, f32[16,256]{1,0:T(8,128)S(1)}, u32[]{:S(2)}, u32[]{:S(2)}) collective-permute-start(f32[16,256]{1,0:T(8,128)S(1)} %get-tuple-element.96), channel_id=1, source_target_pairs={{0,3},{1,2},{2,1},{3,0},{4,7},{5,6},{6,5},{7,4},{8,11},{9,10},{10,... | collective-permute-start | bytes 49160 | tf_op jit(solution)/shard_map/ppermute | solution.py:403
  56.9 2.2 %shard_map.92.base_ref = f32[16,256]{1,0:T(8,128)S(1)} custom-call(f32[16,256]{1,0:T(8,128)S(1)} %get-tuple-element.93.value_ref, f32[1,256]{1,0:T(1,128)S(1)} %get-tuple-element.94.entry_ref, bf16[16,256,256]{2,1,0:T(8,128)(2,1)S(1)} %get-tuple-element.73.refs_3_.diag_ref, bf16[16,256,256]{2,1,0:T(8,128)(2,1)S(1)} %get-tuple-element.71.refs_1_.lower_ref.refs_8_, ...), custom_call_target="tpu_custom_call" | custom-call | tf_op jit(solution)/shard_map/pallas_call | solution.py:336
  59.1 0.0 collective-permute-done.8.first_ref
  59.1 1.8 %collective-permute-done.9.second_ref = f32[16,256]{1,0:T(8,128)S(1)} collective-permute-done((f32[16,256]{1,0:T(8,128)S(1)}, f32[16,256]{1,0:T(8,128)S(1)}, u32[]{:S(2)}, u32[]{:S(2)}) %collective-permute-start.9) | collective-permute-done | bytes 16416 | tf_op jit(solution)/shard_map/ppermute | solution.py:403
  60.9 2.9 %shard_map.93 = (f32[4,16,256]{2,1,0:T(8,128)S(1)}, f32[16,256]{1,0:T(8,128)S(1)}, f32[4,256]{1,0:T(4,128)S(1)}, f32[32,4,128]{2,1,0:T(4,128)S(1)}) custom-call(f32[16,256]{1,0:T(8,128)S(1)} %shard_map.92.base_ref, f32[16,256]{1,0:T(8,128)S(1)} %collective-permute-done.8.first_ref, f32[16,256]{1,0:T(8,128)S(1)} %collective-permute-done.9.second_ref, ...), custom_call_target="tpu_custom_call" | custom-call | tf_op jit(solution)/shard_map/pallas_call | solution.py:336
  63.8 9.1 %all_to_all.37.recv_ref = f32[32,4,128]{2,1,0:T(4,128)S(1)} all-to-all(f32[32,4,128]{2,1,0:T(4,128)S(1)} %get-tuple-element.98), channel_id=1, replica_groups=mesh['track'=8,'strip'=4] {'strip','track'}, dimensions={0} | all-to-all | bytes 131072 | tf_op jit(solution)/shard_map/all_to_all | solution.py:389
  72.9 1.7 %shard_map.94 = (f32[16,256]{1,0:T(8,128)S(1)}, f32[16,256]{1,0:T(8,128)S(1)}, f32[16,256]{1,0:T(8,128)S(1)}, f32[1,256]{1,0:T(1,128)S(1)}) custom-call(f32[32,4,128]{2,1,0:T(4,128)S(1)} %all_to_all.37.recv_ref, f32[16,256]{1,0:T(8,128)S(1)} %get-tuple-element.99.local_ref, f32[4,256]{1,0:T(4,128)S(1)} %get-tuple-element.100.begins_ref, ...), custom_call_target="tpu_custom_call" | custom-call | tf_op jit(solution)/shard_map/pallas_call | solution.py:336
  74.6 0.7 collective-permute-start.10
  75.2 1.5 %collective-permute-start.11 = (f32[16,256]{1,0:T(8,128)S(1)}, f32[16,256]{1,0:T(8,128)S(1)}, u32[]{:S(2)}, u32[]{:S(2)}) collective-permute-start(f32[16,256]{1,0:T(8,128)S(1)} %get-tuple-element.104), channel_id=1, source_target_pairs={{0,3},{1,2},{2,1},{3,0},{4,7},{5,6},{6,5},{7,4},{8,11},{9,10},{10,... | collective-permute-start | bytes 49160 | tf_op jit(solution)/shard_map/ppermute | solution.py:403
  76.8 2.2 %shard_map.95.base_ref = f32[16,256]{1,0:T(8,128)S(1)} custom-call(f32[16,256]{1,0:T(8,128)S(1)} %get-tuple-element.101.value_ref, f32[1,256]{1,0:T(1,128)S(1)} %get-tuple-element.102.entry_ref, bf16[16,256,256]{2,1,0:T(8,128)(2,1)S(1)} %get-tuple-element.73.refs_3_.diag_ref, bf16[16,256,256]{2,1,0:T(8,128)(2,1)S(1)} %get-tuple-element.71.refs_1_.lower_ref.refs_8_, ...), custom_call_target="tpu_custom_call" | custom-call | tf_op jit(solution)/shard_map/pallas_call | solution.py:336
  79.0 0.0 collective-permute-done.10.first_ref
  79.0 1.8 %collective-permute-done.11.second_ref = f32[16,256]{1,0:T(8,128)S(1)} collective-permute-done((f32[16,256]{1,0:T(8,128)S(1)}, f32[16,256]{1,0:T(8,128)S(1)}, u32[]{:S(2)}, u32[]{:S(2)}) %collective-permute-start.11) | collective-permute-done | bytes 16416 | tf_op jit(solution)/shard_map/ppermute | solution.py:403
  80.8 2.9 %shard_map.96 = (f32[4,16,256]{2,1,0:T(8,128)S(1)}, f32[16,256]{1,0:T(8,128)S(1)}, f32[4,256]{1,0:T(4,128)S(1)}, f32[32,4,128]{2,1,0:T(4,128)S(1)}) custom-call(f32[16,256]{1,0:T(8,128)S(1)} %shard_map.95.base_ref, f32[16,256]{1,0:T(8,128)S(1)} %collective-permute-done.10.first_ref, f32[16,256]{1,0:T(8,128)S(1)} %collective-permute-done.11.second_ref, ...), custom_call_target="tpu_custom_call" | custom-call | tf_op jit(solution)/shard_map/pallas_call | solution.py:336
  83.7 9.1 %all_to_all.38.recv_ref = f32[32,4,128]{2,1,0:T(4,128)S(1)} all-to-all(f32[32,4,128]{2,1,0:T(4,128)S(1)} %get-tuple-element.106), channel_id=1, replica_groups=mesh['track'=8,'strip'=4] {'strip','track'}, dimensions={0} | all-to-all | bytes 131072 | tf_op jit(solution)/shard_map/all_to_all | solution.py:389
  92.8 1.7 %shard_map.97 = (f32[16,256]{1,0:T(8,128)S(1)}, f32[16,256]{1,0:T(8,128)S(1)}, f32[16,256]{1,0:T(8,128)S(1)}, f32[1,256]{1,0:T(1,128)S(1)}) custom-call(f32[32,4,128]{2,1,0:T(4,128)S(1)} %all_to_all.38.recv_ref, f32[16,256]{1,0:T(8,128)S(1)} %get-tuple-element.107.local_ref, f32[4,256]{1,0:T(4,128)S(1)} %get-tuple-element.108.begins_ref, ...), custom_call_target="tpu_custom_call" | custom-call | tf_op jit(solution)/shard_map/pallas_call | solution.py:336
  94.5 0.7 collective-permute-start.12
  95.1 1.5 %collective-permute-start.13 = (f32[16,256]{1,0:T(8,128)S(1)}, f32[16,256]{1,0:T(8,128)S(1)}, u32[]{:S(2)}, u32[]{:S(2)}) collective-permute-start(f32[16,256]{1,0:T(8,128)S(1)} %get-tuple-element.112), channel_id=1, source_target_pairs={{0,3},{1,2},{2,1},{3,0},{4,7},{5,6},{6,5},{7,4},{8,11},{9,10},{10,... | collective-permute-start | bytes 49160 | tf_op jit(solution)/shard_map/ppermute | solution.py:403
  96.7 2.2 %shard_map.98.base_ref = f32[16,256]{1,0:T(8,128)S(1)} custom-call(f32[16,256]{1,0:T(8,128)S(1)} %get-tuple-element.109.value_ref, f32[1,256]{1,0:T(1,128)S(1)} %get-tuple-element.110.entry_ref, bf16[16,256,256]{2,1,0:T(8,128)(2,1)S(1)} %get-tuple-element.73.refs_3_.diag_ref, bf16[16,256,256]{2,1,0:T(8,128)(2,1)S(1)} %get-tuple-element.71.refs_1_.lower_ref.refs_8_, ...), custom_call_target="tpu_custom_call" | custom-call | tf_op jit(solution)/shard_map/pallas_call | solution.py:336
  98.8 0.0 collective-permute-done.12.first_ref
  98.9 1.8 %collective-permute-done.13.second_ref = f32[16,256]{1,0:T(8,128)S(1)} collective-permute-done((f32[16,256]{1,0:T(8,128)S(1)}, f32[16,256]{1,0:T(8,128)S(1)}, u32[]{:S(2)}, u32[]{:S(2)}) %collective-permute-start.13) | collective-permute-done | bytes 16416 | tf_op jit(solution)/shard_map/ppermute | solution.py:403
  100.7 2.9 %shard_map.99 = (f32[4,16,256]{2,1,0:T(8,128)S(1)}, f32[16,256]{1,0:T(8,128)S(1)}, f32[4,256]{1,0:T(4,128)S(1)}, f32[32,4,128]{2,1,0:T(4,128)S(1)}) custom-call(f32[16,256]{1,0:T(8,128)S(1)} %shard_map.98.base_ref, f32[16,256]{1,0:T(8,128)S(1)} %collective-permute-done.12.first_ref, f32[16,256]{1,0:T(8,128)S(1)} %collective-permute-done.13.second_ref, ...), custom_call_target="tpu_custom_call" | custom-call | tf_op jit(solution)/shard_map/pallas_call | solution.py:336
  103.6 9.1 %all_to_all.39.recv_ref = f32[32,4,128]{2,1,0:T(4,128)S(1)} all-to-all(f32[32,4,128]{2,1,0:T(4,128)S(1)} %get-tuple-element.114), channel_id=1, replica_groups=mesh['track'=8,'strip'=4] {'strip','track'}, dimensions={0} | all-to-all | bytes 131072 | tf_op jit(solution)/shard_map/all_to_all | solution.py:389
  112.7 1.7 %shard_map.100 = (f32[16,256]{1,0:T(8,128)S(1)}, f32[16,256]{1,0:T(8,128)S(1)}, f32[16,256]{1,0:T(8,128)S(1)}, f32[1,256]{1,0:T(1,128)S(1)}) custom-call(f32[32,4,128]{2,1,0:T(4,128)S(1)} %all_to_all.39.recv_ref, f32[16,256]{1,0:T(8,128)S(1)} %get-tuple-element.115.local_ref, f32[4,256]{1,0:T(4,128)S(1)} %get-tuple-element.116.begins_ref, ...), custom_call_target="tpu_custom_call" | custom-call | tf_op jit(solution)/shard_map/pallas_call | solution.py:336
  114.4 0.7 collective-permute-start.14
  115.0 1.5 %collective-permute-start.15 = (f32[16,256]{1,0:T(8,128)S(1)}, f32[16,256]{1,0:T(8,128)S(1)}, u32[]{:S(2)}, u32[]{:S(2)}) collective-permute-start(f32[16,256]{1,0:T(8,128)S(1)} %get-tuple-element.120), channel_id=1, source_target_pairs={{0,3},{1,2},{2,1},{3,0},{4,7},{5,6},{6,5},{7,4},{8,11},{9,10},{10,... | collective-permute-start | bytes 49160 | tf_op jit(solution)/shard_map/ppermute | solution.py:403
  116.6 2.2 %shard_map.101.base_ref = f32[16,256]{1,0:T(8,128)S(1)} custom-call(f32[16,256]{1,0:T(8,128)S(1)} %get-tuple-element.117.value_ref, f32[1,256]{1,0:T(1,128)S(1)} %get-tuple-element.118.entry_ref, bf16[16,256,256]{2,1,0:T(8,128)(2,1)S(1)} %get-tuple-element.73.refs_3_.diag_ref, bf16[16,256,256]{2,1,0:T(8,128)(2,1)S(1)} %get-tuple-element.71.refs_1_.lower_ref.refs_8_, ...), custom_call_target="tpu_custom_call" | custom-call | tf_op jit(solution)/shard_map/pallas_call | solution.py:336
  118.7 0.0 collective-permute-done.14.first_ref
  118.8 1.8 %collective-permute-done.15.second_ref = f32[16,256]{1,0:T(8,128)S(1)} collective-permute-done((f32[16,256]{1,0:T(8,128)S(1)}, f32[16,256]{1,0:T(8,128)S(1)}, u32[]{:S(2)}, u32[]{:S(2)}) %collective-permute-start.15) | collective-permute-done | bytes 16416 | tf_op jit(solution)/shard_map/ppermute | solution.py:403
  120.6 2.9 %shard_map.102 = (f32[4,16,256]{2,1,0:T(8,128)S(1)}, f32[16,256]{1,0:T(8,128)S(1)}, f32[4,256]{1,0:T(4,128)S(1)}, f32[32,4,128]{2,1,0:T(4,128)S(1)}) custom-call(f32[16,256]{1,0:T(8,128)S(1)} %shard_map.101.base_ref, f32[16,256]{1,0:T(8,128)S(1)} %collective-permute-done.14.first_ref, f32[16,256]{1,0:T(8,128)S(1)} %collective-permute-done.15.second_ref, ...), custom_call_target="tpu_custom_call" | custom-call | tf_op jit(solution)/shard_map/pallas_call | solution.py:336
  123.4 9.1 %all_to_all.40.recv_ref.refs_3_ = f32[32,4,128]{2,1,0:T(4,128)S(1)} all-to-all(f32[32,4,128]{2,1,0:T(4,128)S(1)} %get-tuple-element.122), channel_id=1, replica_groups=mesh['track'=8,'strip'=4] {'strip','track'}, dimensions={0} | all-to-all | bytes 131072 | tf_op jit(solution)/shard_map/all_to_all | solution.py:389
  132.6 1.7 %shard_map.103 = (f32[16,256]{1,0:T(8,128)S(1)}, f32[16,256]{1,0:T(8,128)S(1)}, f32[16,256]{1,0:T(8,128)S(1)}, f32[1,256]{1,0:T(1,128)S(1)}) custom-call(f32[32,4,128]{2,1,0:T(4,128)S(1)} %all_to_all.40.recv_ref.refs_3_, f32[16,256]{1,0:T(8,128)S(1)} %get-tuple-element.123.local_ref, f32[4,256]{1,0:T(4,128)S(1)} %get-tuple-element.124.begins_ref, ...), custom_call_target="tpu_custom_call" | custom-call | tf_op jit(solution)/shard_map/pallas_call | solution.py:336
  134.3 0.7 collective-permute-start.16
  134.9 1.5 %collective-permute-start.17 = (f32[16,256]{1,0:T(8,128)S(1)}, f32[16,256]{1,0:T(8,128)S(1)}, u32[]{:S(2)}, u32[]{:S(2)}) collective-permute-start(f32[16,256]{1,0:T(8,128)S(1)} %get-tuple-element.128), channel_id=1, source_target_pairs={{0,3},{1,2},{2,1},{3,0},{4,7},{5,6},{6,5},{7,4},{8,11},{9,10},{10,... | collective-permute-start | bytes 49160 | tf_op jit(solution)/shard_map/ppermute | solution.py:403
  136.5 2.2 %shard_map.104.refs_0_ = f32[16,256]{1,0:T(8,128)S(1)} custom-call(f32[16,256]{1,0:T(8,128)S(1)} %get-tuple-element.125.value_ref.refs_4_, f32[1,256]{1,0:T(1,128)S(1)} %get-tuple-element.126.entry_ref, bf16[16,256,256]{2,1,0:T(8,128)(2,1)S(1)} %get-tuple-element.73.refs_3_.diag_ref, bf16[16,256,256]{2,1,0:T(8,128)(2,1)S(1)} %get-tuple-element.71.refs_1_.lower_ref.refs_8_, ...), custom_call_target="tpu_custom_call" | custom-call | tf_op jit(solution)/shard_map/pallas_call | solution.py:336
  138.6 0.0 collective-permute-done.16.refs_1_
  138.7 1.8 %collective-permute-done.17.refs_2_ = f32[16,256]{1,0:T(8,128)S(1)} collective-permute-done((f32[16,256]{1,0:T(8,128)S(1)}, f32[16,256]{1,0:T(8,128)S(1)}, u32[]{:S(2)}, u32[]{:S(2)}) %collective-permute-start.17) | collective-permute-done | bytes 16416 | tf_op jit(solution)/shard_map/ppermute | solution.py:403
  140.5 1.3 shard_map.105
  141.8 9.1 %all_to_all.41.recv_ref = f32[32,4,128]{2,1,0:T(4,128)S(1)} all-to-all(f32[32,4,128]{2,1,0:T(4,128)S(1)} %get-tuple-element.130), channel_id=1, replica_groups=mesh['track'=8,'strip'=4] {'strip','track'}, dimensions={0} | all-to-all | bytes 131072 | tf_op jit(solution)/shard_map/all_to_all | solution.py:418
  150.9 0.8 shard_map.106
  (5 shorter events, 0.0 us)
Async XLA Ops:
  9.5 1.7 %collective-permute-start = (f32[256,256]{1,0:T(8,128)S(1)}, f32[256,256]{1,0:T(8,128)S(1)}, u32[]{:S(2)}, u32[]{:S(2)}) collective-permute-start(f32[256,256]{1,0:T(8,128)S(1)} %get-tuple-element.68.total_ref), channel_id=1, source_target_pairs={{0,4},{4,0},{8,12},{12,8},{16,20},{20,16},{24,28},{28,24},{1,5},{5... | collective-permute-start | bytes 786440 | tf_op jit(solution)/shard_map/ppermute | solution.py:374
  12.0 18.2 %collective-permute-start.1 = (f32[128,256]{1,0:T(8,128)S(1)}, f32[128,256]{1,0:T(8,128)S(1)}, u32[]{:S(2)}, u32[]{:S(2)}) collective-permute-start(f32[128,256]{1,0:T(8,128)S(1)} %get-tuple-element.76), channel_id=1, source_target_pairs={{8,16},{12,20},{16,24},{20,28},{9,17},{13,21},{17,25},{21,29},{10,... | collective-permute-start | bytes 393224 | tf_op jit(solution)/shard_map/ppermute | solution.py:382
  12.7 17.5 %collective-permute-start.2 = (f32[128,256]{1,0:T(8,128)S(1)}, f32[128,256]{1,0:T(8,128)S(1)}, u32[]{:S(2)}, u32[]{:S(2)}) collective-permute-start(f32[128,256]{1,0:T(8,128)S(1)} %get-tuple-element.76), channel_id=1, source_target_pairs={{8,24},{12,28},{9,25},{13,29},{10,26},{14,30},{11,27},{15,31}} | collective-permute-start | bytes 393224 | tf_op jit(solution)/shard_map/ppermute | solution.py:382
  30.2 1.4 collective-permute-start.3
  30.3 1.4 collective-permute-start.4
  31.7 4.4 %copy-start = (s32[1,16]{1,0:T(1,128)S(1)}, s32[1,16]{1,0:T(1,128)}, u32[]{:S(2)}) copy-start(s32[1,16]{1,0:T(1,128)} %refs_12_.1) | copy-start | bytes 196
  33.4 6.9 %collective-permute-start.7 = (f32[256,256]{1,0:T(8,128)S(1)}, f32[256,256]{1,0:T(8,128)S(1)}, u32[]{:S(2)}, u32[]{:S(2)}) collective-permute-start(f32[256,256]{1,0:T(8,128)S(1)} %get-tuple-element.89), channel_id=1, source_target_pairs={{4,0},{8,4},{12,8},{16,12},{20,16},{24,20},{28,24},{0,28},{5,1},{9... | collective-permute-start | bytes 786440 | tf_op jit(solution)/shard_map/ppermute | solution.py:401
  34.1 4.2 %collective-permute-start.5 = (f32[16,256]{1,0:T(8,128)S(1)}, f32[16,256]{1,0:T(8,128)S(1)}, u32[]{:S(2)}, u32[]{:S(2)}) collective-permute-start(f32[16,256]{1,0:T(8,128)S(1)} %get-tuple-element.87), channel_id=1, source_target_pairs={{0,1},{1,0},{2,3},{3,2},{4,5},{5,4},{6,7},{7,6},{8,9},{9,8},{10,11... | collective-permute-start | bytes 49160 | tf_op jit(solution)/shard_map/ppermute | solution.py:402
  34.8 5.5 %collective-permute-start.6 = (f32[16,256]{1,0:T(8,128)S(1)}, f32[16,256]{1,0:T(8,128)S(1)}, u32[]{:S(2)}, u32[]{:S(2)}) collective-permute-start(f32[16,256]{1,0:T(8,128)S(1)} %get-tuple-element.88), channel_id=1, source_target_pairs={{0,3},{1,2},{2,1},{3,0},{4,7},{5,6},{6,5},{7,4},{8,11},{9,10},{10,... | collective-permute-start | bytes 49160 | tf_op jit(solution)/shard_map/ppermute | solution.py:403
  36.1 4.2 %copy-start.1 = (f32[1,16,256]{2,1,0:T(8,128)S(1)}, f32[1,16,256]{2,1,0:T(8,128)}, u32[]{:S(2)}) copy-start(f32[1,16,256]{2,1,0:T(8,128)} %param.7) | copy-start | bytes 49156
  54.7 4.4 %collective-permute-start.8 = (f32[16,256]{1,0:T(8,128)S(1)}, f32[16,256]{1,0:T(8,128)S(1)}, u32[]{:S(2)}, u32[]{:S(2)}) collective-permute-start(f32[16,256]{1,0:T(8,128)S(1)} %get-tuple-element.95), channel_id=1, source_target_pairs={{0,1},{1,0},{2,3},{3,2},{4,5},{5,4},{6,7},{7,6},{8,9},{9,8},{10,11... | collective-permute-start | bytes 49160 | tf_op jit(solution)/shard_map/ppermute | solution.py:402
  55.4 5.5 %collective-permute-start.9 = (f32[16,256]{1,0:T(8,128)S(1)}, f32[16,256]{1,0:T(8,128)S(1)}, u32[]{:S(2)}, u32[]{:S(2)}) collective-permute-start(f32[16,256]{1,0:T(8,128)S(1)} %get-tuple-element.96), channel_id=1, source_target_pairs={{0,3},{1,2},{2,1},{3,0},{4,7},{5,6},{6,5},{7,4},{8,11},{9,10},{10,... | collective-permute-start | bytes 49160 | tf_op jit(solution)/shard_map/ppermute | solution.py:403
  74.6 4.4 %collective-permute-start.10 = (f32[16,256]{1,0:T(8,128)S(1)}, f32[16,256]{1,0:T(8,128)S(1)}, u32[]{:S(2)}, u32[]{:S(2)}) collective-permute-start(f32[16,256]{1,0:T(8,128)S(1)} %get-tuple-element.103), channel_id=1, source_target_pairs={{0,1},{1,0},{2,3},{3,2},{4,5},{5,4},{6,7},{7,6},{8,9},{9,8},{10,11... | collective-permute-start | bytes 49160 | tf_op jit(solution)/shard_map/ppermute | solution.py:402
  75.2 5.5 %collective-permute-start.11 = (f32[16,256]{1,0:T(8,128)S(1)}, f32[16,256]{1,0:T(8,128)S(1)}, u32[]{:S(2)}, u32[]{:S(2)}) collective-permute-start(f32[16,256]{1,0:T(8,128)S(1)} %get-tuple-element.104), channel_id=1, source_target_pairs={{0,3},{1,2},{2,1},{3,0},{4,7},{5,6},{6,5},{7,4},{8,11},{9,10},{10,... | collective-permute-start | bytes 49160 | tf_op jit(solution)/shard_map/ppermute | solution.py:403
  94.5 4.4 %collective-permute-start.12 = (f32[16,256]{1,0:T(8,128)S(1)}, f32[16,256]{1,0:T(8,128)S(1)}, u32[]{:S(2)}, u32[]{:S(2)}) collective-permute-start(f32[16,256]{1,0:T(8,128)S(1)} %get-tuple-element.111), channel_id=1, source_target_pairs={{0,1},{1,0},{2,3},{3,2},{4,5},{5,4},{6,7},{7,6},{8,9},{9,8},{10,11... | collective-permute-start | bytes 49160 | tf_op jit(solution)/shard_map/ppermute | solution.py:402
  95.1 5.5 %collective-permute-start.13 = (f32[16,256]{1,0:T(8,128)S(1)}, f32[16,256]{1,0:T(8,128)S(1)}, u32[]{:S(2)}, u32[]{:S(2)}) collective-permute-start(f32[16,256]{1,0:T(8,128)S(1)} %get-tuple-element.112), channel_id=1, source_target_pairs={{0,3},{1,2},{2,1},{3,0},{4,7},{5,6},{6,5},{7,4},{8,11},{9,10},{10,... | collective-permute-start | bytes 49160 | tf_op jit(solution)/shard_map/ppermute | solution.py:403
  114.4 4.4 %collective-permute-start.14 = (f32[16,256]{1,0:T(8,128)S(1)}, f32[16,256]{1,0:T(8,128)S(1)}, u32[]{:S(2)}, u32[]{:S(2)}) collective-permute-start(f32[16,256]{1,0:T(8,128)S(1)} %get-tuple-element.119), channel_id=1, source_target_pairs={{0,1},{1,0},{2,3},{3,2},{4,5},{5,4},{6,7},{7,6},{8,9},{9,8},{10,11... | collective-permute-start | bytes 49160 | tf_op jit(solution)/shard_map/ppermute | solution.py:402
  115.0 5.5 %collective-permute-start.15 = (f32[16,256]{1,0:T(8,128)S(1)}, f32[16,256]{1,0:T(8,128)S(1)}, u32[]{:S(2)}, u32[]{:S(2)}) collective-permute-start(f32[16,256]{1,0:T(8,128)S(1)} %get-tuple-element.120), channel_id=1, source_target_pairs={{0,3},{1,2},{2,1},{3,0},{4,7},{5,6},{6,5},{7,4},{8,11},{9,10},{10,... | collective-permute-start | bytes 49160 | tf_op jit(solution)/shard_map/ppermute | solution.py:403
  134.3 4.4 %collective-permute-start.16 = (f32[16,256]{1,0:T(8,128)S(1)}, f32[16,256]{1,0:T(8,128)S(1)}, u32[]{:S(2)}, u32[]{:S(2)}) collective-permute-start(f32[16,256]{1,0:T(8,128)S(1)} %get-tuple-element.127), channel_id=1, source_target_pairs={{0,1},{1,0},{2,3},{3,2},{4,5},{5,4},{6,7},{7,6},{8,9},{9,8},{10,11... | collective-permute-start | bytes 49160 | tf_op jit(solution)/shard_map/ppermute | solution.py:402
  134.9 5.5 %collective-permute-start.17 = (f32[16,256]{1,0:T(8,128)S(1)}, f32[16,256]{1,0:T(8,128)S(1)}, u32[]{:S(2)}, u32[]{:S(2)}) collective-permute-start(f32[16,256]{1,0:T(8,128)S(1)} %get-tuple-element.128), channel_id=1, source_target_pairs={{0,3},{1,2},{2,1},{3,0},{4,7},{5,6},{6,5},{7,4},{8,11},{9,10},{10,... | collective-permute-start | bytes 49160 | tf_op jit(solution)/shard_map/ppermute | solution.py:403

commit v4 on v3

--- a/solution.py
+++ b/solution.py
@@ -236,19 +236,11 @@
         second_ref[j : j + 1, :] = jnp.where(even, crossed, masked)
 
 
-def local_kernel(cap, value_ref, entry_ref, diag_ref, lower_ref, links_ref, pos_ref, base_ref):
-    lowered = link(links_ref, pos_ref, 0) * times(split_row(wide_row(entry_ref, 0)), lower_ref[0], NT)
-    held = None
-    for j in range(cap):
-        lhs = split_row(wide_row(value_ref, j))
-        own = times(lhs, diag_ref[j], NT) + lowered
-        if j > 0:
-            held = held + link(links_ref, pos_ref, j) * times(lhs, lower_ref[j], NN)
-            base_ref[j - 1 : j, :] = held[:1]
-        if j < cap - 1:
-            lowered = link(links_ref, pos_ref, j + 1) * times(lhs, lower_ref[j + 1], NT)
-        held = own
-    base_ref[cap - 1 : cap, :] = held[:1]
+def flip_kernel(cap, *refs):
+    sources, targets = refs[: len(refs) // 2], refs[len(refs) // 2 :]
+    for source, target in zip(sources, targets):
+        for j in range(cap):
+            target[j] = jnp.transpose(source[j])
 
 
 def alpha_of(recv_ref, half):
@@ -258,15 +250,46 @@
     return inner / (energy + 1e-6)
 
 
+def local_kernel(
+    cap, first, value_ref, entry_ref, recv_ref, state_ref, image_ref, diag_flip_ref, lower_ref,
+    lower_flip_ref, links_ref, pos_ref, base_ref, next_ref, alpha_ref,
+):
+    width = value_ref.shape[1]
+    on = [link(links_ref, pos_ref, j) for j in range(cap)]
+    lowered = on[0] * times(split_row(wide_row(entry_ref, 0)), lower_flip_ref[0], NN)
+    held = None
+    for j in range(cap):
+        lhs = split_row(wide_row(value_ref, j))
+        own = times(lhs, diag_flip_ref[j], NN) + lowered
+        if j > 0:
+            held = held + on[j] * times(lhs, lower_ref[j], NN)
+            base_ref[j - 1 : j, :] = held[:1]
+        if j < cap - 1:
+            lowered = on[j + 1] * times(lhs, lower_flip_ref[j + 1], NN)
+        held = own
+    base_ref[cap - 1 : cap, :] = held[:1]
+    if first:
+        next_ref[0] = jnp.where(live_mask(pos_ref, (cap, width)), state_ref[...], 0.0)
+        next_ref[1] = value_ref[...]
+        next_ref[2] = jnp.zeros_like(value_ref[...])
+        alpha_ref[...] = jnp.zeros((1, width), F32)
+    else:
+        alpha = alpha_of(recv_ref, width // 128)
+        next_ref[0] = state_ref[0] - alpha * image_ref[...]
+        next_ref[1] = state_ref[1] - alpha * value_ref[...]
+        next_ref[2] = state_ref[2] + alpha * state_ref[1]
+        alpha_ref[...] = jnp.broadcast_to(alpha, (1, width))
+
+
 def update_kernel(
-    cap, n_track, n_strip, first, base_ref, first_ref, second_ref, recv_ref, value_ref, state_ref, edge_map_ref, coupling_ref,
-    lower_ref, precond_ref, maps_ref, other_ref, links_ref, pos_ref, next_ref, local_ref, begins_ref, send_ref,
+    cap, n_track, n_strip, first, base_ref, first_ref, second_ref, value_ref, recv_ref, state_ref, image_ref, alpha_ref,
+    edge_map_ref, coupling_flip_ref, lower_ref, lower_flip_ref, precond_flip_ref, maps_ref, other_ref, links_ref, pos_ref,
+    next_ref, local_ref, begins_ref, send_ref,
 ):
     track, strip, count = pos_ref[0], pos_ref[1], pos_ref[2]
     width = base_ref.shape[1]
     length = cap // CHAINS
     odd = strip % 2 == 1
-    image_ref = next_ref.at[1]
     one, two = first_ref[...], second_ref[...]
     below = jnp.where(strip > 0, jnp.where(odd, one, two), 0.0)
     above = jnp.where(strip < n_strip - 1, jnp.where(odd, two, one), 0.0)
@@ -275,43 +298,36 @@
     ahead = ahead + times_f32(spread(value_ref[pl.ds(count - 1, 1), :]), edge_map_ref[...])
     ahead = jnp.where(track < n_track - 1, ahead, 0.0)
     at_end = lax.broadcasted_iota(jnp.int32, (cap, width), 0) == count - 1
-    image_ref[...] = base_ref[...] + above + jnp.where(at_end, ahead, 0.0)
+    known = base_ref[...] + above + jnp.where(at_end, ahead, 0.0)
+    alpha = alpha_ref[...]
     for j in range(cap):
-        row = jnp.broadcast_to(below[j : j + 1, :], (ROWS, width))
-        crossed = times(split_row(row), coupling_ref[j], NT)
-        image_ref[j : j + 1, :] = image_ref[j : j + 1, :] + crossed[:1]
-    mask = live_mask(pos_ref, (cap, width))
-    image = jnp.where(mask, image_ref[...], 0.0)
-    if first:
-        next_ref[0] = jnp.where(mask, state_ref[...], 0.0)
-        next_ref[2] = value_ref[...]
-        next_ref[3] = jnp.zeros_like(image)
-        next_ref[1] = image
-    else:
-        alpha = alpha_of(recv_ref, width // 128)
-        next_ref[0] = state_ref[0] - alpha * state_ref[1]
-        next_ref[3] = state_ref[3] + alpha * state_ref[2]
-        next_ref[2] = state_ref[2] - alpha * value_ref[...]
-        next_ref[1] = state_ref[1] - alpha * image
-    dots = dot_parts(next_ref[0], next_ref[1])
+        crossed = times(split_row(wide_row(below, j)), coupling_flip_ref[j], NN)
+        next_ref[j : j + 1, :] = known[j : j + 1, :] + crossed[:1]
+    image = jnp.where(live_mask(pos_ref, (cap, width)), next_ref[...], 0.0)
+    next_ref[...] = image if first else image_ref[...] - alpha * image
+    state = [None] * CHAINS
+    steps = range(0 if local_ref is None else length)
+    for t in steps:
+        inner = []
+        for q in range(CHAINS):
+            j = q * length + t
+            inner.append(wide_row(next_ref, j))
+            if t > 0:
+                lowered = times(split_row(state[q]), lower_flip_ref[j], NN)
+                inner[q] = inner[q] - link(links_ref, pos_ref, j) * lowered
+        for q in range(CHAINS):
+            j = q * length + t
+            value = times(split_row(inner[q]), precond_flip_ref[j], NN)
+            state[q] = jnp.where(is_live(pos_ref, j), value, state[q] if t > 0 else 0.0)
+            local_ref[j : j + 1, :] = state[q][:1]
+            if j == 0:
+                edge = link(links_ref, pos_ref, 0) * times(split_row(state[q]), lower_ref[0], NN)
+    dots = dot_parts(state_ref[0], next_ref[...])
     if local_ref is None:
         packed = jnp.concatenate([jnp.zeros((width // 128, 128), F32)] + dots, axis=0)
         for i in range(send_ref.shape[0]):
             send_ref[i] = packed
         return
-    state = [None] * CHAINS
-    for t in range(length):
-        for q in range(CHAINS):
-            j = q * length + t
-            inner = wide_row(image_ref, j)
-            if t > 0:
-                lowered = times(split_row(state[q]), lower_ref[j], NT)
-                inner = inner - link(links_ref, pos_ref, j) * lowered
-            value = times(split_row(inner), precond_ref[j], NT)
-            state[q] = jnp.where(is_live(pos_ref, j), value, state[q] if t > 0 else 0.0)
-            local_ref[j : j + 1, :] = state[q][:1]
-            if j == 0:
-                edge = link(links_ref, pos_ref, 0) * times(split_row(state[q]), lower_ref[0], NN)
     ends = chain_ends(state, maps_ref, length)
     begins_ref[...] = jnp.concatenate(ends, axis=0)
     send_ends(ends[-1], edge[:1], dots, other_ref, pos_ref, n_track, send_ref)
@@ -321,10 +337,10 @@
     update_kernel(cap, n_track, n_strip, False, *refs[:-1], None, None, refs[-1])
 
 
-def final_kernel(recv_ref, state_ref, solution_ref, residual_ref):
+def final_kernel(recv_ref, state_ref, image_ref, solution_ref, residual_ref):
     alpha = alpha_of(recv_ref, state_ref.shape[2] // 128)
-    solution_ref[...] = state_ref[3] + alpha * state_ref[2]
-    residual_ref[...] = state_ref[0] - alpha * state_ref[1]
+    solution_ref[...] = state_ref[2] + alpha * state_ref[1]
+    residual_ref[...] = state_ref[0] - alpha * image_ref[...]
 
 
 def call(kernel, outs, specs, *args, scratch=(), vmem=VMEM_BYTES):
@@ -361,6 +377,10 @@
     chain = (CHAINS, width)
     swap = [(i, i ^ 1) for i in range(n_track)]
 
+    def flip(*stacks):
+        kernel = functools.partial(flip_kernel, cap)
+        return call(kernel, [(stack, jnp.bfloat16)] * len(stacks), [VMEM] * len(stacks), *stacks)
+
     maps, total, edge_map, local, ends, begins, through, lower, precond, diag, coupling = call(
         functools.partial(maps_kernel, cap),
         [stack, square, square, block, (2, width), chain, (CHAINS - 1,) + square] + [(stack, jnp.bfloat16)] * 4,
@@ -372,24 +392,35 @@
         ],
     )
     other = lax.ppermute(total, "track", swap)
+    lower_flip, precond_flip = flip(lower, precond)
     chip, send = call(
         functools.partial(pair_kernel, n_track),
         [(width // 2, width), chunk],
-        [VMEM] * 3 + [SMEM] + [VMEM] * 5,
-        total, other, ends, pos, maps, lower, precond, diag, coupling,
+        [VMEM] * 3 + [SMEM] + [VMEM] * 6,
+        total, other, ends, pos, maps, lower, lower_flip, precond_flip, diag, coupling,
     )
     nearer = [
-        lax.ppermute(chip, "track", [(i, i + 2 * k) for i in range(2, n_track - 2 * k)])
+        lax.ppermute(
+            chip, "track", swap[:2] + [(i, 2 + (i - 2 + 2 * k) % (n_track - 2)) for i in range(2, n_track)]
+        )
         for k in range(1, chips - 1)
     ]
-    state = rhs
+    state = image = rhs
     pairs = [(i, i ^ 1) for i in range(n_strip) if i ^ 1 < n_strip]
-    cross = [(i, (i + 1 if i % 2 else i - 1) % n_strip) for i in range(n_strip)]
+    cross = []
+    for d in range(n_track):
+        for i in range(n_strip):
+            partner = i + 1 if i % 2 else i - 1
+            if 0 <= partner < n_strip:
+                cross.append((d * n_strip + i, d * n_strip + partner))
+            else:
+                cross.append((d * n_strip + i, (d ^ 1) * n_strip + i))
     for step_number in range(ITERS):
         recv = lax.all_to_all(send, ("strip", "track"), 0, 0)
         if step_number == 0:
-            recv, *nearer = lax.optimization_barrier((recv, *nearer))
+            recv, diag, coupling, *nearer = lax.optimization_barrier((recv, diag, coupling, *nearer))
             nearer += [lax.ppermute(part, "track", swap) for part in nearer]
+            diag_flip, coupling_flip = flip(diag, coupling)
         value, first, second, entry = call(
             functools.partial(direction_kernel, cap, n_track),
             [block, block, block, (1, width)],
@@ -400,23 +431,26 @@
             edge_map, entry = lax.optimization_barrier((edge_map, entry))
             edge_map = lax.ppermute(edge_map, "track", [((i + 1) % n_track, i) for i in range(n_track)])
         first = lax.ppermute(first, "strip", pairs)
-        second = lax.ppermute(second, "strip", cross)
-        base, = call(
-            functools.partial(local_kernel, cap),
-            [block],
-            [VMEM] * 4 + [SMEM] * 2,
-            value, entry, diag, lower, links, pos,
+        second = lax.ppermute(second, ("track", "strip"), cross)
+        base, state, alpha = call(
+            functools.partial(local_kernel, cap, step_number == 0),
+            [block, (3,) + block, (1, width)],
+            [VMEM] * 8 + [SMEM] * 2,
+            value, entry, recv, state, image, diag_flip, lower, lower_flip, links, pos,
         )
-        args = (base, first, second, recv, value, state, edge_map, coupling, lower, precond, maps, other, links, pos)
-        specs = [VMEM] * 12 + [SMEM] * 2
+        args = (
+            base, first, second, value, recv, state, image, alpha, edge_map, coupling_flip, lower, lower_flip,
+            precond_flip, maps, other, links, pos,
+        )
+        specs = [VMEM] * 15 + [SMEM] * 2
         if step_number < ITERS - 1:
             kernel = functools.partial(update_kernel, cap, n_track, n_strip, step_number == 0)
-            state, local, begins, send = call(kernel, [(4,) + block, block, chain, chunk], specs, *args)
+            image, local, begins, send = call(kernel, [block, block, chain, chunk], specs, *args)
         else:
             kernel = functools.partial(last_update_kernel, cap, n_track, n_strip)
-            state, send = call(kernel, [(4,) + block, chunk], specs, *args)
+            image, send = call(kernel, [block, chunk], specs, *args)
     recv = lax.all_to_all(send, ("strip", "track"), 0, 0)
-    solution, residual = call(final_kernel, [block, block], [VMEM] * 2, recv, state)
+    solution, residual = call(final_kernel, [block, block], [VMEM] * 3, recv, state, image)
     return (solution[None], residual[None])
 
 

time: 152 us -> 138 us (0.908)
  starting transfers between devices: 16 us -> 6.26 us
  waiting for transfers between devices: 13.3 us -> 8.65 us
  blocking collectives: 72.4 us -> 75.6 us
  Pallas kernels: 48.4 us -> 45.5 us
    ppermute x8, waiting for transfers between devices: 11 us -> 0.02 us  [the longest x6 0.02 us: body(): second = lax.ppermute(second, ('track', 'strip'), cross)]
    ppermute x8, starting transfers between devices: 10.4 us -> 0.58 us  [the longest x2 0.56 us: body(): lax.ppermute(chip, 'track', swap[:2] + [(i, 2 + (i - 2 + 2 * k) % (n_trac...]
    ppermute x6, waiting for transfers between devices: 0.07 us -> 7.43 us  [body(): first = lax.ppermute(first, 'strip', pairs)]
    all_to_all x7, blocking collectives: 72.4 us -> 75.6 us  [body(): recv = lax.all_to_all(send, ('strip', 'track'), 0, 0)]
    pallas_call x21 -> x23, Pallas kernels: 48.4 us -> 45.5 us  [call(): pl.pallas_call(kernel, out_shape=[pltpu.VMEM(shape, dtype) if math.prod(s...]
where the time goes in v4:
time: 138 us; the launch traced here: 137 us
  blocking collectives  75.6 us (55%)
  Pallas kernels  45.5 us (33%)
  waiting for transfers between devices  8.65 us (6%)
  starting transfers between devices  6.26 us (5%)
  between operations  1.4 us (1%)
    all_to_all x7, blocking collectives, body(): recv = lax.all_to_all(send, ('strip', 'track'), 0, 0)  75.6 us
    pallas_call x23, Pallas kernels, call(): pl.pallas_call(kernel, out_shape=[pltpu.VMEM(shape, dtype) if math.prod(s...  45.5 us
    ppermute x6, waiting for transfers between devices, body(): first = lax.ppermute(first, 'strip', pairs)  7.43 us
    ppermute x6, starting transfers between devices, body(): first = lax.ppermute(first, 'strip', pairs)  3.97 us
  transfers between devices with their start and end apart: 18, of which 9 were waited for; matrix products, arithmetic and copies ran while one was open for 0% of the time, Pallas kernels for 9%

profile of v4, /device:TPU:0, one launch (start us, length us, event | category | flops | bytes accessed | tf_op | source)
XLA Modules:
  0.0 137.4 jit_solution(11314112677438560601)
XLA Ops:
  1.3 0.1 pad_add_fusion.pos_ref.refs_4_.refs_16_
  1.4 8.1 %shard_map.86 = (f32[16,256,256]{2,1,0:T(8,128)S(1)}, f32[256,256]{1,0:T(8,128)S(1)}, f32[256,256]{1,0:T(8,128)S(1)}, f32[16,256]{1,0:T(8,128)S(1)}, f32[2,256]{...) custom-call(f32[16,256]{1,0:T(8,128)} %bitcast.9, ...), custom_call_target="tpu_custom_call" | custom-call | tf_op jit(solution)/shard_map/pallas_call | solution.py:352
  9.5 0.5 collective-permute-start
  10.0 1.1 shard_map.87
  11.1 0.0 collective-permute-done.other_ref.refs_14_
  11.1 0.8 shard_map.88
  12.0 0.4 collective-permute-start.1
  12.4 0.1 collective-permute-start.2
  12.5 15.9 %all_to_all.35.recv_ref = f32[32,4,128]{2,1,0:T(4,128)S(1)} all-to-all(f32[32,4,128]{2,1,0:T(4,128)S(1)} %get-tuple-element.101), channel_id=1, replica_groups=mesh['track'=8,'strip'=4] {'strip','track'}, dimensions={0} | all-to-all | bytes 131072 | tf_op jit(solution)/shard_map/all_to_all | solution.py:419
  28.5 0.0 collective-permute-done.1.refs_0_
  28.5 0.0 collective-permute-done.2.refs_1_
  28.5 0.1 collective-permute-start.3
  28.6 0.4 collective-permute-start.4
  29.0 0.8 collective-permute-done.3.refs_2_
  29.8 0.2 collective-permute-done.4.refs_3_
  30.0 1.7 %shard_map.89 = (f32[16,256]{1,0:T(8,128)S(1)}, f32[16,256]{1,0:T(8,128)S(1)}, f32[16,256]{1,0:T(8,128)S(1)}, f32[1,256]{1,0:T(1,128)S(1)}) custom-call(f32[32,4,128]{2,1,0:T(4,128)S(1)} %all_to_all.35.recv_ref, f32[16,256]{1,0:T(8,128)S(1)} %get-tuple-element.104.local_ref, f32[4,256]{1,0:T(4,128)S(1)} %get-tuple-element.105.begins_ref, ...), custom_call_target="tpu_custom_call" | custom-call | tf_op jit(solution)/shard_map/pallas_call | solution.py:352
  31.7 0.7 collective-permute-start.7
  32.4 0.6 collective-permute-start.5
  33.0 0.0 collective-permute-start.6
  33.0 1.1 shard_map.90
  34.2 1.7 %shard_map.91 = (f32[16,256]{1,0:T(8,128)S(1)}, f32[3,16,256]{2,1,0:T(8,128)S(1)}, f32[1,256]{1,0:T(1,128)S(1)}) custom-call(f32[16,256]{1,0:T(8,128)S(1)} %get-tuple-element.110.value_ref, f32[1,256]{1,0:T(1,128)S(1)} %get-tuple-element.113.entry_ref, f32[32,4,128]{2,1,0:T(4,128)S(1)} %all_to_all.35.recv_ref, f32[16,256]{1,0:T(8,128)S(1)} %bitcast.10, ...), custom_call_target="tpu_custom_call" | custom-call | tf_op jit(solution)/shard_map/pallas_call | solution.py:352
  35.9 0.3 collective-permute-done.5.first_ref
  36.1 0.1 collective-permute-done.7.edge_map_ref.refs_8_
  36.3 2.4 %shard_map.92 = (f32[16,256]{1,0:T(8,128)S(1)}, f32[16,256]{1,0:T(8,128)S(1)}, f32[4,256]{1,0:T(4,128)S(1)}, f32[32,4,128]{2,1,0:T(4,128)S(1)}) custom-call(f32[16,256]{1,0:T(8,128)S(1)} %get-tuple-element.116.base_ref, f32[16,256]{1,0:T(8,128)S(1)} %collective-permute-done.5.first_ref, f32[16,256]{1,0:T(8,128)S(1)} %collective-permute-done.6.second_ref, ...), custom_call_target="tpu_custom_call" | custom-call | tf_op jit(solution)/shard_map/pallas_call | solution.py:352
  38.7 10.8 %all_to_all.36.recv_ref = f32[32,4,128]{2,1,0:T(4,128)S(1)} all-to-all(f32[32,4,128]{2,1,0:T(4,128)S(1)} %get-tuple-element.123), channel_id=1, replica_groups=mesh['track'=8,'strip'=4] {'strip','track'}, dimensions={0} | all-to-all | bytes 131072 | tf_op jit(solution)/shard_map/all_to_all | solution.py:419
  49.6 1.7 %shard_map.93 = (f32[16,256]{1,0:T(8,128)S(1)}, f32[16,256]{1,0:T(8,128)S(1)}, f32[16,256]{1,0:T(8,128)S(1)}, f32[1,256]{1,0:T(1,128)S(1)}) custom-call(f32[32,4,128]{2,1,0:T(4,128)S(1)} %all_to_all.36.recv_ref, f32[16,256]{1,0:T(8,128)S(1)} %get-tuple-element.124.local_ref, f32[4,256]{1,0:T(4,128)S(1)} %get-tuple-element.125.begins_ref, ...), custom_call_target="tpu_custom_call" | custom-call | tf_op jit(solution)/shard_map/pallas_call | solution.py:352
  51.3 0.7 collective-permute-start.8
  52.0 1.7 %shard_map.94 = (f32[16,256]{1,0:T(8,128)S(1)}, f32[3,16,256]{2,1,0:T(8,128)S(1)}, f32[1,256]{1,0:T(1,128)S(1)}) custom-call(f32[16,256]{1,0:T(8,128)S(1)} %get-tuple-element.126.value_ref, f32[1,256]{1,0:T(1,128)S(1)} %get-tuple-element.127.entry_ref, f32[32,4,128]{2,1,0:T(4,128)S(1)} %all_to_all.36.recv_ref, ...), custom_call_target="tpu_custom_call" | custom-call | tf_op jit(solution)/shard_map/pallas_call | solution.py:352
  53.6 1.4 %collective-permute-done.8.first_ref = f32[16,256]{1,0:T(8,128)S(1)} collective-permute-done((f32[16,256]{1,0:T(8,128)S(1)}, f32[16,256]{1,0:T(8,128)S(1)}, u32[]{:S(2)}, u32[]{:S(2)}) %collective-permute-start.8) | collective-permute-done | bytes 16416 | tf_op jit(solution)/shard_map/ppermute | solution.py:433
  55.1 0.0 collective-permute-done.9.second_ref
  55.1 2.4 %shard_map.95 = (f32[16,256]{1,0:T(8,128)S(1)}, f32[16,256]{1,0:T(8,128)S(1)}, f32[4,256]{1,0:T(4,128)S(1)}, f32[32,4,128]{2,1,0:T(4,128)S(1)}) custom-call(f32[16,256]{1,0:T(8,128)S(1)} %get-tuple-element.129.base_ref, f32[16,256]{1,0:T(8,128)S(1)} %collective-permute-done.8.first_ref, f32[16,256]{1,0:T(8,128)S(1)} %collective-permute-done.9.second_ref, ...), custom_call_target="tpu_custom_call" | custom-call | tf_op jit(solution)/shard_map/pallas_call | solution.py:352
  57.5 9.8 %all_to_all.37.recv_ref = f32[32,4,128]{2,1,0:T(4,128)S(1)} all-to-all(f32[32,4,128]{2,1,0:T(4,128)S(1)} %get-tuple-element.134), channel_id=1, replica_groups=mesh['track'=8,'strip'=4] {'strip','track'}, dimensions={0} | all-to-all | bytes 131072 | tf_op jit(solution)/shard_map/all_to_all | solution.py:419
  67.3 1.7 %shard_map.96 = (f32[16,256]{1,0:T(8,128)S(1)}, f32[16,256]{1,0:T(8,128)S(1)}, f32[16,256]{1,0:T(8,128)S(1)}, f32[1,256]{1,0:T(1,128)S(1)}) custom-call(f32[32,4,128]{2,1,0:T(4,128)S(1)} %all_to_all.37.recv_ref, f32[16,256]{1,0:T(8,128)S(1)} %get-tuple-element.135.local_ref, f32[4,256]{1,0:T(4,128)S(1)} %get-tuple-element.136.begins_ref, ...), custom_call_target="tpu_custom_call" | custom-call | tf_op jit(solution)/shard_map/pallas_call | solution.py:352
  69.0 0.7 collective-permute-start.10
  69.6 0.0 collective-permute-start.11
  69.6 1.7 %shard_map.97 = (f32[16,256]{1,0:T(8,128)S(1)}, f32[3,16,256]{2,1,0:T(8,128)S(1)}, f32[1,256]{1,0:T(1,128)S(1)}) custom-call(f32[16,256]{1,0:T(8,128)S(1)} %get-tuple-element.137.value_ref, f32[1,256]{1,0:T(1,128)S(1)} %get-tuple-element.138.entry_ref, f32[32,4,128]{2,1,0:T(4,128)S(1)} %all_to_all.37.recv_ref, ...), custom_call_target="tpu_custom_call" | custom-call | tf_op jit(solution)/shard_map/pallas_call | solution.py:352
  71.3 1.4 %collective-permute-done.10.first_ref = f32[16,256]{1,0:T(8,128)S(1)} collective-permute-done((f32[16,256]{1,0:T(8,128)S(1)}, f32[16,256]{1,0:T(8,128)S(1)}, u32[]{:S(2)}, u32[]{:S(2)}) %collective-permute-start.10) | collective-permute-done | bytes 16416 | tf_op jit(solution)/shard_map/ppermute | solution.py:433
  72.8 0.0 collective-permute-done.11.second_ref
  72.8 2.4 %shard_map.98 = (f32[16,256]{1,0:T(8,128)S(1)}, f32[16,256]{1,0:T(8,128)S(1)}, f32[4,256]{1,0:T(4,128)S(1)}, f32[32,4,128]{2,1,0:T(4,128)S(1)}) custom-call(f32[16,256]{1,0:T(8,128)S(1)} %get-tuple-element.140.base_ref, f32[16,256]{1,0:T(8,128)S(1)} %collective-permute-done.10.first_ref, f32[16,256]{1,0:T(8,128)S(1)} %collective-permute-done.11.second_ref, ...), custom_call_target="tpu_custom_call" | custom-call | tf_op jit(solution)/shard_map/pallas_call | solution.py:352
  75.2 9.8 %all_to_all.38.recv_ref = f32[32,4,128]{2,1,0:T(4,128)S(1)} all-to-all(f32[32,4,128]{2,1,0:T(4,128)S(1)} %get-tuple-element.145), channel_id=1, replica_groups=mesh['track'=8,'strip'=4] {'strip','track'}, dimensions={0} | all-to-all | bytes 131072 | tf_op jit(solution)/shard_map/all_to_all | solution.py:419
  85.0 1.7 %shard_map.99 = (f32[16,256]{1,0:T(8,128)S(1)}, f32[16,256]{1,0:T(8,128)S(1)}, f32[16,256]{1,0:T(8,128)S(1)}, f32[1,256]{1,0:T(1,128)S(1)}) custom-call(f32[32,4,128]{2,1,0:T(4,128)S(1)} %all_to_all.38.recv_ref, f32[16,256]{1,0:T(8,128)S(1)} %get-tuple-element.146.local_ref, f32[4,256]{1,0:T(4,128)S(1)} %get-tuple-element.147.begins_ref, ...), custom_call_target="tpu_custom_call" | custom-call | tf_op jit(solution)/shard_map/pallas_call | solution.py:352
  86.7 0.7 collective-permute-start.12
  87.3 0.0 collective-permute-start.13
  87.3 1.7 %shard_map.100 = (f32[16,256]{1,0:T(8,128)S(1)}, f32[3,16,256]{2,1,0:T(8,128)S(1)}, f32[1,256]{1,0:T(1,128)S(1)}) custom-call(f32[16,256]{1,0:T(8,128)S(1)} %get-tuple-element.148.value_ref, f32[1,256]{1,0:T(1,128)S(1)} %get-tuple-element.149.entry_ref, f32[32,4,128]{2,1,0:T(4,128)S(1)} %all_to_all.38.recv_ref, ...), custom_call_target="tpu_custom_call" | custom-call | tf_op jit(solution)/shard_map/pallas_call | solution.py:352
  89.0 1.4 %collective-permute-done.12.first_ref = f32[16,256]{1,0:T(8,128)S(1)} collective-permute-done((f32[16,256]{1,0:T(8,128)S(1)}, f32[16,256]{1,0:T(8,128)S(1)}, u32[]{:S(2)}, u32[]{:S(2)}) %collective-permute-start.12) | collective-permute-done | bytes 16416 | tf_op jit(solution)/shard_map/ppermute | solution.py:433
  90.5 0.0 collective-permute-done.13.second_ref
  90.5 2.4 %shard_map.101 = (f32[16,256]{1,0:T(8,128)S(1)}, f32[16,256]{1,0:T(8,128)S(1)}, f32[4,256]{1,0:T(4,128)S(1)}, f32[32,4,128]{2,1,0:T(4,128)S(1)}) custom-call(f32[16,256]{1,0:T(8,128)S(1)} %get-tuple-element.151.base_ref, f32[16,256]{1,0:T(8,128)S(1)} %collective-permute-done.12.first_ref, f32[16,256]{1,0:T(8,128)S(1)} %collective-permute-done.13.second_ref, ...), custom_call_target="tpu_custom_call" | custom-call | tf_op jit(solution)/shard_map/pallas_call | solution.py:352
  92.9 9.8 %all_to_all.39.recv_ref = f32[32,4,128]{2,1,0:T(4,128)S(1)} all-to-all(f32[32,4,128]{2,1,0:T(4,128)S(1)} %get-tuple-element.156), channel_id=1, replica_groups=mesh['track'=8,'strip'=4] {'strip','track'}, dimensions={0} | all-to-all | bytes 131072 | tf_op jit(solution)/shard_map/all_to_all | solution.py:419
  102.7 1.7 %shard_map.102 = (f32[16,256]{1,0:T(8,128)S(1)}, f32[16,256]{1,0:T(8,128)S(1)}, f32[16,256]{1,0:T(8,128)S(1)}, f32[1,256]{1,0:T(1,128)S(1)}) custom-call(f32[32,4,128]{2,1,0:T(4,128)S(1)} %all_to_all.39.recv_ref, f32[16,256]{1,0:T(8,128)S(1)} %get-tuple-element.157.local_ref, f32[4,256]{1,0:T(4,128)S(1)} %get-tuple-element.158.begins_ref, ...), custom_call_target="tpu_custom_call" | custom-call | tf_op jit(solution)/shard_map/pallas_call | solution.py:352
  104.4 0.7 collective-permute-start.14
  105.0 0.0 collective-permute-start.15
  105.0 1.7 %shard_map.103 = (f32[16,256]{1,0:T(8,128)S(1)}, f32[3,16,256]{2,1,0:T(8,128)S(1)}, f32[1,256]{1,0:T(1,128)S(1)}) custom-call(f32[16,256]{1,0:T(8,128)S(1)} %get-tuple-element.159.value_ref, f32[1,256]{1,0:T(1,128)S(1)} %get-tuple-element.160.entry_ref, f32[32,4,128]{2,1,0:T(4,128)S(1)} %all_to_all.39.recv_ref, ...), custom_call_target="tpu_custom_call" | custom-call | tf_op jit(solution)/shard_map/pallas_call | solution.py:352
  106.7 1.4 %collective-permute-done.14.first_ref = f32[16,256]{1,0:T(8,128)S(1)} collective-permute-done((f32[16,256]{1,0:T(8,128)S(1)}, f32[16,256]{1,0:T(8,128)S(1)}, u32[]{:S(2)}, u32[]{:S(2)}) %collective-permute-start.14) | collective-permute-done | bytes 16416 | tf_op jit(solution)/shard_map/ppermute | solution.py:433
  108.2 0.0 collective-permute-done.15.second_ref
  108.2 2.4 %shard_map.104 = (f32[16,256]{1,0:T(8,128)S(1)}, f32[16,256]{1,0:T(8,128)S(1)}, f32[4,256]{1,0:T(4,128)S(1)}, f32[32,4,128]{2,1,0:T(4,128)S(1)}) custom-call(f32[16,256]{1,0:T(8,128)S(1)} %get-tuple-element.162.base_ref, f32[16,256]{1,0:T(8,128)S(1)} %collective-permute-done.14.first_ref, f32[16,256]{1,0:T(8,128)S(1)} %collective-permute-done.15.second_ref, ...), custom_call_target="tpu_custom_call" | custom-call | tf_op jit(solution)/shard_map/pallas_call | solution.py:352
  110.6 9.8 %all_to_all.40.recv_ref.refs_4_ = f32[32,4,128]{2,1,0:T(4,128)S(1)} all-to-all(f32[32,4,128]{2,1,0:T(4,128)S(1)} %get-tuple-element.167), channel_id=1, replica_groups=mesh['track'=8,'strip'=4] {'strip','track'}, dimensions={0} | all-to-all | bytes 131072 | tf_op jit(solution)/shard_map/all_to_all | solution.py:419
  120.3 1.7 %shard_map.105 = (f32[16,256]{1,0:T(8,128)S(1)}, f32[16,256]{1,0:T(8,128)S(1)}, f32[16,256]{1,0:T(8,128)S(1)}, f32[1,256]{1,0:T(1,128)S(1)}) custom-call(f32[32,4,128]{2,1,0:T(4,128)S(1)} %all_to_all.40.recv_ref.refs_4_, f32[16,256]{1,0:T(8,128)S(1)} %get-tuple-element.168.local_ref, f32[4,256]{1,0:T(4,128)S(1)} %get-tuple-element.169.begins_ref, ...), custom_call_target="tpu_custom_call" | custom-call | tf_op jit(solution)/shard_map/pallas_call | solution.py:352
  122.0 0.7 collective-permute-start.16
  122.7 1.7 %shard_map.106 = (f32[16,256]{1,0:T(8,128)S(1)}, f32[3,16,256]{2,1,0:T(8,128)S(1)}, f32[1,256]{1,0:T(1,128)S(1)}) custom-call(f32[16,256]{1,0:T(8,128)S(1)} %get-tuple-element.170.value_ref.refs_3_, f32[1,256]{1,0:T(1,128)S(1)} %get-tuple-element.171.entry_ref, f32[32,4,128]{2,1,0:T(4,128)S(1)} %all_to_all.40.recv_ref.refs_4_, ...), custom_call_target="tpu_custom_call" | custom-call | tf_op jit(solution)/shard_map/pallas_call | solution.py:352
  124.4 1.4 %collective-permute-done.16.refs_1_ = f32[16,256]{1,0:T(8,128)S(1)} collective-permute-done((f32[16,256]{1,0:T(8,128)S(1)}, f32[16,256]{1,0:T(8,128)S(1)}, u32[]{:S(2)}, u32[]{:S(2)}) %collective-permute-start.16) | collective-permute-done | bytes 16416 | tf_op jit(solution)/shard_map/ppermute | solution.py:433
  125.8 0.0 collective-permute-done.17.refs_2_
  125.8 1.0 shard_map.107
  126.9 9.8 %all_to_all.41.recv_ref = f32[32,4,128]{2,1,0:T(4,128)S(1)} all-to-all(f32[32,4,128]{2,1,0:T(4,128)S(1)} %get-tuple-element.178), channel_id=1, replica_groups=mesh['track'=8,'strip'=4] {'strip','track'}, dimensions={0} | all-to-all | bytes 131072 | tf_op jit(solution)/shard_map/all_to_all | solution.py:452
  136.6 0.8 shard_map.108
  (7 shorter events, 0.0 us)
Async XLA Ops:
  9.5 1.7 %collective-permute-start = (f32[256,256]{1,0:T(8,128)S(1)}, f32[256,256]{1,0:T(8,128)S(1)}, u32[]{:S(2)}, u32[]{:S(2)}) collective-permute-start(f32[256,256]{1,0:T(8,128)S(1)} %get-tuple-element.92.total_ref), channel_id=1, source_target_pairs={{0,4},{4,0},{8,12},{12,8},{16,20},{20,16},{24,28},{28,24},{1,5},{5... | collective-permute-start | bytes 786440 | tf_op jit(solution)/shard_map/ppermute | solution.py:394
  12.0 16.5 %collective-permute-start.1 = (f32[128,256]{1,0:T(8,128)S(1)}, f32[128,256]{1,0:T(8,128)S(1)}, u32[]{:S(2)}, u32[]{:S(2)}) collective-permute-start(f32[128,256]{1,0:T(8,128)S(1)} %get-tuple-element.102), channel_id=1, source_target_pairs={{0,4},{4,0},{8,16},{12,20},{16,24},{20,28},{24,8},{28,12},{1,5},{5... | collective-permute-start | bytes 393224 | tf_op jit(solution)/shard_map/ppermute | solution.py:403
  12.4 16.1 %collective-permute-start.2 = (f32[128,256]{1,0:T(8,128)S(1)}, f32[128,256]{1,0:T(8,128)S(1)}, u32[]{:S(2)}, u32[]{:S(2)}) collective-permute-start(f32[128,256]{1,0:T(8,128)S(1)} %get-tuple-element.102), channel_id=1, source_target_pairs={{0,4},{4,0},{8,24},{12,28},{16,8},{20,12},{24,16},{28,20},{1,5},{5... | collective-permute-start | bytes 393224 | tf_op jit(solution)/shard_map/ppermute | solution.py:403
  28.5 1.4 collective-permute-start.3
  28.6 1.4 %collective-permute-start.4 = (f32[128,256]{1,0:T(8,128)S(1)}, f32[128,256]{1,0:T(8,128)S(1)}, u32[]{:S(2)}, u32[]{:S(2)}) collective-permute-start(f32[128,256]{1,0:T(8,128)S(1)} %collective-permute-done.2.refs_1_), channel_id=1, source_target_pairs={{0,4},{4,0},{8,12},{12,8},{16,20},{20,16},{24,28},{28,24},{1,5},{5... | collective-permute-start | bytes 393224 | tf_op jit(solution)/shard_map/ppermute | solution.py:422
  31.7 4.6 %collective-permute-start.7 = (f32[256,256]{1,0:T(8,128)S(1)}, f32[256,256]{1,0:T(8,128)S(1)}, u32[]{:S(2)}, u32[]{:S(2)}) collective-permute-start(f32[256,256]{1,0:T(8,128)S(1)} %get-tuple-element.121), channel_id=1, source_target_pairs={{4,0},{8,4},{12,8},{16,12},{20,16},{24,20},{28,24},{0,28},{5,1},{9... | collective-permute-start | bytes 786440 | tf_op jit(solution)/shard_map/ppermute | solution.py:432
  32.4 3.7 %collective-permute-start.5 = (f32[16,256]{1,0:T(8,128)S(1)}, f32[16,256]{1,0:T(8,128)S(1)}, u32[]{:S(2)}, u32[]{:S(2)}) collective-permute-start(f32[16,256]{1,0:T(8,128)S(1)} %get-tuple-element.117), channel_id=1, source_target_pairs={{0,1},{1,0},{2,3},{3,2},{4,5},{5,4},{6,7},{7,6},{8,9},{9,8},{10,11... | collective-permute-start | bytes 49160 | tf_op jit(solution)/shard_map/ppermute | solution.py:433
  33.0 1.1 copy-start
  33.0 1.2 copy-start.1
  33.0 3.1 %collective-permute-start.6 = (f32[16,256]{1,0:T(8,128)S(1)}, f32[16,256]{1,0:T(8,128)S(1)}, u32[]{:S(2)}, u32[]{:S(2)}) collective-permute-start(f32[16,256]{1,0:T(8,128)S(1)} %get-tuple-element.118), channel_id=1, source_target_pairs={{0,4},{1,2},{2,1},{3,7},{4,0},{5,6},{6,5},{7,3},{8,12},{9,10},{10,... | collective-permute-start | bytes 49160 | tf_op jit(solution)/shard_map/ppermute | solution.py:434
  51.3 3.8 %collective-permute-start.8 = (f32[16,256]{1,0:T(8,128)S(1)}, f32[16,256]{1,0:T(8,128)S(1)}, u32[]{:S(2)}, u32[]{:S(2)}) collective-permute-start(f32[16,256]{1,0:T(8,128)S(1)} %get-tuple-element.130), channel_id=1, source_target_pairs={{0,1},{1,0},{2,3},{3,2},{4,5},{5,4},{6,7},{7,6},{8,9},{9,8},{10,11... | collective-permute-start | bytes 49160 | tf_op jit(solution)/shard_map/ppermute | solution.py:433
  51.9 3.1 %collective-permute-start.9 = (f32[16,256]{1,0:T(8,128)S(1)}, f32[16,256]{1,0:T(8,128)S(1)}, u32[]{:S(2)}, u32[]{:S(2)}) collective-permute-start(f32[16,256]{1,0:T(8,128)S(1)} %get-tuple-element.131), channel_id=1, source_target_pairs={{0,4},{1,2},{2,1},{3,7},{4,0},{5,6},{6,5},{7,3},{8,12},{9,10},{10,... | collective-permute-start | bytes 49160 | tf_op jit(solution)/shard_map/ppermute | solution.py:434
  69.0 3.8 %collective-permute-start.10 = (f32[16,256]{1,0:T(8,128)S(1)}, f32[16,256]{1,0:T(8,128)S(1)}, u32[]{:S(2)}, u32[]{:S(2)}) collective-permute-start(f32[16,256]{1,0:T(8,128)S(1)} %get-tuple-element.141), channel_id=1, source_target_pairs={{0,1},{1,0},{2,3},{3,2},{4,5},{5,4},{6,7},{7,6},{8,9},{9,8},{10,11... | collective-permute-start | bytes 49160 | tf_op jit(solution)/shard_map/ppermute | solution.py:433
  69.6 3.1 %collective-permute-start.11 = (f32[16,256]{1,0:T(8,128)S(1)}, f32[16,256]{1,0:T(8,128)S(1)}, u32[]{:S(2)}, u32[]{:S(2)}) collective-permute-start(f32[16,256]{1,0:T(8,128)S(1)} %get-tuple-element.142), channel_id=1, source_target_pairs={{0,4},{1,2},{2,1},{3,7},{4,0},{5,6},{6,5},{7,3},{8,12},{9,10},{10,... | collective-permute-start | bytes 49160 | tf_op jit(solution)/shard_map/ppermute | solution.py:434
  86.7 3.8 %collective-permute-start.12 = (f32[16,256]{1,0:T(8,128)S(1)}, f32[16,256]{1,0:T(8,128)S(1)}, u32[]{:S(2)}, u32[]{:S(2)}) collective-permute-start(f32[16,256]{1,0:T(8,128)S(1)} %get-tuple-element.152), channel_id=1, source_target_pairs={{0,1},{1,0},{2,3},{3,2},{4,5},{5,4},{6,7},{7,6},{8,9},{9,8},{10,11... | collective-permute-start | bytes 49160 | tf_op jit(solution)/shard_map/ppermute | solution.py:433
  87.3 3.1 %collective-permute-start.13 = (f32[16,256]{1,0:T(8,128)S(1)}, f32[16,256]{1,0:T(8,128)S(1)}, u32[]{:S(2)}, u32[]{:S(2)}) collective-permute-start(f32[16,256]{1,0:T(8,128)S(1)} %get-tuple-element.153), channel_id=1, source_target_pairs={{0,4},{1,2},{2,1},{3,7},{4,0},{5,6},{6,5},{7,3},{8,12},{9,10},{10,... | collective-permute-start | bytes 49160 | tf_op jit(solution)/shard_map/ppermute | solution.py:434
  104.4 3.8 %collective-permute-start.14 = (f32[16,256]{1,0:T(8,128)S(1)}, f32[16,256]{1,0:T(8,128)S(1)}, u32[]{:S(2)}, u32[]{:S(2)}) collective-permute-start(f32[16,256]{1,0:T(8,128)S(1)} %get-tuple-element.163), channel_id=1, source_target_pairs={{0,1},{1,0},{2,3},{3,2},{4,5},{5,4},{6,7},{7,6},{8,9},{9,8},{10,11... | collective-permute-start | bytes 49160 | tf_op jit(solution)/shard_map/ppermute | solution.py:433
  105.0 3.1 %collective-permute-start.15 = (f32[16,256]{1,0:T(8,128)S(1)}, f32[16,256]{1,0:T(8,128)S(1)}, u32[]{:S(2)}, u32[]{:S(2)}) collective-permute-start(f32[16,256]{1,0:T(8,128)S(1)} %get-tuple-element.164), channel_id=1, source_target_pairs={{0,4},{1,2},{2,1},{3,7},{4,0},{5,6},{6,5},{7,3},{8,12},{9,10},{10,... | collective-permute-start | bytes 49160 | tf_op jit(solution)/shard_map/ppermute | solution.py:434
  122.0 3.8 %collective-permute-start.16 = (f32[16,256]{1,0:T(8,128)S(1)}, f32[16,256]{1,0:T(8,128)S(1)}, u32[]{:S(2)}, u32[]{:S(2)}) collective-permute-start(f32[16,256]{1,0:T(8,128)S(1)} %get-tuple-element.174), channel_id=1, source_target_pairs={{0,1},{1,0},{2,3},{3,2},{4,5},{5,4},{6,7},{7,6},{8,9},{9,8},{10,11... | collective-permute-start | bytes 49160 | tf_op jit(solution)/shard_map/ppermute | solution.py:433
  122.7 3.1 %collective-permute-start.17 = (f32[16,256]{1,0:T(8,128)S(1)}, f32[16,256]{1,0:T(8,128)S(1)}, u32[]{:S(2)}, u32[]{:S(2)}) collective-permute-start(f32[16,256]{1,0:T(8,128)S(1)} %get-tuple-element.175), channel_id=1, source_target_pairs={{0,4},{1,2},{2,1},{3,7},{4,0},{5,6},{6,5},{7,3},{8,12},{9,10},{10,... | collective-permute-start | bytes 49160 | tf_op jit(solution)/shard_map/ppermute | solution.py:434

commit v5 on v4

--- a/solution.py
+++ b/solution.py
@@ -94,16 +94,18 @@
         out_ref[i] = jnp.where(ahead > 1, far, jnp.where(ahead == 1, near, back))
 
 
-def chain_ends(state, maps_ref, length):
+def chain_ends(state, maps_ref, last_two_ref, length):
     ends = [state[0][:1]]
-    for q in range(1, CHAINS):
+    for q in range(1, CHAINS - 1):
         ends.append(state[q][:1] + times_f32(spread(ends[-1]), maps_ref[q * length + length - 1]))
+    last = state[-1][:1] + times_f32(spread(state[-2][:1]), maps_ref[CHAINS * length - 1])
+    ends.append(last + times_f32(spread(ends[-2]), last_two_ref[...]))
     return ends
 
 
 def maps_kernel(
     cap, rhs_hbm, links_hbm, lower_hbm, precond_hbm, diag_hbm, coupling_hbm, pos_ref,
-    maps_ref, total_ref, edge_ref, local_ref, ends_ref, begins_ref, through_ref,
+    maps_ref, total_ref, edge_ref, local_ref, ends_ref, begins_ref, through_ref, last_two_ref,
     lower_ref, precond_ref, diag_ref, coupling_ref,
     rhs_ref, links_ref, sems,
 ):
@@ -168,11 +170,13 @@
             state[q] if q < span else jnp.dot(state[q - span], state[q], precision=lax.Precision.HIGHEST)
             for q in range(CHAINS)
         ]
+        if span == 1:
+            last_two_ref[...] = state[-1]
         span *= 2
     for q in range(CHAINS - 1):
         through_ref[q] = state[q]
     total_ref[...] = state[-1]
-    ends = chain_ends(local, maps_ref, length)
+    ends = chain_ends(local, maps_ref, last_two_ref, length)
     ends_ref[0:1, :] = ends[-1]
     begins_ref[...] = jnp.concatenate(ends, axis=0)
     for copy in copies[-2:]:
@@ -183,9 +187,7 @@
     chip_ref, send_ref = refs[-2:]
     first_core = pos_ref[0] % 2 == 0
     own, other = total_ref[...], other_ref[...]
-    half = own.shape[0] // 2
-    early = jnp.where(first_core, own[:half], other[half:])
-    late = jnp.where(first_core, other, own)
+    early, late = jnp.where(first_core, own, other), jnp.where(first_core, other, own)
     chip_ref[...] = jnp.dot(early, late, precision=lax.Precision.HIGHEST)
     dots = [jnp.zeros((1, 128), F32)] * 2
     send_ends(ends_ref[0:1, :], ends_ref[1:2, :], dots, other_ref, pos_ref, n_track, send_ref)
@@ -210,10 +212,8 @@
         return chunk(2 * (chip - i), valid) + chunk(2 * (chip - i) + 1, valid)
 
     def chip_map(i):
-        mine, paired = chip_refs[i][...], chip_refs[i + len(chip_refs) // 2][...]
-        first_core = track % 2 == 0
-        top, bottom = jnp.where(first_core, mine, paired), jnp.where(first_core, paired, mine)
-        return jnp.concatenate([top, bottom], axis=0)
+        mine, paired = chip_refs[i // 2][...], chip_refs[i // 2 + len(chip_refs) // 2][...]
+        return jnp.where(track % 2 == i % 2, mine, paired)
 
     furthest = n_track // 2 - 1
     entry = chip_end(furthest)
@@ -243,10 +243,10 @@
             target[j] = jnp.transpose(source[j])
 
 
-def alpha_of(recv_ref, half):
+def alpha_of(recv_ref):
     total = jnp.sum(recv_ref[...], axis=0)
-    inner = jnp.sum(total[half : half + 1], axis=1, keepdims=True)
-    energy = jnp.sum(total[half + 1 : half + 2], axis=1, keepdims=True)
+    inner = jnp.sum(total[-2:-1], axis=1, keepdims=True)
+    energy = jnp.sum(total[-1:], axis=1, keepdims=True)
     return inner / (energy + 1e-6)
 
 
@@ -274,7 +274,7 @@
         next_ref[2] = jnp.zeros_like(value_ref[...])
         alpha_ref[...] = jnp.zeros((1, width), F32)
     else:
-        alpha = alpha_of(recv_ref, width // 128)
+        alpha = alpha_of(recv_ref)
         next_ref[0] = state_ref[0] - alpha * image_ref[...]
         next_ref[1] = state_ref[1] - alpha * value_ref[...]
         next_ref[2] = state_ref[2] + alpha * state_ref[1]
@@ -283,7 +283,7 @@
 
 def update_kernel(
     cap, n_track, n_strip, first, base_ref, first_ref, second_ref, value_ref, recv_ref, state_ref, image_ref, alpha_ref,
-    edge_map_ref, coupling_flip_ref, lower_ref, lower_flip_ref, precond_flip_ref, maps_ref, other_ref, links_ref, pos_ref,
+    edge_map_ref, coupling_flip_ref, lower_ref, lower_flip_ref, precond_flip_ref, maps_ref, last_two_ref, other_ref, links_ref, pos_ref,
     next_ref, local_ref, begins_ref, send_ref,
 ):
     track, strip, count = pos_ref[0], pos_ref[1], pos_ref[2]
@@ -299,36 +299,39 @@
     ahead = jnp.where(track < n_track - 1, ahead, 0.0)
     at_end = lax.broadcasted_iota(jnp.int32, (cap, width), 0) == count - 1
     known = base_ref[...] + above + jnp.where(at_end, ahead, 0.0)
-    alpha = alpha_ref[...]
-    for j in range(cap):
-        crossed = times(split_row(wide_row(below, j)), coupling_flip_ref[j], NN)
-        next_ref[j : j + 1, :] = known[j : j + 1, :] + crossed[:1]
-    image = jnp.where(live_mask(pos_ref, (cap, width)), next_ref[...], 0.0)
-    next_ref[...] = image if first else image_ref[...] - alpha * image
+    alpha = wide_row(alpha_ref, 0)
+
+    def image_row(j):
+        row = wide_row(known, j) + times(split_row(wide_row(below, j)), coupling_flip_ref[j], NN)
+        row = jnp.where(is_live(pos_ref, j), row, 0.0)
+        row = row if first else wide_row(image_ref, j) - alpha * row
+        next_ref[j : j + 1, :] = row[:1]
+        return row
+
     state = [None] * CHAINS
-    steps = range(0 if local_ref is None else length)
-    for t in steps:
-        inner = []
-        for q in range(CHAINS):
+    rows = [image_row(q * length) for q in range(CHAINS)]
+    for t in range(length):
+        if local_ref is not None and t > 0:
+            for q in range(CHAINS):
+                j = q * length + t
+                lowered = times(split_row(state[q]), lower_flip_ref[j], NN)
+                rows[q] = rows[q] - link(links_ref, pos_ref, j) * lowered
+        later = [image_row(q * length + t + 1) for q in range(CHAINS)] if t + 1 < length else []
+        for q in range(0 if local_ref is None else CHAINS):
             j = q * length + t
-            inner.append(wide_row(next_ref, j))
-            if t > 0:
-                lowered = times(split_row(state[q]), lower_flip_ref[j], NN)
-                inner[q] = inner[q] - link(links_ref, pos_ref, j) * lowered
-        for q in range(CHAINS):
-            j = q * length + t
-            value = times(split_row(inner[q]), precond_flip_ref[j], NN)
+            value = times(split_row(rows[q]), precond_flip_ref[j], NN)
             state[q] = jnp.where(is_live(pos_ref, j), value, state[q] if t > 0 else 0.0)
             local_ref[j : j + 1, :] = state[q][:1]
             if j == 0:
                 edge = link(links_ref, pos_ref, 0) * times(split_row(state[q]), lower_ref[0], NN)
+        rows = later
     dots = dot_parts(state_ref[0], next_ref[...])
     if local_ref is None:
-        packed = jnp.concatenate([jnp.zeros((width // 128, 128), F32)] + dots, axis=0)
+        packed = jnp.concatenate(dots, axis=0)
         for i in range(send_ref.shape[0]):
             send_ref[i] = packed
         return
-    ends = chain_ends(state, maps_ref, length)
+    ends = chain_ends(state, maps_ref, last_two_ref, length)
     begins_ref[...] = jnp.concatenate(ends, axis=0)
     send_ends(ends[-1], edge[:1], dots, other_ref, pos_ref, n_track, send_ref)
 
@@ -338,7 +341,7 @@
 
 
 def final_kernel(recv_ref, state_ref, image_ref, solution_ref, residual_ref):
-    alpha = alpha_of(recv_ref, state_ref.shape[2] // 128)
+    alpha = alpha_of(recv_ref)
     solution_ref[...] = state_ref[2] + alpha * state_ref[1]
     residual_ref[...] = state_ref[0] - alpha * image_ref[...]
 
@@ -381,9 +384,9 @@
         kernel = functools.partial(flip_kernel, cap)
         return call(kernel, [(stack, jnp.bfloat16)] * len(stacks), [VMEM] * len(stacks), *stacks)
 
-    maps, total, edge_map, local, ends, begins, through, lower, precond, diag, coupling = call(
+    maps, total, edge_map, local, ends, begins, through, last_two, lower, precond, diag, coupling = call(
         functools.partial(maps_kernel, cap),
-        [stack, square, square, block, (2, width), chain, (CHAINS - 1,) + square] + [(stack, jnp.bfloat16)] * 4,
+        [stack, square, square, block, (2, width), chain, (CHAINS - 1,) + square, square] + [(stack, jnp.bfloat16)] * 4,
         [HBM] * 6 + [SMEM],
         rhs, links, lower_blocks[0], precond_blocks[0], principal_tiles[0], coupling_blocks[0], pos,
         scratch=[
@@ -395,16 +398,17 @@
     lower_flip, precond_flip = flip(lower, precond)
     chip, send = call(
         functools.partial(pair_kernel, n_track),
-        [(width // 2, width), chunk],
+        [square, chunk],
         [VMEM] * 3 + [SMEM] + [VMEM] * 6,
         total, other, ends, pos, maps, lower, lower_flip, precond_flip, diag, coupling,
     )
-    nearer = [
-        lax.ppermute(
-            chip, "track", swap[:2] + [(i, 2 + (i - 2 + 2 * k) % (n_track - 2)) for i in range(2, n_track)]
-        )
-        for k in range(1, chips - 1)
-    ]
+    nearer = []
+    for k in range(1, chips - 1, 2):
+        shifted = swap[:2]
+        for i in range(2, n_track):
+            shifted = shifted + [(i, 2 + (i - 2 + 2 * (k + i % 2)) % (n_track - 2))]
+        nearer.append(lax.ppermute(chip, "track", shifted))
+
     state = image = rhs
     pairs = [(i, i ^ 1) for i in range(n_strip) if i ^ 1 < n_strip]
     cross = []
@@ -418,7 +422,10 @@
     for step_number in range(ITERS):
         recv = lax.all_to_all(send, ("strip", "track"), 0, 0)
         if step_number == 0:
-            recv, diag, coupling, *nearer = lax.optimization_barrier((recv, diag, coupling, *nearer))
+            recv, diag, coupling, edge_map, *nearer = lax.optimization_barrier(
+                (recv, diag, coupling, edge_map, *nearer)
+            )
+            edge_map = lax.ppermute(edge_map, "track", [((i + 1) % n_track, i) for i in range(n_track)])
             nearer += [lax.ppermute(part, "track", swap) for part in nearer]
             diag_flip, coupling_flip = flip(diag, coupling)
         value, first, second, entry = call(
@@ -427,9 +434,6 @@
             [VMEM] * (7 + len(nearer)) + [SMEM],
             recv, local, begins, maps, through, other, coupling, *nearer, pos,
         )
-        if step_number == 0:
-            edge_map, entry = lax.optimization_barrier((edge_map, entry))
-            edge_map = lax.ppermute(edge_map, "track", [((i + 1) % n_track, i) for i in range(n_track)])
         first = lax.ppermute(first, "strip", pairs)
         second = lax.ppermute(second, ("track", "strip"), cross)
         base, state, alpha = call(
@@ -440,15 +444,15 @@
         )
         args = (
             base, first, second, value, recv, state, image, alpha, edge_map, coupling_flip, lower, lower_flip,
-            precond_flip, maps, other, links, pos,
+            precond_flip, maps, last_two, other, links, pos,
         )
-        specs = [VMEM] * 15 + [SMEM] * 2
+        specs = [VMEM] * 16 + [SMEM] * 2
         if step_number < ITERS - 1:
             kernel = functools.partial(update_kernel, cap, n_track, n_strip, step_number == 0)
             image, local, begins, send = call(kernel, [block, block, chain, chunk], specs, *args)
         else:
             kernel = functools.partial(last_update_kernel, cap, n_track, n_strip)
-            image, send = call(kernel, [block, chunk], specs, *args)
+            image, send = call(kernel, [block, (whole, 2, 128)], specs, *args)
     recv = lax.all_to_all(send, ("strip", "track"), 0, 0)
     solution, residual = call(final_kernel, [block, block], [VMEM] * 3, recv, state, image)
     return (solution[None], residual[None])

time: 138 us -> 134 us (0.971)
  blocking collectives: 75.6 us -> 73.6 us
    all_to_all x7, blocking collectives: 75.6 us -> 73.6 us  [body(): recv = lax.all_to_all(send, ('strip', 'track'), 0, 0)]
  transfers between devices with their start and end apart: 18 -> 16, of which waited for: 9 -> 7; matrix products, arithmetic and copies ran while one was open for 0% -> 0% of each run, Pallas kernels for 9% -> 11%
where the time goes in v5:
time: 134 us
  blocking collectives  73.6 us (55%)
  Pallas kernels  44.8 us (33%)
  waiting for transfers between devices  8.2 us (6%)
  starting transfers between devices  5.79 us (4%)
  between operations  1.41 us (1%)
    all_to_all x7, blocking collectives, body(): recv = lax.all_to_all(send, ('strip', 'track'), 0, 0)  73.6 us
    pallas_call x23, Pallas kernels, call(): pl.pallas_call(kernel, out_shape=[pltpu.VMEM(shape, dtype) if math.prod(s...  44.8 us
    ppermute x6, waiting for transfers between devices, body(): first = lax.ppermute(first, 'strip', pairs)  7.43 us
    ppermute x6, starting transfers between devices, body(): first = lax.ppermute(first, 'strip', pairs)  4 us
  transfers between devices with their start and end apart: 16, of which 7 were waited for; matrix products, arithmetic and copies ran while one was open for 0% of the time, Pallas kernels for 11%

profile of v5, /device:TPU:0, one launch (start us, length us, event | category | flops | bytes accessed | tf_op | source)
XLA Modules:
  0.0 133.9 jit_solution(7113647978155952061)
XLA Ops:
  1.3 0.1 pad_add_fusion.pos_ref.refs_2_.refs_17_
  1.4 8.1 %shard_map.86 = (f32[16,256,256]{2,1,0:T(8,128)S(1)}, f32[256,256]{1,0:T(8,128)S(1)}, f32[256,256]{1,0:T(8,128)S(1)}, f32[16,256]{1,0:T(8,128)S(1)}, f32[2,256]{...) custom-call(f32[16,256]{1,0:T(8,128)} %bitcast.9, ...), custom_call_target="tpu_custom_call" | custom-call | tf_op jit(solution)/shard_map/pallas_call | solution.py:355
  9.5 0.5 collective-permute-start
  10.0 1.1 shard_map.87
  11.1 0.0 collective-permute-done.other_ref.refs_15_
  11.2 0.9 shard_map.88
  12.1 0.4 collective-permute-start.1
  12.5 14.6 %all_to_all.35.recv_ref = f32[32,4,128]{2,1,0:T(4,128)S(1)} all-to-all(f32[32,4,128]{2,1,0:T(4,128)S(1)} %get-tuple-element.100), channel_id=1, replica_groups=mesh['track'=8,'strip'=4] {'strip','track'}, dimensions={0} | all-to-all | bytes 131072 | tf_op jit(solution)/shard_map/all_to_all | solution.py:423
  27.1 0.0 collective-permute-done.1.refs_0_
  27.1 0.1 collective-permute-start.2
  27.3 0.7 collective-permute-start.5
  28.0 0.7 collective-permute-done.2.refs_1_
  28.7 1.7 %shard_map.89 = (f32[16,256]{1,0:T(8,128)S(1)}, f32[16,256]{1,0:T(8,128)S(1)}, f32[16,256]{1,0:T(8,128)S(1)}, f32[1,256]{1,0:T(1,128)S(1)}) custom-call(f32[32,4,128]{2,1,0:T(4,128)S(1)} %all_to_all.35.recv_ref, f32[16,256]{1,0:T(8,128)S(1)} %get-tuple-element.104.local_ref, f32[4,256]{1,0:T(4,128)S(1)} %get-tuple-element.105.begins_ref, ...), custom_call_target="tpu_custom_call" | custom-call | tf_op jit(solution)/shard_map/pallas_call | solution.py:355
  30.4 0.7 collective-permute-start.3
  31.1 0.0 collective-permute-start.4
  31.1 1.1 shard_map.90
  32.2 0.0 copy-done
  32.2 1.7 %shard_map.91 = (f32[16,256]{1,0:T(8,128)S(1)}, f32[3,16,256]{2,1,0:T(8,128)S(1)}, f32[1,256]{1,0:T(1,128)S(1)}) custom-call(f32[16,256]{1,0:T(8,128)S(1)} %get-tuple-element.109.value_ref, f32[1,256]{1,0:T(1,128)S(1)} %get-tuple-element.110.entry_ref, f32[32,4,128]{2,1,0:T(4,128)S(1)} %all_to_all.35.recv_ref, f32[16,256]{1,0:T(8,128)S(1)} %bitcast.10, ...), custom_call_target="tpu_custom_call" | custom-call | tf_op jit(solution)/shard_map/pallas_call | solution.py:355
  33.9 0.0 collective-permute-done.5.edge_map_ref.refs_8_
  33.9 0.3 collective-permute-done.3.first_ref
  34.2 0.0 collective-permute-done.4.second_ref
  34.2 2.3 %shard_map.92 = (f32[16,256]{1,0:T(8,128)S(1)}, f32[16,256]{1,0:T(8,128)S(1)}, f32[4,256]{1,0:T(4,128)S(1)}, f32[32,4,128]{2,1,0:T(4,128)S(1)}) custom-call(f32[16,256]{1,0:T(8,128)S(1)} %get-tuple-element.113.base_ref, f32[16,256]{1,0:T(8,128)S(1)} %collective-permute-done.3.first_ref, f32[16,256]{1,0:T(8,128)S(1)} %collective-permute-done.4.second_ref, ...), custom_call_target="tpu_custom_call" | custom-call | tf_op jit(solution)/shard_map/pallas_call | solution.py:355
  36.5 10.4 %all_to_all.36.recv_ref = f32[32,4,128]{2,1,0:T(4,128)S(1)} all-to-all(f32[32,4,128]{2,1,0:T(4,128)S(1)} %get-tuple-element.121), channel_id=1, replica_groups=mesh['track'=8,'strip'=4] {'strip','track'}, dimensions={0} | all-to-all | bytes 131072 | tf_op jit(solution)/shard_map/all_to_all | solution.py:423
  46.8 1.7 %shard_map.93 = (f32[16,256]{1,0:T(8,128)S(1)}, f32[16,256]{1,0:T(8,128)S(1)}, f32[16,256]{1,0:T(8,128)S(1)}, f32[1,256]{1,0:T(1,128)S(1)}) custom-call(f32[32,4,128]{2,1,0:T(4,128)S(1)} %all_to_all.36.recv_ref, f32[16,256]{1,0:T(8,128)S(1)} %get-tuple-element.122.local_ref, f32[4,256]{1,0:T(4,128)S(1)} %get-tuple-element.123.begins_ref, ...), custom_call_target="tpu_custom_call" | custom-call | tf_op jit(solution)/shard_map/pallas_call | solution.py:355
  48.5 0.7 collective-permute-start.6
  49.2 0.0 collective-permute-start.7
  49.2 1.7 %shard_map.94 = (f32[16,256]{1,0:T(8,128)S(1)}, f32[3,16,256]{2,1,0:T(8,128)S(1)}, f32[1,256]{1,0:T(1,128)S(1)}) custom-call(f32[16,256]{1,0:T(8,128)S(1)} %get-tuple-element.124.value_ref, f32[1,256]{1,0:T(1,128)S(1)} %get-tuple-element.125.entry_ref, f32[32,4,128]{2,1,0:T(4,128)S(1)} %all_to_all.36.recv_ref, ...), custom_call_target="tpu_custom_call" | custom-call | tf_op jit(solution)/shard_map/pallas_call | solution.py:355
  50.9 1.4 %collective-permute-done.6.first_ref = f32[16,256]{1,0:T(8,128)S(1)} collective-permute-done((f32[16,256]{1,0:T(8,128)S(1)}, f32[16,256]{1,0:T(8,128)S(1)}, u32[]{:S(2)}, u32[]{:S(2)}) %collective-permute-start.6) | collective-permute-done | bytes 16416 | tf_op jit(solution)/shard_map/ppermute | solution.py:437
  52.3 0.0 collective-permute-done.7.second_ref
  52.3 2.3 %shard_map.95 = (f32[16,256]{1,0:T(8,128)S(1)}, f32[16,256]{1,0:T(8,128)S(1)}, f32[4,256]{1,0:T(4,128)S(1)}, f32[32,4,128]{2,1,0:T(4,128)S(1)}) custom-call(f32[16,256]{1,0:T(8,128)S(1)} %get-tuple-element.127.base_ref, f32[16,256]{1,0:T(8,128)S(1)} %collective-permute-done.6.first_ref, f32[16,256]{1,0:T(8,128)S(1)} %collective-permute-done.7.second_ref, ...), custom_call_target="tpu_custom_call" | custom-call | tf_op jit(solution)/shard_map/pallas_call | solution.py:355
  54.6 9.8 %all_to_all.37.recv_ref = f32[32,4,128]{2,1,0:T(4,128)S(1)} all-to-all(f32[32,4,128]{2,1,0:T(4,128)S(1)} %get-tuple-element.132), channel_id=1, replica_groups=mesh['track'=8,'strip'=4] {'strip','track'}, dimensions={0} | all-to-all | bytes 131072 | tf_op jit(solution)/shard_map/all_to_all | solution.py:423
  64.4 1.7 %shard_map.96 = (f32[16,256]{1,0:T(8,128)S(1)}, f32[16,256]{1,0:T(8,128)S(1)}, f32[16,256]{1,0:T(8,128)S(1)}, f32[1,256]{1,0:T(1,128)S(1)}) custom-call(f32[32,4,128]{2,1,0:T(4,128)S(1)} %all_to_all.37.recv_ref, f32[16,256]{1,0:T(8,128)S(1)} %get-tuple-element.133.local_ref, f32[4,256]{1,0:T(4,128)S(1)} %get-tuple-element.134.begins_ref, ...), custom_call_target="tpu_custom_call" | custom-call | tf_op jit(solution)/shard_map/pallas_call | solution.py:355
  66.1 0.7 collective-permute-start.8
  66.7 0.0 collective-permute-start.9
  66.7 1.7 %shard_map.97 = (f32[16,256]{1,0:T(8,128)S(1)}, f32[3,16,256]{2,1,0:T(8,128)S(1)}, f32[1,256]{1,0:T(1,128)S(1)}) custom-call(f32[16,256]{1,0:T(8,128)S(1)} %get-tuple-element.135.value_ref, f32[1,256]{1,0:T(1,128)S(1)} %get-tuple-element.136.entry_ref, f32[32,4,128]{2,1,0:T(4,128)S(1)} %all_to_all.37.recv_ref, ...), custom_call_target="tpu_custom_call" | custom-call | tf_op jit(solution)/shard_map/pallas_call | solution.py:355
  68.4 1.4 %collective-permute-done.8.first_ref = f32[16,256]{1,0:T(8,128)S(1)} collective-permute-done((f32[16,256]{1,0:T(8,128)S(1)}, f32[16,256]{1,0:T(8,128)S(1)}, u32[]{:S(2)}, u32[]{:S(2)}) %collective-permute-start.8) | collective-permute-done | bytes 16416 | tf_op jit(solution)/shard_map/ppermute | solution.py:437
  69.9 0.0 collective-permute-done.9.second_ref
  69.9 2.3 %shard_map.98 = (f32[16,256]{1,0:T(8,128)S(1)}, f32[16,256]{1,0:T(8,128)S(1)}, f32[4,256]{1,0:T(4,128)S(1)}, f32[32,4,128]{2,1,0:T(4,128)S(1)}) custom-call(f32[16,256]{1,0:T(8,128)S(1)} %get-tuple-element.138.base_ref, f32[16,256]{1,0:T(8,128)S(1)} %collective-permute-done.8.first_ref, f32[16,256]{1,0:T(8,128)S(1)} %collective-permute-done.9.second_ref, ...), custom_call_target="tpu_custom_call" | custom-call | tf_op jit(solution)/shard_map/pallas_call | solution.py:355
  72.1 9.8 %all_to_all.38.recv_ref = f32[32,4,128]{2,1,0:T(4,128)S(1)} all-to-all(f32[32,4,128]{2,1,0:T(4,128)S(1)} %get-tuple-element.143), channel_id=1, replica_groups=mesh['track'=8,'strip'=4] {'strip','track'}, dimensions={0} | all-to-all | bytes 131072 | tf_op jit(solution)/shard_map/all_to_all | solution.py:423
  81.9 1.7 %shard_map.99 = (f32[16,256]{1,0:T(8,128)S(1)}, f32[16,256]{1,0:T(8,128)S(1)}, f32[16,256]{1,0:T(8,128)S(1)}, f32[1,256]{1,0:T(1,128)S(1)}) custom-call(f32[32,4,128]{2,1,0:T(4,128)S(1)} %all_to_all.38.recv_ref, f32[16,256]{1,0:T(8,128)S(1)} %get-tuple-element.144.local_ref, f32[4,256]{1,0:T(4,128)S(1)} %get-tuple-element.145.begins_ref, ...), custom_call_target="tpu_custom_call" | custom-call | tf_op jit(solution)/shard_map/pallas_call | solution.py:355
  83.6 0.7 collective-permute-start.10
  84.3 0.0 collective-permute-start.11
  84.3 1.7 %shard_map.100 = (f32[16,256]{1,0:T(8,128)S(1)}, f32[3,16,256]{2,1,0:T(8,128)S(1)}, f32[1,256]{1,0:T(1,128)S(1)}) custom-call(f32[16,256]{1,0:T(8,128)S(1)} %get-tuple-element.146.value_ref, f32[1,256]{1,0:T(1,128)S(1)} %get-tuple-element.147.entry_ref, f32[32,4,128]{2,1,0:T(4,128)S(1)} %all_to_all.38.recv_ref, ...), custom_call_target="tpu_custom_call" | custom-call | tf_op jit(solution)/shard_map/pallas_call | solution.py:355
  86.0 1.4 %collective-permute-done.10.first_ref = f32[16,256]{1,0:T(8,128)S(1)} collective-permute-done((f32[16,256]{1,0:T(8,128)S(1)}, f32[16,256]{1,0:T(8,128)S(1)}, u32[]{:S(2)}, u32[]{:S(2)}) %collective-permute-start.10) | collective-permute-done | bytes 16416 | tf_op jit(solution)/shard_map/ppermute | solution.py:437
  87.4 0.0 collective-permute-done.11.second_ref
  87.4 2.3 %shard_map.101 = (f32[16,256]{1,0:T(8,128)S(1)}, f32[16,256]{1,0:T(8,128)S(1)}, f32[4,256]{1,0:T(4,128)S(1)}, f32[32,4,128]{2,1,0:T(4,128)S(1)}) custom-call(f32[16,256]{1,0:T(8,128)S(1)} %get-tuple-element.149.base_ref, f32[16,256]{1,0:T(8,128)S(1)} %collective-permute-done.10.first_ref, f32[16,256]{1,0:T(8,128)S(1)} %collective-permute-done.11.second_ref, ...), custom_call_target="tpu_custom_call" | custom-call | tf_op jit(solution)/shard_map/pallas_call | solution.py:355
  89.7 9.8 %all_to_all.39.recv_ref = f32[32,4,128]{2,1,0:T(4,128)S(1)} all-to-all(f32[32,4,128]{2,1,0:T(4,128)S(1)} %get-tuple-element.154), channel_id=1, replica_groups=mesh['track'=8,'strip'=4] {'strip','track'}, dimensions={0} | all-to-all | bytes 131072 | tf_op jit(solution)/shard_map/all_to_all | solution.py:423
  99.4 1.7 %shard_map.102 = (f32[16,256]{1,0:T(8,128)S(1)}, f32[16,256]{1,0:T(8,128)S(1)}, f32[16,256]{1,0:T(8,128)S(1)}, f32[1,256]{1,0:T(1,128)S(1)}) custom-call(f32[32,4,128]{2,1,0:T(4,128)S(1)} %all_to_all.39.recv_ref, f32[16,256]{1,0:T(8,128)S(1)} %get-tuple-element.155.local_ref, f32[4,256]{1,0:T(4,128)S(1)} %get-tuple-element.156.begins_ref, ...), custom_call_target="tpu_custom_call" | custom-call | tf_op jit(solution)/shard_map/pallas_call | solution.py:355
  101.1 0.7 collective-permute-start.12
  101.8 0.0 collective-permute-start.13
  101.8 1.7 %shard_map.103 = (f32[16,256]{1,0:T(8,128)S(1)}, f32[3,16,256]{2,1,0:T(8,128)S(1)}, f32[1,256]{1,0:T(1,128)S(1)}) custom-call(f32[16,256]{1,0:T(8,128)S(1)} %get-tuple-element.157.value_ref, f32[1,256]{1,0:T(1,128)S(1)} %get-tuple-element.158.entry_ref, f32[32,4,128]{2,1,0:T(4,128)S(1)} %all_to_all.39.recv_ref, ...), custom_call_target="tpu_custom_call" | custom-call | tf_op jit(solution)/shard_map/pallas_call | solution.py:355
  103.5 1.4 %collective-permute-done.12.first_ref = f32[16,256]{1,0:T(8,128)S(1)} collective-permute-done((f32[16,256]{1,0:T(8,128)S(1)}, f32[16,256]{1,0:T(8,128)S(1)}, u32[]{:S(2)}, u32[]{:S(2)}) %collective-permute-start.12) | collective-permute-done | bytes 16416 | tf_op jit(solution)/shard_map/ppermute | solution.py:437
  104.9 0.0 collective-permute-done.13.second_ref
  104.9 2.3 %shard_map.104 = (f32[16,256]{1,0:T(8,128)S(1)}, f32[16,256]{1,0:T(8,128)S(1)}, f32[4,256]{1,0:T(4,128)S(1)}, f32[32,4,128]{2,1,0:T(4,128)S(1)}) custom-call(f32[16,256]{1,0:T(8,128)S(1)} %get-tuple-element.160.base_ref, f32[16,256]{1,0:T(8,128)S(1)} %collective-permute-done.12.first_ref, f32[16,256]{1,0:T(8,128)S(1)} %collective-permute-done.13.second_ref, ...), custom_call_target="tpu_custom_call" | custom-call | tf_op jit(solution)/shard_map/pallas_call | solution.py:355
  107.2 9.8 %all_to_all.40.recv_ref.refs_4_ = f32[32,4,128]{2,1,0:T(4,128)S(1)} all-to-all(f32[32,4,128]{2,1,0:T(4,128)S(1)} %get-tuple-element.165), channel_id=1, replica_groups=mesh['track'=8,'strip'=4] {'strip','track'}, dimensions={0} | all-to-all | bytes 131072 | tf_op jit(solution)/shard_map/all_to_all | solution.py:423
  117.0 1.7 %shard_map.105 = (f32[16,256]{1,0:T(8,128)S(1)}, f32[16,256]{1,0:T(8,128)S(1)}, f32[16,256]{1,0:T(8,128)S(1)}, f32[1,256]{1,0:T(1,128)S(1)}) custom-call(f32[32,4,128]{2,1,0:T(4,128)S(1)} %all_to_all.40.recv_ref.refs_4_, f32[16,256]{1,0:T(8,128)S(1)} %get-tuple-element.166.local_ref, f32[4,256]{1,0:T(4,128)S(1)} %get-tuple-element.167.begins_ref, ...), custom_call_target="tpu_custom_call" | custom-call | tf_op jit(solution)/shard_map/pallas_call | solution.py:355
  118.7 0.7 collective-permute-start.14
  119.3 0.0 collective-permute-start.15
  119.3 1.7 %shard_map.106 = (f32[16,256]{1,0:T(8,128)S(1)}, f32[3,16,256]{2,1,0:T(8,128)S(1)}, f32[1,256]{1,0:T(1,128)S(1)}) custom-call(f32[16,256]{1,0:T(8,128)S(1)} %get-tuple-element.168.value_ref.refs_3_, f32[1,256]{1,0:T(1,128)S(1)} %get-tuple-element.169.entry_ref, f32[32,4,128]{2,1,0:T(4,128)S(1)} %all_to_all.40.recv_ref.refs_4_, ...), custom_call_target="tpu_custom_call" | custom-call | tf_op jit(solution)/shard_map/pallas_call | solution.py:355
  121.0 1.4 %collective-permute-done.14.refs_1_ = f32[16,256]{1,0:T(8,128)S(1)} collective-permute-done((f32[16,256]{1,0:T(8,128)S(1)}, f32[16,256]{1,0:T(8,128)S(1)}, u32[]{:S(2)}, u32[]{:S(2)}) %collective-permute-start.14) | collective-permute-done | bytes 16416 | tf_op jit(solution)/shard_map/ppermute | solution.py:437
  122.5 0.0 collective-permute-done.15.refs_2_
  122.5 1.0 shard_map.107
  123.5 9.6 %all_to_all.41.recv_ref = f32[32,2,128]{2,1,0:T(2,128)S(1)} all-to-all(f32[32,2,128]{2,1,0:T(2,128)S(1)} %get-tuple-element.176), channel_id=1, replica_groups=mesh['track'=8,'strip'=4] {'strip','track'}, dimensions={0} | all-to-all | bytes 65536 | tf_op jit(solution)/shard_map/all_to_all | solution.py:456
  133.1 0.8 shard_map.108
  (3 shorter events, 0.0 us)
Async XLA Ops:
  9.5 1.7 %collective-permute-start = (f32[256,256]{1,0:T(8,128)S(1)}, f32[256,256]{1,0:T(8,128)S(1)}, u32[]{:S(2)}, u32[]{:S(2)}) collective-permute-start(f32[256,256]{1,0:T(8,128)S(1)} %get-tuple-element.91.total_ref), channel_id=1, source_target_pairs={{0,4},{4,0},{8,12},{12,8},{16,20},{20,16},{24,28},{28,24},{1,5},{5... | collective-permute-start | bytes 786440 | tf_op jit(solution)/shard_map/ppermute | solution.py:397
  12.1 15.0 %collective-permute-start.1 = (f32[256,256]{1,0:T(8,128)S(1)}, f32[256,256]{1,0:T(8,128)S(1)}, u32[]{:S(2)}, u32[]{:S(2)}) collective-permute-start(f32[256,256]{1,0:T(8,128)S(1)} %get-tuple-element.102), channel_id=1, source_target_pairs={{0,4},{4,0},{8,16},{12,28},{16,24},{20,12},{24,8},{28,20},{1,5},{5... | collective-permute-start | bytes 786440 | tf_op jit(solution)/shard_map/ppermute | solution.py:410
  27.1 1.5 %collective-permute-start.2 = (f32[256,256]{1,0:T(8,128)S(1)}, f32[256,256]{1,0:T(8,128)S(1)}, u32[]{:S(2)}, u32[]{:S(2)}) collective-permute-start(f32[256,256]{1,0:T(8,128)S(1)} %collective-permute-done.1.refs_0_), channel_id=1, source_target_pairs={{0,4},{4,0},{8,12},{12,8},{16,20},{20,16},{24,28},{28,24},{1,5},{5... | collective-permute-start | bytes 786440 | tf_op jit(solution)/shard_map/ppermute | solution.py:429
  27.3 6.6 %collective-permute-start.5 = (f32[256,256]{1,0:T(8,128)S(1)}, f32[256,256]{1,0:T(8,128)S(1)}, u32[]{:S(2)}, u32[]{:S(2)}) collective-permute-start(f32[256,256]{1,0:T(8,128)S(1)} %get-tuple-element.118), channel_id=1, source_target_pairs={{4,0},{8,4},{12,8},{16,12},{20,16},{24,20},{28,24},{0,28},{5,1},{9... | collective-permute-start | bytes 786440 | tf_op jit(solution)/shard_map/ppermute | solution.py:428
  30.4 3.8 %collective-permute-start.3 = (f32[16,256]{1,0:T(8,128)S(1)}, f32[16,256]{1,0:T(8,128)S(1)}, u32[]{:S(2)}, u32[]{:S(2)}) collective-permute-start(f32[16,256]{1,0:T(8,128)S(1)} %get-tuple-element.114), channel_id=1, source_target_pairs={{0,1},{1,0},{2,3},{3,2},{4,5},{5,4},{6,7},{7,6},{8,9},{9,8},{10,11... | collective-permute-start | bytes 49160 | tf_op jit(solution)/shard_map/ppermute | solution.py:437
  31.1 1.1 copy-start
  31.1 1.2 copy-start.1
  31.1 3.1 %collective-permute-start.4 = (f32[16,256]{1,0:T(8,128)S(1)}, f32[16,256]{1,0:T(8,128)S(1)}, u32[]{:S(2)}, u32[]{:S(2)}) collective-permute-start(f32[16,256]{1,0:T(8,128)S(1)} %get-tuple-element.115), channel_id=1, source_target_pairs={{0,4},{1,2},{2,1},{3,7},{4,0},{5,6},{6,5},{7,3},{8,12},{9,10},{10,... | collective-permute-start | bytes 49160 | tf_op jit(solution)/shard_map/ppermute | solution.py:438
  48.5 3.8 %collective-permute-start.6 = (f32[16,256]{1,0:T(8,128)S(1)}, f32[16,256]{1,0:T(8,128)S(1)}, u32[]{:S(2)}, u32[]{:S(2)}) collective-permute-start(f32[16,256]{1,0:T(8,128)S(1)} %get-tuple-element.128), channel_id=1, source_target_pairs={{0,1},{1,0},{2,3},{3,2},{4,5},{5,4},{6,7},{7,6},{8,9},{9,8},{10,11... | collective-permute-start | bytes 49160 | tf_op jit(solution)/shard_map/ppermute | solution.py:437
  49.2 3.1 %collective-permute-start.7 = (f32[16,256]{1,0:T(8,128)S(1)}, f32[16,256]{1,0:T(8,128)S(1)}, u32[]{:S(2)}, u32[]{:S(2)}) collective-permute-start(f32[16,256]{1,0:T(8,128)S(1)} %get-tuple-element.129), channel_id=1, source_target_pairs={{0,4},{1,2},{2,1},{3,7},{4,0},{5,6},{6,5},{7,3},{8,12},{9,10},{10,... | collective-permute-start | bytes 49160 | tf_op jit(solution)/shard_map/ppermute | solution.py:438
  66.1 3.8 %collective-permute-start.8 = (f32[16,256]{1,0:T(8,128)S(1)}, f32[16,256]{1,0:T(8,128)S(1)}, u32[]{:S(2)}, u32[]{:S(2)}) collective-permute-start(f32[16,256]{1,0:T(8,128)S(1)} %get-tuple-element.139), channel_id=1, source_target_pairs={{0,1},{1,0},{2,3},{3,2},{4,5},{5,4},{6,7},{7,6},{8,9},{9,8},{10,11... | collective-permute-start | bytes 49160 | tf_op jit(solution)/shard_map/ppermute | solution.py:437
  66.7 3.1 %collective-permute-start.9 = (f32[16,256]{1,0:T(8,128)S(1)}, f32[16,256]{1,0:T(8,128)S(1)}, u32[]{:S(2)}, u32[]{:S(2)}) collective-permute-start(f32[16,256]{1,0:T(8,128)S(1)} %get-tuple-element.140), channel_id=1, source_target_pairs={{0,4},{1,2},{2,1},{3,7},{4,0},{5,6},{6,5},{7,3},{8,12},{9,10},{10,... | collective-permute-start | bytes 49160 | tf_op jit(solution)/shard_map/ppermute | solution.py:438
  83.6 3.8 %collective-permute-start.10 = (f32[16,256]{1,0:T(8,128)S(1)}, f32[16,256]{1,0:T(8,128)S(1)}, u32[]{:S(2)}, u32[]{:S(2)}) collective-permute-start(f32[16,256]{1,0:T(8,128)S(1)} %get-tuple-element.150), channel_id=1, source_target_pairs={{0,1},{1,0},{2,3},{3,2},{4,5},{5,4},{6,7},{7,6},{8,9},{9,8},{10,11... | collective-permute-start | bytes 49160 | tf_op jit(solution)/shard_map/ppermute | solution.py:437
  84.3 3.1 %collective-permute-start.11 = (f32[16,256]{1,0:T(8,128)S(1)}, f32[16,256]{1,0:T(8,128)S(1)}, u32[]{:S(2)}, u32[]{:S(2)}) collective-permute-start(f32[16,256]{1,0:T(8,128)S(1)} %get-tuple-element.151), channel_id=1, source_target_pairs={{0,4},{1,2},{2,1},{3,7},{4,0},{5,6},{6,5},{7,3},{8,12},{9,10},{10,... | collective-permute-start | bytes 49160 | tf_op jit(solution)/shard_map/ppermute | solution.py:438
  101.1 3.8 %collective-permute-start.12 = (f32[16,256]{1,0:T(8,128)S(1)}, f32[16,256]{1,0:T(8,128)S(1)}, u32[]{:S(2)}, u32[]{:S(2)}) collective-permute-start(f32[16,256]{1,0:T(8,128)S(1)} %get-tuple-element.161), channel_id=1, source_target_pairs={{0,1},{1,0},{2,3},{3,2},{4,5},{5,4},{6,7},{7,6},{8,9},{9,8},{10,11... | collective-permute-start | bytes 49160 | tf_op jit(solution)/shard_map/ppermute | solution.py:437
  101.8 3.1 %collective-permute-start.13 = (f32[16,256]{1,0:T(8,128)S(1)}, f32[16,256]{1,0:T(8,128)S(1)}, u32[]{:S(2)}, u32[]{:S(2)}) collective-permute-start(f32[16,256]{1,0:T(8,128)S(1)} %get-tuple-element.162), channel_id=1, source_target_pairs={{0,4},{1,2},{2,1},{3,7},{4,0},{5,6},{6,5},{7,3},{8,12},{9,10},{10,... | collective-permute-start | bytes 49160 | tf_op jit(solution)/shard_map/ppermute | solution.py:438
  118.7 3.8 %collective-permute-start.14 = (f32[16,256]{1,0:T(8,128)S(1)}, f32[16,256]{1,0:T(8,128)S(1)}, u32[]{:S(2)}, u32[]{:S(2)}) collective-permute-start(f32[16,256]{1,0:T(8,128)S(1)} %get-tuple-element.172), channel_id=1, source_target_pairs={{0,1},{1,0},{2,3},{3,2},{4,5},{5,4},{6,7},{7,6},{8,9},{9,8},{10,11... | collective-permute-start | bytes 49160 | tf_op jit(solution)/shard_map/ppermute | solution.py:437
  119.3 3.1 %collective-permute-start.15 = (f32[16,256]{1,0:T(8,128)S(1)}, f32[16,256]{1,0:T(8,128)S(1)}, u32[]{:S(2)}, u32[]{:S(2)}) collective-permute-start(f32[16,256]{1,0:T(8,128)S(1)} %get-tuple-element.173), channel_id=1, source_target_pairs={{0,4},{1,2},{2,1},{3,7},{4,0},{5,6},{6,5},{7,3},{8,12},{9,10},{10,... | collective-permute-start | bytes 49160 | tf_op jit(solution)/shard_map/ppermute | solution.py:438

commit v6 on v5

--- a/solution.py
+++ b/solution.py
@@ -39,10 +39,22 @@
     return out[:ROWS] + out[2 * ROWS : 3 * ROWS] + out[4 * ROWS : 5 * ROWS]
 
 
+def two_pieces(value):
+    high = value.astype(jnp.bfloat16)
+    return high, (value - high.astype(F32)).astype(jnp.bfloat16)
+
+
 def times_matrix(value, matrix, dims):
-    out = lax.dot_general(pieces(value), matrix, dims, preferred_element_type=F32)
+    lhs = jnp.concatenate(two_pieces(value), axis=0)
+    out = lax.dot_general(lhs, matrix, dims, preferred_element_type=F32)
     n = value.shape[0]
-    return out[:n] + out[n : 2 * n] + out[2 * n :]
+    return out[:n] + out[n:]
+
+
+def product(left, right):
+    high, rest = two_pieces(right)
+    cross = lax.dot_general(left.astype(jnp.bfloat16), rest, NN, preferred_element_type=F32)
+    return times_matrix(left, high, NN) + cross
 
 
 def spread(row):
@@ -83,9 +95,9 @@
     return [row[:, i : i + 128] for i in range(0, row.shape[1], 128)]
 
 
-def send_ends(end, first, dots, other_ref, pos_ref, n_track, out_ref):
+def send_ends(end, carried, first, dots, pos_ref, n_track, out_ref):
     track = pos_ref[0]
-    carried = jnp.where(track % 2 == 0, times_f32(spread(end), other_ref[...]), end)
+    carried = jnp.where(track % 2 == 0, carried, end)
     near = jnp.concatenate(halves(end) + dots, axis=0)
     far = jnp.concatenate(halves(carried) + dots, axis=0)
     back = jnp.concatenate(halves(first) + dots, axis=0)
@@ -100,7 +112,7 @@
         ends.append(state[q][:1] + times_f32(spread(ends[-1]), maps_ref[q * length + length - 1]))
     last = state[-1][:1] + times_f32(spread(state[-2][:1]), maps_ref[CHAINS * length - 1])
     ends.append(last + times_f32(spread(ends[-2]), last_two_ref[...]))
-    return ends
+    return ends, last
 
 
 def maps_kernel(
@@ -167,7 +179,7 @@
     span = 1
     while span < CHAINS:
         state = [
-            state[q] if q < span else jnp.dot(state[q - span], state[q], precision=lax.Precision.HIGHEST)
+            state[q] if q < span else product(state[q - span], state[q])
             for q in range(CHAINS)
         ]
         if span == 1:
@@ -176,21 +188,24 @@
     for q in range(CHAINS - 1):
         through_ref[q] = state[q]
     total_ref[...] = state[-1]
-    ends = chain_ends(local, maps_ref, last_two_ref, length)
+    ends, _ = chain_ends(local, maps_ref, last_two_ref, length)
     ends_ref[0:1, :] = ends[-1]
     begins_ref[...] = jnp.concatenate(ends, axis=0)
     for copy in copies[-2:]:
         copy.wait()
 
 
-def pair_kernel(n_track, total_ref, other_ref, ends_ref, pos_ref, *refs):
-    chip_ref, send_ref = refs[-2:]
+def pair_kernel(n_track, total_ref, other_ref, ends_ref, last_two_ref, pos_ref, *refs):
+    chip_ref, beyond_ref, send_ref = refs[-3:]
     first_core = pos_ref[0] % 2 == 0
     own, other = total_ref[...], other_ref[...]
     early, late = jnp.where(first_core, own, other), jnp.where(first_core, other, own)
-    chip_ref[...] = jnp.dot(early, late, precision=lax.Precision.HIGHEST)
+    chip_ref[...] = product(early, late)
     dots = [jnp.zeros((1, 128), F32)] * 2
-    send_ends(ends_ref[0:1, :], ends_ref[1:2, :], dots, other_ref, pos_ref, n_track, send_ref)
+    end = ends_ref[0:1, :]
+    carried = times_f32(spread(end), other_ref[...])
+    send_ends(end, carried, ends_ref[1:2, :], dots, pos_ref, n_track, send_ref)
+    beyond_ref[...] = product(last_two_ref[...], other_ref[...])
 
 
 def direction_kernel(cap, n_track, recv_ref, local_ref, begins_ref, maps_ref, through_ref, other_ref, coupling_ref, *refs):
@@ -199,7 +214,7 @@
     width = local_ref.shape[1]
     length = cap // CHAINS
     half = width // 128
-    base = strip * n_track
+    base = strip * n_track if recv_ref.shape[0] > n_track else 0
     chip = track // 2
 
     def chunk(index, valid):
@@ -251,7 +266,7 @@
 
 
 def local_kernel(
-    cap, first, value_ref, entry_ref, recv_ref, state_ref, image_ref, diag_flip_ref, lower_ref,
+    cap, first, value_ref, entry_ref, recv_ref, state_ref, image_ref, diag_ref, lower_ref,
     lower_flip_ref, links_ref, pos_ref, base_ref, next_ref, alpha_ref,
 ):
     width = value_ref.shape[1]
@@ -260,7 +275,7 @@
     held = None
     for j in range(cap):
         lhs = split_row(wide_row(value_ref, j))
-        own = times(lhs, diag_flip_ref[j], NN) + lowered
+        own = times(lhs, diag_ref[j], NT) + lowered
         if j > 0:
             held = held + on[j] * times(lhs, lower_ref[j], NN)
             base_ref[j - 1 : j, :] = held[:1]
@@ -283,7 +298,7 @@
 
 def update_kernel(
     cap, n_track, n_strip, first, base_ref, first_ref, second_ref, value_ref, recv_ref, state_ref, image_ref, alpha_ref,
-    edge_map_ref, coupling_flip_ref, lower_ref, lower_flip_ref, precond_flip_ref, maps_ref, last_two_ref, other_ref, links_ref, pos_ref,
+    edge_map_ref, coupling_flip_ref, lower_ref, lower_flip_ref, precond_flip_ref, maps_ref, last_two_ref, beyond_ref, other_ref, links_ref, pos_ref,
     next_ref, local_ref, begins_ref, send_ref,
 ):
     track, strip, count = pos_ref[0], pos_ref[1], pos_ref[2]
@@ -293,7 +308,8 @@
     one, two = first_ref[...], second_ref[...]
     below = jnp.where(strip > 0, jnp.where(odd, one, two), 0.0)
     above = jnp.where(strip < n_strip - 1, jnp.where(odd, two, one), 0.0)
-    ahead = recv_ref[strip * n_track + jnp.minimum(track + 1, n_track - 1)]
+    base = strip * n_track if recv_ref.shape[0] > n_track else 0
+    ahead = recv_ref[base + jnp.minimum(track + 1, n_track - 1)]
     ahead = jnp.concatenate([ahead[h : h + 1] for h in range(width // 128)], axis=1)
     ahead = ahead + times_f32(spread(value_ref[pl.ds(count - 1, 1), :]), edge_map_ref[...])
     ahead = jnp.where(track < n_track - 1, ahead, 0.0)
@@ -331,9 +347,10 @@
         for i in range(send_ref.shape[0]):
             send_ref[i] = packed
         return
-    ends = chain_ends(state, maps_ref, last_two_ref, length)
+    ends, last = chain_ends(state, maps_ref, last_two_ref, length)
     begins_ref[...] = jnp.concatenate(ends, axis=0)
-    send_ends(ends[-1], edge[:1], dots, other_ref, pos_ref, n_track, send_ref)
+    carried = times_f32(spread(last), other_ref[...]) + times_f32(spread(ends[-3]), beyond_ref[...])
+    send_ends(ends[-1], carried, edge[:1], dots, pos_ref, n_track, send_ref)
 
 
 def last_update_kernel(cap, n_track, n_strip, *refs):
@@ -396,11 +413,11 @@
     )
     other = lax.ppermute(total, "track", swap)
     lower_flip, precond_flip = flip(lower, precond)
-    chip, send = call(
+    chip, beyond, send = call(
         functools.partial(pair_kernel, n_track),
-        [square, chunk],
-        [VMEM] * 3 + [SMEM] + [VMEM] * 6,
-        total, other, ends, pos, maps, lower, lower_flip, precond_flip, diag, coupling,
+        [square, square, (n_track,) + chunk[1:]],
+        [VMEM] * 4 + [SMEM] + [VMEM] * 6,
+        total, other, ends, last_two, pos, maps, lower, lower_flip, precond_flip, diag, coupling,
     )
     nearer = []
     for k in range(1, chips - 1, 2):
@@ -420,14 +437,12 @@
             else:
                 cross.append((d * n_strip + i, (d ^ 1) * n_strip + i))
     for step_number in range(ITERS):
-        recv = lax.all_to_all(send, ("strip", "track"), 0, 0)
+        recv = lax.all_to_all(send, ("strip", "track") if step_number else "track", 0, 0)
         if step_number == 0:
-            recv, diag, coupling, edge_map, *nearer = lax.optimization_barrier(
-                (recv, diag, coupling, edge_map, *nearer)
-            )
+            recv, edge_map, coupling, *nearer = lax.optimization_barrier((recv, edge_map, coupling, *nearer))
+            coupling_flip, = flip(coupling)
             edge_map = lax.ppermute(edge_map, "track", [((i + 1) % n_track, i) for i in range(n_track)])
             nearer += [lax.ppermute(part, "track", swap) for part in nearer]
-            diag_flip, coupling_flip = flip(diag, coupling)
         value, first, second, entry = call(
             functools.partial(direction_kernel, cap, n_track),
             [block, block, block, (1, width)],
@@ -440,13 +455,13 @@
             functools.partial(local_kernel, cap, step_number == 0),
             [block, (3,) + block, (1, width)],
             [VMEM] * 8 + [SMEM] * 2,
-            value, entry, recv, state, image, diag_flip, lower, lower_flip, links, pos,
+            value, entry, recv, state, image, diag, lower, lower_flip, links, pos,
         )
         args = (
             base, first, second, value, recv, state, image, alpha, edge_map, coupling_flip, lower, lower_flip,
-            precond_flip, maps, last_two, other, links, pos,
+            precond_flip, maps, last_two, beyond, other, links, pos,
         )
-        specs = [VMEM] * 16 + [SMEM] * 2
+        specs = [VMEM] * 17 + [SMEM] * 2
         if step_number < ITERS - 1:
             kernel = functools.partial(update_kernel, cap, n_track, n_strip, step_number == 0)
             image, local, begins, send = call(kernel, [block, block, chain, chunk], specs, *args)

time: 134 us -> 131 us (0.978)
  blocking collectives: 73.6 us -> 70.6 us
  starting transfers between devices: 5.79 us -> 8.13 us
  waiting for transfers between devices: 8.2 us -> 6.36 us
    all_to_all x7 -> x1, blocking collectives: 73.6 us -> 9.6 us  [body(): recv = lax.all_to_all(send, ('strip', 'track'), 0, 0)]
    all_to_all x0 -> x6, blocking collectives: none -> 61 us  [body(): lax.all_to_all(send, ('strip', 'track') if step_number else 'track', 0, 0)]
    ppermute x1, starting transfers between devices: 0.72 us -> 2.2 us  [body(): lax.ppermute(edge_map, 'track', [((i + 1) % n_track, i) for i in range(n_...]
  transfers between devices with their start and end apart: 16 -> 16, of which waited for: 7 -> 5; matrix products, arithmetic and copies ran while one was open for 0% -> 0% of each run, Pallas kernels for 11% -> 11%
where the time goes in v6:
time: 131 us; the launch traced here: 130 us
  blocking collectives  70.6 us (54%)
  Pallas kernels  43.6 us (33%)
  starting transfers between devices  8.13 us (6%)
  waiting for transfers between devices  6.36 us (5%)
  between operations  1.45 us (1%)
    all_to_all x6, blocking collectives, body(): lax.all_to_all(send, ('strip', 'track') if step_number else 'track', 0, 0)  61 us
    pallas_call x23, Pallas kernels, call(): pl.pallas_call(kernel, out_shape=[pltpu.VMEM(shape, dtype) if math.prod(s...  43.6 us
    all_to_all x1, blocking collectives, body(): recv = lax.all_to_all(send, ('strip', 'track'), 0, 0)  9.6 us
    ppermute x6, waiting for transfers between devices, body(): first = lax.ppermute(first, 'strip', pairs)  6.31 us
    ppermute x6, starting transfers between devices, body(): first = lax.ppermute(first, 'strip', pairs)  4.97 us
  transfers between devices with their start and end apart: 16, of which 5 were waited for; matrix products, arithmetic and copies ran while one was open for 0% of the time, Pallas kernels for 11%

profile of v6, /device:TPU:0, one launch (start us, length us, event | category | flops | bytes accessed | tf_op | source)
XLA Modules:
  0.0 130.3 jit_solution(8901979892245046617)
XLA Ops:
  1.3 0.1 pad_add_fusion.pos_ref.refs_2_.refs_18_
  1.4 6.8 %shard_map.86 = (f32[16,256,256]{2,1,0:T(8,128)S(1)}, f32[256,256]{1,0:T(8,128)S(1)}, f32[256,256]{1,0:T(8,128)S(1)}, f32[16,256]{1,0:T(8,128)S(1)}, f32[2,256]{...) custom-call(f32[16,256]{1,0:T(8,128)} %bitcast.9, ...), custom_call_target="tpu_custom_call" | custom-call | tf_op jit(solution)/shard_map/pallas_call | solution.py:372
  8.1 0.5 collective-permute-start
  8.6 1.1 shard_map.87
  9.8 0.0 collective-permute-done.other_ref.refs_16_
  9.8 0.9 shard_map.88
  10.7 0.4 collective-permute-start.1
  11.2 9.8 %all_to_all.35.recv_ref = f32[8,4,128]{2,1,0:T(4,128)S(1)} all-to-all(f32[8,4,128]{2,1,0:T(4,128)S(1)} %get-tuple-element.99), channel_id=1, replica_groups=mesh['track'=8,'strip'=4] {'track'}, dimensions={0} | all-to-all | bytes 32768 | tf_op jit(solution)/shard_map/all_to_all | solution.py:440
  21.0 0.0 collective-permute-done.1.refs_0_
  21.0 0.0 collective-permute-start.2
  21.0 2.2 %collective-permute-start.5 = (f32[256,256]{1,0:T(8,128)S(1)}, f32[256,256]{1,0:T(8,128)S(1)}, u32[]{:S(2)}, u32[]{:S(2)}) collective-permute-start(f32[256,256]{1,0:T(8,128)S(1)} %get-tuple-element.115), channel_id=1, source_target_pairs={{4,0},{8,4},{12,8},{16,12},{20,16},{24,20},{28,24},{0,28},{5,1},{9... | collective-permute-start | bytes 786440 | tf_op jit(solution)/shard_map/ppermute | solution.py:444
  23.2 0.0 collective-permute-done.2.refs_1_
  23.2 1.7 %shard_map.89 = (f32[16,256]{1,0:T(8,128)S(1)}, f32[16,256]{1,0:T(8,128)S(1)}, f32[16,256]{1,0:T(8,128)S(1)}, f32[1,256]{1,0:T(1,128)S(1)}) custom-call(f32[8,4,128]{2,1,0:T(4,128)S(1)} %all_to_all.35.recv_ref, f32[16,256]{1,0:T(8,128)S(1)} %get-tuple-element.103.local_ref, f32[4,256]{1,0:T(4,128)S(1)} %get-tuple-element.104.begins_ref, ...), custom_call_target="tpu_custom_call" | custom-call | tf_op jit(solution)/shard_map/pallas_call | solution.py:372
  24.9 1.6 %collective-permute-start.3 = (f32[16,256]{1,0:T(8,128)S(1)}, f32[16,256]{1,0:T(8,128)S(1)}, u32[]{:S(2)}, u32[]{:S(2)}) collective-permute-start(f32[16,256]{1,0:T(8,128)S(1)} %get-tuple-element.111), channel_id=1, source_target_pairs={{0,1},{1,0},{2,3},{3,2},{4,5},{5,4},{6,7},{7,6},{8,9},{9,8},{10,11... | collective-permute-start | bytes 49160 | tf_op jit(solution)/shard_map/ppermute | solution.py:452
  26.5 0.0 collective-permute-start.4
  26.5 0.6 shard_map.91.coupling_flip_ref.refs_9_
  27.1 0.1 copy-done
  27.3 1.9 %shard_map.90 = (f32[16,256]{1,0:T(8,128)S(1)}, f32[3,16,256]{2,1,0:T(8,128)S(1)}, f32[1,256]{1,0:T(1,128)S(1)}) custom-call(f32[16,256]{1,0:T(8,128)S(1)} %get-tuple-element.108.value_ref, f32[1,256]{1,0:T(1,128)S(1)} %get-tuple-element.109.entry_ref, f32[8,4,128]{2,1,0:T(4,128)S(1)} %all_to_all.35.recv_ref, f32[16,256]{1,0:T(8,128)S(1)} %bitcast.10, ...), custom_call_target="tpu_custom_call" | custom-call | tf_op jit(solution)/shard_map/pallas_call | solution.py:372
  29.1 0.0 collective-permute-done.5.edge_map_ref.refs_8_
  29.1 0.0 collective-permute-done.3.first_ref
  29.1 0.0 collective-permute-done.4.second_ref
  29.2 2.2 %shard_map.92 = (f32[16,256]{1,0:T(8,128)S(1)}, f32[16,256]{1,0:T(8,128)S(1)}, f32[4,256]{1,0:T(4,128)S(1)}, f32[32,4,128]{2,1,0:T(4,128)S(1)}) custom-call(f32[16,256]{1,0:T(8,128)S(1)} %get-tuple-element.110.base_ref, f32[16,256]{1,0:T(8,128)S(1)} %collective-permute-done.3.first_ref, f32[16,256]{1,0:T(8,128)S(1)} %collective-permute-done.4.second_ref, ...), custom_call_target="tpu_custom_call" | custom-call | tf_op jit(solution)/shard_map/pallas_call | solution.py:372
  31.4 12.2 %all_to_all.36.recv_ref = f32[32,4,128]{2,1,0:T(4,128)S(1)} all-to-all(f32[32,4,128]{2,1,0:T(4,128)S(1)} %get-tuple-element.117), channel_id=1, replica_groups=mesh['track'=8,'strip'=4] {'strip','track'}, dimensions={0} | all-to-all | bytes 131072 | tf_op jit(solution)/shard_map/all_to_all | solution.py:440
  43.5 1.7 %shard_map.93 = (f32[16,256]{1,0:T(8,128)S(1)}, f32[16,256]{1,0:T(8,128)S(1)}, f32[16,256]{1,0:T(8,128)S(1)}, f32[1,256]{1,0:T(1,128)S(1)}) custom-call(f32[32,4,128]{2,1,0:T(4,128)S(1)} %all_to_all.36.recv_ref, f32[16,256]{1,0:T(8,128)S(1)} %get-tuple-element.118.local_ref, f32[4,256]{1,0:T(4,128)S(1)} %get-tuple-element.119.begins_ref, ...), custom_call_target="tpu_custom_call" | custom-call | tf_op jit(solution)/shard_map/pallas_call | solution.py:372
  45.2 0.7 collective-permute-start.6
  45.9 0.0 collective-permute-start.7
  45.9 1.9 %shard_map.94 = (f32[16,256]{1,0:T(8,128)S(1)}, f32[3,16,256]{2,1,0:T(8,128)S(1)}, f32[1,256]{1,0:T(1,128)S(1)}) custom-call(f32[16,256]{1,0:T(8,128)S(1)} %get-tuple-element.120.value_ref, f32[1,256]{1,0:T(1,128)S(1)} %get-tuple-element.121.entry_ref, f32[32,4,128]{2,1,0:T(4,128)S(1)} %all_to_all.36.recv_ref, ...), custom_call_target="tpu_custom_call" | custom-call | tf_op jit(solution)/shard_map/pallas_call | solution.py:372
  47.8 1.3 collective-permute-done.6.first_ref
  49.0 0.0 collective-permute-done.7.second_ref
  49.0 2.2 %shard_map.95 = (f32[16,256]{1,0:T(8,128)S(1)}, f32[16,256]{1,0:T(8,128)S(1)}, f32[4,256]{1,0:T(4,128)S(1)}, f32[32,4,128]{2,1,0:T(4,128)S(1)}) custom-call(f32[16,256]{1,0:T(8,128)S(1)} %get-tuple-element.123.base_ref, f32[16,256]{1,0:T(8,128)S(1)} %collective-permute-done.6.first_ref, f32[16,256]{1,0:T(8,128)S(1)} %collective-permute-done.7.second_ref, ...), custom_call_target="tpu_custom_call" | custom-call | tf_op jit(solution)/shard_map/pallas_call | solution.py:372
  51.2 9.8 %all_to_all.37.recv_ref = f32[32,4,128]{2,1,0:T(4,128)S(1)} all-to-all(f32[32,4,128]{2,1,0:T(4,128)S(1)} %get-tuple-element.128), channel_id=1, replica_groups=mesh['track'=8,'strip'=4] {'strip','track'}, dimensions={0} | all-to-all | bytes 131072 | tf_op jit(solution)/shard_map/all_to_all | solution.py:440
  61.0 1.7 %shard_map.96 = (f32[16,256]{1,0:T(8,128)S(1)}, f32[16,256]{1,0:T(8,128)S(1)}, f32[16,256]{1,0:T(8,128)S(1)}, f32[1,256]{1,0:T(1,128)S(1)}) custom-call(f32[32,4,128]{2,1,0:T(4,128)S(1)} %all_to_all.37.recv_ref, f32[16,256]{1,0:T(8,128)S(1)} %get-tuple-element.129.local_ref, f32[4,256]{1,0:T(4,128)S(1)} %get-tuple-element.130.begins_ref, ...), custom_call_target="tpu_custom_call" | custom-call | tf_op jit(solution)/shard_map/pallas_call | solution.py:372
  62.7 0.7 collective-permute-start.8
  63.4 0.0 collective-permute-start.9
  63.4 1.9 %shard_map.97 = (f32[16,256]{1,0:T(8,128)S(1)}, f32[3,16,256]{2,1,0:T(8,128)S(1)}, f32[1,256]{1,0:T(1,128)S(1)}) custom-call(f32[16,256]{1,0:T(8,128)S(1)} %get-tuple-element.131.value_ref, f32[1,256]{1,0:T(1,128)S(1)} %get-tuple-element.132.entry_ref, f32[32,4,128]{2,1,0:T(4,128)S(1)} %all_to_all.37.recv_ref, ...), custom_call_target="tpu_custom_call" | custom-call | tf_op jit(solution)/shard_map/pallas_call | solution.py:372
  65.2 1.3 collective-permute-done.8.first_ref
  66.5 0.0 collective-permute-done.9.second_ref
  66.5 2.2 %shard_map.98 = (f32[16,256]{1,0:T(8,128)S(1)}, f32[16,256]{1,0:T(8,128)S(1)}, f32[4,256]{1,0:T(4,128)S(1)}, f32[32,4,128]{2,1,0:T(4,128)S(1)}) custom-call(f32[16,256]{1,0:T(8,128)S(1)} %get-tuple-element.134.base_ref, f32[16,256]{1,0:T(8,128)S(1)} %collective-permute-done.8.first_ref, f32[16,256]{1,0:T(8,128)S(1)} %collective-permute-done.9.second_ref, ...), custom_call_target="tpu_custom_call" | custom-call | tf_op jit(solution)/shard_map/pallas_call | solution.py:372
  68.7 9.8 %all_to_all.38.recv_ref = f32[32,4,128]{2,1,0:T(4,128)S(1)} all-to-all(f32[32,4,128]{2,1,0:T(4,128)S(1)} %get-tuple-element.139), channel_id=1, replica_groups=mesh['track'=8,'strip'=4] {'strip','track'}, dimensions={0} | all-to-all | bytes 131072 | tf_op jit(solution)/shard_map/all_to_all | solution.py:440
  78.4 1.7 %shard_map.99 = (f32[16,256]{1,0:T(8,128)S(1)}, f32[16,256]{1,0:T(8,128)S(1)}, f32[16,256]{1,0:T(8,128)S(1)}, f32[1,256]{1,0:T(1,128)S(1)}) custom-call(f32[32,4,128]{2,1,0:T(4,128)S(1)} %all_to_all.38.recv_ref, f32[16,256]{1,0:T(8,128)S(1)} %get-tuple-element.140.local_ref, f32[4,256]{1,0:T(4,128)S(1)} %get-tuple-element.141.begins_ref, ...), custom_call_target="tpu_custom_call" | custom-call | tf_op jit(solution)/shard_map/pallas_call | solution.py:372
  80.2 0.7 collective-permute-start.10
  80.8 0.0 collective-permute-start.11
  80.8 1.9 %shard_map.100 = (f32[16,256]{1,0:T(8,128)S(1)}, f32[3,16,256]{2,1,0:T(8,128)S(1)}, f32[1,256]{1,0:T(1,128)S(1)}) custom-call(f32[16,256]{1,0:T(8,128)S(1)} %get-tuple-element.142.value_ref, f32[1,256]{1,0:T(1,128)S(1)} %get-tuple-element.143.entry_ref, f32[32,4,128]{2,1,0:T(4,128)S(1)} %all_to_all.38.recv_ref, ...), custom_call_target="tpu_custom_call" | custom-call | tf_op jit(solution)/shard_map/pallas_call | solution.py:372
  82.7 1.3 collective-permute-done.10.first_ref
  84.0 0.0 collective-permute-done.11.second_ref
  84.0 2.2 %shard_map.101 = (f32[16,256]{1,0:T(8,128)S(1)}, f32[16,256]{1,0:T(8,128)S(1)}, f32[4,256]{1,0:T(4,128)S(1)}, f32[32,4,128]{2,1,0:T(4,128)S(1)}) custom-call(f32[16,256]{1,0:T(8,128)S(1)} %get-tuple-element.145.base_ref, f32[16,256]{1,0:T(8,128)S(1)} %collective-permute-done.10.first_ref, f32[16,256]{1,0:T(8,128)S(1)} %collective-permute-done.11.second_ref, ...), custom_call_target="tpu_custom_call" | custom-call | tf_op jit(solution)/shard_map/pallas_call | solution.py:372
  86.2 9.8 %all_to_all.39.recv_ref = f32[32,4,128]{2,1,0:T(4,128)S(1)} all-to-all(f32[32,4,128]{2,1,0:T(4,128)S(1)} %get-tuple-element.150), channel_id=1, replica_groups=mesh['track'=8,'strip'=4] {'strip','track'}, dimensions={0} | all-to-all | bytes 131072 | tf_op jit(solution)/shard_map/all_to_all | solution.py:440
  95.9 1.7 %shard_map.102 = (f32[16,256]{1,0:T(8,128)S(1)}, f32[16,256]{1,0:T(8,128)S(1)}, f32[16,256]{1,0:T(8,128)S(1)}, f32[1,256]{1,0:T(1,128)S(1)}) custom-call(f32[32,4,128]{2,1,0:T(4,128)S(1)} %all_to_all.39.recv_ref, f32[16,256]{1,0:T(8,128)S(1)} %get-tuple-element.151.local_ref, f32[4,256]{1,0:T(4,128)S(1)} %get-tuple-element.152.begins_ref, ...), custom_call_target="tpu_custom_call" | custom-call | tf_op jit(solution)/shard_map/pallas_call | solution.py:372
  97.6 0.7 collective-permute-start.12
  98.3 0.0 collective-permute-start.13
  98.3 1.9 %shard_map.103 = (f32[16,256]{1,0:T(8,128)S(1)}, f32[3,16,256]{2,1,0:T(8,128)S(1)}, f32[1,256]{1,0:T(1,128)S(1)}) custom-call(f32[16,256]{1,0:T(8,128)S(1)} %get-tuple-element.153.value_ref, f32[1,256]{1,0:T(1,128)S(1)} %get-tuple-element.154.entry_ref, f32[32,4,128]{2,1,0:T(4,128)S(1)} %all_to_all.39.recv_ref, ...), custom_call_target="tpu_custom_call" | custom-call | tf_op jit(solution)/shard_map/pallas_call | solution.py:372
  100.2 1.3 collective-permute-done.12.first_ref
  101.4 0.0 collective-permute-done.13.second_ref
  101.4 2.2 %shard_map.104 = (f32[16,256]{1,0:T(8,128)S(1)}, f32[16,256]{1,0:T(8,128)S(1)}, f32[4,256]{1,0:T(4,128)S(1)}, f32[32,4,128]{2,1,0:T(4,128)S(1)}) custom-call(f32[16,256]{1,0:T(8,128)S(1)} %get-tuple-element.156.base_ref, f32[16,256]{1,0:T(8,128)S(1)} %collective-permute-done.12.first_ref, f32[16,256]{1,0:T(8,128)S(1)} %collective-permute-done.13.second_ref, ...), custom_call_target="tpu_custom_call" | custom-call | tf_op jit(solution)/shard_map/pallas_call | solution.py:372
  103.6 9.8 %all_to_all.40.recv_ref.refs_4_ = f32[32,4,128]{2,1,0:T(4,128)S(1)} all-to-all(f32[32,4,128]{2,1,0:T(4,128)S(1)} %get-tuple-element.161), channel_id=1, replica_groups=mesh['track'=8,'strip'=4] {'strip','track'}, dimensions={0} | all-to-all | bytes 131072 | tf_op jit(solution)/shard_map/all_to_all | solution.py:440
  113.4 1.7 %shard_map.105 = (f32[16,256]{1,0:T(8,128)S(1)}, f32[16,256]{1,0:T(8,128)S(1)}, f32[16,256]{1,0:T(8,128)S(1)}, f32[1,256]{1,0:T(1,128)S(1)}) custom-call(f32[32,4,128]{2,1,0:T(4,128)S(1)} %all_to_all.40.recv_ref.refs_4_, f32[16,256]{1,0:T(8,128)S(1)} %get-tuple-element.162.local_ref, f32[4,256]{1,0:T(4,128)S(1)} %get-tuple-element.163.begins_ref, ...), custom_call_target="tpu_custom_call" | custom-call | tf_op jit(solution)/shard_map/pallas_call | solution.py:372
  115.1 0.7 collective-permute-start.14
  115.8 0.0 collective-permute-start.15
  115.8 1.9 %shard_map.106 = (f32[16,256]{1,0:T(8,128)S(1)}, f32[3,16,256]{2,1,0:T(8,128)S(1)}, f32[1,256]{1,0:T(1,128)S(1)}) custom-call(f32[16,256]{1,0:T(8,128)S(1)} %get-tuple-element.164.value_ref.refs_3_, f32[1,256]{1,0:T(1,128)S(1)} %get-tuple-element.165.entry_ref, f32[32,4,128]{2,1,0:T(4,128)S(1)} %all_to_all.40.recv_ref.refs_4_, ...), custom_call_target="tpu_custom_call" | custom-call | tf_op jit(solution)/shard_map/pallas_call | solution.py:372
  117.6 1.3 collective-permute-done.14.refs_1_
  118.9 0.0 collective-permute-done.15.refs_2_
  118.9 1.1 shard_map.107
  120.0 9.6 %all_to_all.41.recv_ref = f32[32,2,128]{2,1,0:T(2,128)S(1)} all-to-all(f32[32,2,128]{2,1,0:T(2,128)S(1)} %get-tuple-element.172), channel_id=1, replica_groups=mesh['track'=8,'strip'=4] {'strip','track'}, dimensions={0} | all-to-all | bytes 65536 | tf_op jit(solution)/shard_map/all_to_all | solution.py:471
  129.6 0.8 shard_map.108
  (3 shorter events, 0.0 us)
Async XLA Ops:
  8.1 1.7 %collective-permute-start = (f32[256,256]{1,0:T(8,128)S(1)}, f32[256,256]{1,0:T(8,128)S(1)}, u32[]{:S(2)}, u32[]{:S(2)}) collective-permute-start(f32[256,256]{1,0:T(8,128)S(1)} %get-tuple-element.89.total_ref), channel_id=1, source_target_pairs={{0,4},{4,0},{8,12},{12,8},{16,20},{20,16},{24,28},{28,24},{1,5},{5... | collective-permute-start | bytes 786440 | tf_op jit(solution)/shard_map/ppermute | solution.py:414
  10.7 10.2 %collective-permute-start.1 = (f32[256,256]{1,0:T(8,128)S(1)}, f32[256,256]{1,0:T(8,128)S(1)}, u32[]{:S(2)}, u32[]{:S(2)}) collective-permute-start(f32[256,256]{1,0:T(8,128)S(1)} %get-tuple-element.101), channel_id=1, source_target_pairs={{0,4},{4,0},{8,16},{12,28},{16,24},{20,12},{24,8},{28,20},{1,5},{5... | collective-permute-start | bytes 786440 | tf_op jit(solution)/shard_map/ppermute | solution.py:427
  21.0 2.2 %collective-permute-start.2 = (f32[256,256]{1,0:T(8,128)S(1)}, f32[256,256]{1,0:T(8,128)S(1)}, u32[]{:S(2)}, u32[]{:S(2)}) collective-permute-start(f32[256,256]{1,0:T(8,128)S(1)} %collective-permute-done.1.refs_0_), channel_id=1, source_target_pairs={{0,4},{4,0},{8,12},{12,8},{16,20},{20,16},{24,28},{28,24},{1,5},{5... | collective-permute-start | bytes 786440 | tf_op jit(solution)/shard_map/ppermute | solution.py:445
  21.0 8.1 %collective-permute-start.5 = (f32[256,256]{1,0:T(8,128)S(1)}, f32[256,256]{1,0:T(8,128)S(1)}, u32[]{:S(2)}, u32[]{:S(2)}) collective-permute-start(f32[256,256]{1,0:T(8,128)S(1)} %get-tuple-element.115), channel_id=1, source_target_pairs={{4,0},{8,4},{12,8},{16,12},{20,16},{24,20},{28,24},{0,28},{5,1},{9... | collective-permute-start | bytes 786440 | tf_op jit(solution)/shard_map/ppermute | solution.py:444
  24.9 4.2 %collective-permute-start.3 = (f32[16,256]{1,0:T(8,128)S(1)}, f32[16,256]{1,0:T(8,128)S(1)}, u32[]{:S(2)}, u32[]{:S(2)}) collective-permute-start(f32[16,256]{1,0:T(8,128)S(1)} %get-tuple-element.111), channel_id=1, source_target_pairs={{0,1},{1,0},{2,3},{3,2},{4,5},{5,4},{6,7},{7,6},{8,9},{9,8},{10,11... | collective-permute-start | bytes 49160 | tf_op jit(solution)/shard_map/ppermute | solution.py:452
  26.5 0.7 copy-start
  26.5 0.7 copy-start.1
  26.5 2.6 %collective-permute-start.4 = (f32[16,256]{1,0:T(8,128)S(1)}, f32[16,256]{1,0:T(8,128)S(1)}, u32[]{:S(2)}, u32[]{:S(2)}) collective-permute-start(f32[16,256]{1,0:T(8,128)S(1)} %get-tuple-element.112), channel_id=1, source_target_pairs={{0,4},{1,2},{2,1},{3,7},{4,0},{5,6},{6,5},{7,3},{8,12},{9,10},{10,... | collective-permute-start | bytes 49160 | tf_op jit(solution)/shard_map/ppermute | solution.py:453
  45.2 3.8 %collective-permute-start.6 = (f32[16,256]{1,0:T(8,128)S(1)}, f32[16,256]{1,0:T(8,128)S(1)}, u32[]{:S(2)}, u32[]{:S(2)}) collective-permute-start(f32[16,256]{1,0:T(8,128)S(1)} %get-tuple-element.124), channel_id=1, source_target_pairs={{0,1},{1,0},{2,3},{3,2},{4,5},{5,4},{6,7},{7,6},{8,9},{9,8},{10,11... | collective-permute-start | bytes 49160 | tf_op jit(solution)/shard_map/ppermute | solution.py:452
  45.9 3.1 %collective-permute-start.7 = (f32[16,256]{1,0:T(8,128)S(1)}, f32[16,256]{1,0:T(8,128)S(1)}, u32[]{:S(2)}, u32[]{:S(2)}) collective-permute-start(f32[16,256]{1,0:T(8,128)S(1)} %get-tuple-element.125), channel_id=1, source_target_pairs={{0,4},{1,2},{2,1},{3,7},{4,0},{5,6},{6,5},{7,3},{8,12},{9,10},{10,... | collective-permute-start | bytes 49160 | tf_op jit(solution)/shard_map/ppermute | solution.py:453
  62.7 3.8 %collective-permute-start.8 = (f32[16,256]{1,0:T(8,128)S(1)}, f32[16,256]{1,0:T(8,128)S(1)}, u32[]{:S(2)}, u32[]{:S(2)}) collective-permute-start(f32[16,256]{1,0:T(8,128)S(1)} %get-tuple-element.135), channel_id=1, source_target_pairs={{0,1},{1,0},{2,3},{3,2},{4,5},{5,4},{6,7},{7,6},{8,9},{9,8},{10,11... | collective-permute-start | bytes 49160 | tf_op jit(solution)/shard_map/ppermute | solution.py:452
  63.4 3.1 %collective-permute-start.9 = (f32[16,256]{1,0:T(8,128)S(1)}, f32[16,256]{1,0:T(8,128)S(1)}, u32[]{:S(2)}, u32[]{:S(2)}) collective-permute-start(f32[16,256]{1,0:T(8,128)S(1)} %get-tuple-element.136), channel_id=1, source_target_pairs={{0,4},{1,2},{2,1},{3,7},{4,0},{5,6},{6,5},{7,3},{8,12},{9,10},{10,... | collective-permute-start | bytes 49160 | tf_op jit(solution)/shard_map/ppermute | solution.py:453
  80.2 3.8 %collective-permute-start.10 = (f32[16,256]{1,0:T(8,128)S(1)}, f32[16,256]{1,0:T(8,128)S(1)}, u32[]{:S(2)}, u32[]{:S(2)}) collective-permute-start(f32[16,256]{1,0:T(8,128)S(1)} %get-tuple-element.146), channel_id=1, source_target_pairs={{0,1},{1,0},{2,3},{3,2},{4,5},{5,4},{6,7},{7,6},{8,9},{9,8},{10,11... | collective-permute-start | bytes 49160 | tf_op jit(solution)/shard_map/ppermute | solution.py:452
  80.8 3.1 %collective-permute-start.11 = (f32[16,256]{1,0:T(8,128)S(1)}, f32[16,256]{1,0:T(8,128)S(1)}, u32[]{:S(2)}, u32[]{:S(2)}) collective-permute-start(f32[16,256]{1,0:T(8,128)S(1)} %get-tuple-element.147), channel_id=1, source_target_pairs={{0,4},{1,2},{2,1},{3,7},{4,0},{5,6},{6,5},{7,3},{8,12},{9,10},{10,... | collective-permute-start | bytes 49160 | tf_op jit(solution)/shard_map/ppermute | solution.py:453
  97.6 3.8 %collective-permute-start.12 = (f32[16,256]{1,0:T(8,128)S(1)}, f32[16,256]{1,0:T(8,128)S(1)}, u32[]{:S(2)}, u32[]{:S(2)}) collective-permute-start(f32[16,256]{1,0:T(8,128)S(1)} %get-tuple-element.157), channel_id=1, source_target_pairs={{0,1},{1,0},{2,3},{3,2},{4,5},{5,4},{6,7},{7,6},{8,9},{9,8},{10,11... | collective-permute-start | bytes 49160 | tf_op jit(solution)/shard_map/ppermute | solution.py:452
  98.3 3.1 %collective-permute-start.13 = (f32[16,256]{1,0:T(8,128)S(1)}, f32[16,256]{1,0:T(8,128)S(1)}, u32[]{:S(2)}, u32[]{:S(2)}) collective-permute-start(f32[16,256]{1,0:T(8,128)S(1)} %get-tuple-element.158), channel_id=1, source_target_pairs={{0,4},{1,2},{2,1},{3,7},{4,0},{5,6},{6,5},{7,3},{8,12},{9,10},{10,... | collective-permute-start | bytes 49160 | tf_op jit(solution)/shard_map/ppermute | solution.py:453
  115.1 3.8 %collective-permute-start.14 = (f32[16,256]{1,0:T(8,128)S(1)}, f32[16,256]{1,0:T(8,128)S(1)}, u32[]{:S(2)}, u32[]{:S(2)}) collective-permute-start(f32[16,256]{1,0:T(8,128)S(1)} %get-tuple-element.168), channel_id=1, source_target_pairs={{0,1},{1,0},{2,3},{3,2},{4,5},{5,4},{6,7},{7,6},{8,9},{9,8},{10,11... | collective-permute-start | bytes 49160 | tf_op jit(solution)/shard_map/ppermute | solution.py:452
  115.8 3.1 %collective-permute-start.15 = (f32[16,256]{1,0:T(8,128)S(1)}, f32[16,256]{1,0:T(8,128)S(1)}, u32[]{:S(2)}, u32[]{:S(2)}) collective-permute-start(f32[16,256]{1,0:T(8,128)S(1)} %get-tuple-element.169), channel_id=1, source_target_pairs={{0,4},{1,2},{2,1},{3,7},{4,0},{5,6},{6,5},{7,3},{8,12},{9,10},{10,... | collective-permute-start | bytes 49160 | tf_op jit(solution)/shard_map/ppermute | solution.py:453

commit v7 on v6

--- a/solution.py
+++ b/solution.py
@@ -208,7 +208,25 @@
     beyond_ref[...] = product(last_two_ref[...], other_ref[...])
 
 
-def direction_kernel(cap, n_track, recv_ref, local_ref, begins_ref, maps_ref, through_ref, other_ref, coupling_ref, *refs):
+def chip_map(chip_refs, pos_ref, i):
+    mine, paired = chip_refs[i // 2][...], chip_refs[i // 2 + len(chip_refs) // 2][...]
+    return jnp.where(pos_ref[0] % 2 == i % 2, mine, paired)
+
+
+def fold_kernel(cap, chips, coupling_ref, other_ref, pos_ref, *refs):
+    chip_refs, (flip_ref, *out_refs) = refs[: chips - 2], refs[chips - 2 :]
+    flip_kernel(cap, coupling_ref, flip_ref)
+    value = None
+    for i, out_ref in enumerate(out_refs):
+        nearer = chip_map(chip_refs, pos_ref, i)
+        if value is None:
+            value = jnp.where(pos_ref[0] % 2 == 1, product(nearer, other_ref[...]), nearer)
+        else:
+            value = product(nearer, value)
+        out_ref[...] = value
+
+
+def direction_kernel(cap, n_track, folded, recv_ref, local_ref, begins_ref, maps_ref, through_ref, other_ref, coupling_ref, *refs):
     chip_refs, (pos_ref, value_ref, first_ref, second_ref, entry_ref) = refs[:-5], refs[-5:]
     track, strip = pos_ref[0], pos_ref[1]
     width = local_ref.shape[1]
@@ -226,16 +244,19 @@
         valid = chip - i >= 0
         return chunk(2 * (chip - i), valid) + chunk(2 * (chip - i) + 1, valid)
 
-    def chip_map(i):
-        mine, paired = chip_refs[i // 2][...], chip_refs[i // 2 + len(chip_refs) // 2][...]
-        return jnp.where(track % 2 == i % 2, mine, paired)
-
     furthest = n_track // 2 - 1
-    entry = chip_end(furthest)
-    for i in range(furthest - 1, 0, -1):
-        entry = chip_end(i) + times_f32(spread(entry), chip_map(i - 1))
-    inside = chunk(track - 1, track > 0) + times_f32(spread(entry), other_ref[...])
-    entry = jnp.where(track % 2 == 1, inside, entry)
+    if folded:
+        entry = chip_end(1)
+        inside = chunk(track - 1, track > 0) + times_f32(spread(entry), other_ref[...])
+        entry = jnp.where(track % 2 == 1, inside, entry)
+        for i in range(2, furthest + 1):
+            entry = entry + times_f32(spread(chip_end(i)), chip_refs[i - 2][...])
+    else:
+        entry = chip_end(furthest)
+        for i in range(furthest - 1, 0, -1):
+            entry = chip_end(i) + times_f32(spread(entry), chip_map(chip_refs, pos_ref, i - 1))
+        inside = chunk(track - 1, track > 0) + times_f32(spread(entry), other_ref[...])
+        entry = jnp.where(track % 2 == 1, inside, entry)
     entry_ref[...] = entry
     columns = [spread(entry)]
     for q in range(1, CHAINS):
@@ -440,15 +461,21 @@
         recv = lax.all_to_all(send, ("strip", "track") if step_number else "track", 0, 0)
         if step_number == 0:
             recv, edge_map, coupling, *nearer = lax.optimization_barrier((recv, edge_map, coupling, *nearer))
-            coupling_flip, = flip(coupling)
             edge_map = lax.ppermute(edge_map, "track", [((i + 1) % n_track, i) for i in range(n_track)])
             nearer += [lax.ppermute(part, "track", swap) for part in nearer]
         value, first, second, entry = call(
-            functools.partial(direction_kernel, cap, n_track),
+            functools.partial(direction_kernel, cap, n_track, step_number > 0),
             [block, block, block, (1, width)],
             [VMEM] * (7 + len(nearer)) + [SMEM],
             recv, local, begins, maps, through, other, coupling, *nearer, pos,
         )
+        if step_number == 0:
+            coupling_flip, *nearer = call(
+                functools.partial(fold_kernel, cap, chips),
+                [(stack, jnp.bfloat16)] + [square] * (chips - 2),
+                [VMEM] * 2 + [SMEM] + [VMEM] * len(nearer),
+                coupling, other, pos, *nearer,
+            )
         first = lax.ppermute(first, "strip", pairs)
         second = lax.ppermute(second, ("track", "strip"), cross)
         base, state, alpha = call(

time: 131 us -> 130 us (level)
  transfers between devices with their start and end apart: 16 -> 16, of which waited for: 5 -> 5; matrix products, arithmetic and copies ran while one was open for 0% -> 0% of each run, Pallas kernels for 11% -> 12%
where the time goes in v7:
time: 130 us; the launch traced here: 129 us
  blocking collectives  70 us (54%)
  Pallas kernels  43.2 us (33%)
  starting transfers between devices  8.12 us (6%)
  waiting for transfers between devices  6.36 us (5%)
  between operations  1.44 us (1%)
    all_to_all x6, blocking collectives, body(): lax.all_to_all(send, ('strip', 'track') if step_number else 'track', 0, 0)  60.5 us
    pallas_call x23, Pallas kernels, call(): pl.pallas_call(kernel, out_shape=[pltpu.VMEM(shape, dtype) if math.prod(s...  43.2 us
    all_to_all x1, blocking collectives, body(): recv = lax.all_to_all(send, ('strip', 'track'), 0, 0)  9.6 us
    ppermute x6, waiting for transfers between devices, body(): first = lax.ppermute(first, 'strip', pairs)  6.31 us
    ppermute x6, starting transfers between devices, body(): first = lax.ppermute(first, 'strip', pairs)  4.96 us
  transfers between devices with their start and end apart: 16, of which 5 were waited for; matrix products, arithmetic and copies ran while one was open for 0% of the time, Pallas kernels for 12%

profile of v7, /device:TPU:0, one launch (start us, length us, event | category | flops | bytes accessed | tf_op | source)
XLA Modules:
  0.0 129.3 jit_solution(2116031169406945913)
XLA Ops:
  1.3 0.1 pad_add_fusion.pos_ref.refs_2_.refs_18_
  1.4 6.8 %shard_map.86 = (f32[16,256,256]{2,1,0:T(8,128)S(1)}, f32[256,256]{1,0:T(8,128)S(1)}, f32[256,256]{1,0:T(8,128)S(1)}, f32[16,256]{1,0:T(8,128)S(1)}, f32[2,256]{...) custom-call(f32[16,256]{1,0:T(8,128)} %bitcast.9, ...), custom_call_target="tpu_custom_call" | custom-call | tf_op jit(solution)/shard_map/pallas_call | solution.py:393
  8.1 0.5 collective-permute-start
  8.6 1.1 shard_map.87
  9.8 0.0 collective-permute-done.other_ref.refs_16_
  9.8 0.9 shard_map.88
  10.7 0.4 collective-permute-start.1
  11.2 9.8 %all_to_all.35.recv_ref = f32[8,4,128]{2,1,0:T(4,128)S(1)} all-to-all(f32[8,4,128]{2,1,0:T(4,128)S(1)} %get-tuple-element.102), channel_id=1, replica_groups=mesh['track'=8,'strip'=4] {'track'}, dimensions={0} | all-to-all | bytes 32768 | tf_op jit(solution)/shard_map/all_to_all | solution.py:461
  21.0 0.0 collective-permute-done.1.refs_0_
  21.0 0.0 collective-permute-start.2
  21.0 2.2 %collective-permute-start.5 = (f32[256,256]{1,0:T(8,128)S(1)}, f32[256,256]{1,0:T(8,128)S(1)}, u32[]{:S(2)}, u32[]{:S(2)}) collective-permute-start(f32[256,256]{1,0:T(8,128)S(1)} %get-tuple-element.118), channel_id=1, source_target_pairs={{4,0},{8,4},{12,8},{16,12},{20,16},{24,20},{28,24},{0,28},{5,1},{9... | collective-permute-start | bytes 786440 | tf_op jit(solution)/shard_map/ppermute | solution.py:464
  23.2 0.0 collective-permute-done.2.refs_1_
  23.2 1.7 %shard_map.89 = (f32[16,256]{1,0:T(8,128)S(1)}, f32[16,256]{1,0:T(8,128)S(1)}, f32[16,256]{1,0:T(8,128)S(1)}, f32[1,256]{1,0:T(1,128)S(1)}) custom-call(f32[8,4,128]{2,1,0:T(4,128)S(1)} %all_to_all.35.recv_ref, f32[16,256]{1,0:T(8,128)S(1)} %get-tuple-element.106.local_ref, f32[4,256]{1,0:T(4,128)S(1)} %get-tuple-element.107.begins_ref, ...), custom_call_target="tpu_custom_call" | custom-call | tf_op jit(solution)/shard_map/pallas_call | solution.py:393
  24.9 1.6 %collective-permute-start.3 = (f32[16,256]{1,0:T(8,128)S(1)}, f32[16,256]{1,0:T(8,128)S(1)}, u32[]{:S(2)}, u32[]{:S(2)}) collective-permute-start(f32[16,256]{1,0:T(8,128)S(1)} %get-tuple-element.114), channel_id=1, source_target_pairs={{0,1},{1,0},{2,3},{3,2},{4,5},{5,4},{6,7},{7,6},{8,9},{9,8},{10,11... | collective-permute-start | bytes 49160 | tf_op jit(solution)/shard_map/ppermute | solution.py:479
  26.5 0.0 collective-permute-start.4
  26.5 0.0 copy-done.1
  26.5 1.9 %shard_map.90 = (f32[16,256]{1,0:T(8,128)S(1)}, f32[3,16,256]{2,1,0:T(8,128)S(1)}, f32[1,256]{1,0:T(1,128)S(1)}) custom-call(f32[16,256]{1,0:T(8,128)S(1)} %get-tuple-element.111.value_ref, f32[1,256]{1,0:T(1,128)S(1)} %get-tuple-element.112.entry_ref, f32[8,4,128]{2,1,0:T(4,128)S(1)} %all_to_all.35.recv_ref, f32[16,256]{1,0:T(8,128)S(1)} %bitcast.10, ...), custom_call_target="tpu_custom_call" | custom-call | tf_op jit(solution)/shard_map/pallas_call | solution.py:393
  28.4 1.3 shard_map.91
  29.7 0.0 collective-permute-done.5.edge_map_ref.refs_8_
  29.7 0.0 collective-permute-done.3.first_ref
  29.7 0.0 collective-permute-done.4.second_ref
  29.7 2.2 %shard_map.92 = (f32[16,256]{1,0:T(8,128)S(1)}, f32[16,256]{1,0:T(8,128)S(1)}, f32[4,256]{1,0:T(4,128)S(1)}, f32[32,4,128]{2,1,0:T(4,128)S(1)}) custom-call(f32[16,256]{1,0:T(8,128)S(1)} %get-tuple-element.113.base_ref, f32[16,256]{1,0:T(8,128)S(1)} %collective-permute-done.3.first_ref, f32[16,256]{1,0:T(8,128)S(1)} %collective-permute-done.4.second_ref, ...), custom_call_target="tpu_custom_call" | custom-call | tf_op jit(solution)/shard_map/pallas_call | solution.py:393
  31.9 11.6 %all_to_all.36.recv_ref = f32[32,4,128]{2,1,0:T(4,128)S(1)} all-to-all(f32[32,4,128]{2,1,0:T(4,128)S(1)} %get-tuple-element.121), channel_id=1, replica_groups=mesh['track'=8,'strip'=4] {'strip','track'}, dimensions={0} | all-to-all | bytes 131072 | tf_op jit(solution)/shard_map/all_to_all | solution.py:461
  43.5 1.5 %shard_map.93 = (f32[16,256]{1,0:T(8,128)S(1)}, f32[16,256]{1,0:T(8,128)S(1)}, f32[16,256]{1,0:T(8,128)S(1)}, f32[1,256]{1,0:T(1,128)S(1)}) custom-call(f32[32,4,128]{2,1,0:T(4,128)S(1)} %all_to_all.36.recv_ref, f32[16,256]{1,0:T(8,128)S(1)} %get-tuple-element.122.local_ref, f32[4,256]{1,0:T(4,128)S(1)} %get-tuple-element.123.begins_ref, ...), custom_call_target="tpu_custom_call" | custom-call | tf_op jit(solution)/shard_map/pallas_call | solution.py:393
  45.0 0.7 collective-permute-start.6
  45.7 0.0 collective-permute-start.7
  45.7 1.9 %shard_map.94 = (f32[16,256]{1,0:T(8,128)S(1)}, f32[3,16,256]{2,1,0:T(8,128)S(1)}, f32[1,256]{1,0:T(1,128)S(1)}) custom-call(f32[16,256]{1,0:T(8,128)S(1)} %get-tuple-element.126.value_ref, f32[1,256]{1,0:T(1,128)S(1)} %get-tuple-element.127.entry_ref, f32[32,4,128]{2,1,0:T(4,128)S(1)} %all_to_all.36.recv_ref, ...), custom_call_target="tpu_custom_call" | custom-call | tf_op jit(solution)/shard_map/pallas_call | solution.py:393
  47.6 1.3 collective-permute-done.6.first_ref
  48.8 0.0 collective-permute-done.7.second_ref
  48.8 2.2 %shard_map.95 = (f32[16,256]{1,0:T(8,128)S(1)}, f32[16,256]{1,0:T(8,128)S(1)}, f32[4,256]{1,0:T(4,128)S(1)}, f32[32,4,128]{2,1,0:T(4,128)S(1)}) custom-call(f32[16,256]{1,0:T(8,128)S(1)} %get-tuple-element.129.base_ref, f32[16,256]{1,0:T(8,128)S(1)} %collective-permute-done.6.first_ref, f32[16,256]{1,0:T(8,128)S(1)} %collective-permute-done.7.second_ref, ...), custom_call_target="tpu_custom_call" | custom-call | tf_op jit(solution)/shard_map/pallas_call | solution.py:393
  51.0 9.8 %all_to_all.37.recv_ref = f32[32,4,128]{2,1,0:T(4,128)S(1)} all-to-all(f32[32,4,128]{2,1,0:T(4,128)S(1)} %get-tuple-element.134), channel_id=1, replica_groups=mesh['track'=8,'strip'=4] {'strip','track'}, dimensions={0} | all-to-all | bytes 131072 | tf_op jit(solution)/shard_map/all_to_all | solution.py:461
  60.8 1.5 %shard_map.96 = (f32[16,256]{1,0:T(8,128)S(1)}, f32[16,256]{1,0:T(8,128)S(1)}, f32[16,256]{1,0:T(8,128)S(1)}, f32[1,256]{1,0:T(1,128)S(1)}) custom-call(f32[32,4,128]{2,1,0:T(4,128)S(1)} %all_to_all.37.recv_ref, f32[16,256]{1,0:T(8,128)S(1)} %get-tuple-element.135.local_ref, f32[4,256]{1,0:T(4,128)S(1)} %get-tuple-element.136.begins_ref, ...), custom_call_target="tpu_custom_call" | custom-call | tf_op jit(solution)/shard_map/pallas_call | solution.py:393
  62.3 0.7 collective-permute-start.8
  62.9 0.0 collective-permute-start.9
  62.9 1.9 %shard_map.97 = (f32[16,256]{1,0:T(8,128)S(1)}, f32[3,16,256]{2,1,0:T(8,128)S(1)}, f32[1,256]{1,0:T(1,128)S(1)}) custom-call(f32[16,256]{1,0:T(8,128)S(1)} %get-tuple-element.137.value_ref, f32[1,256]{1,0:T(1,128)S(1)} %get-tuple-element.138.entry_ref, f32[32,4,128]{2,1,0:T(4,128)S(1)} %all_to_all.37.recv_ref, ...), custom_call_target="tpu_custom_call" | custom-call | tf_op jit(solution)/shard_map/pallas_call | solution.py:393
  64.8 1.3 collective-permute-done.8.first_ref
  66.1 0.0 collective-permute-done.9.second_ref
  66.1 2.2 %shard_map.98 = (f32[16,256]{1,0:T(8,128)S(1)}, f32[16,256]{1,0:T(8,128)S(1)}, f32[4,256]{1,0:T(4,128)S(1)}, f32[32,4,128]{2,1,0:T(4,128)S(1)}) custom-call(f32[16,256]{1,0:T(8,128)S(1)} %get-tuple-element.140.base_ref, f32[16,256]{1,0:T(8,128)S(1)} %collective-permute-done.8.first_ref, f32[16,256]{1,0:T(8,128)S(1)} %collective-permute-done.9.second_ref, ...), custom_call_target="tpu_custom_call" | custom-call | tf_op jit(solution)/shard_map/pallas_call | solution.py:393
  68.3 9.8 %all_to_all.38.recv_ref = f32[32,4,128]{2,1,0:T(4,128)S(1)} all-to-all(f32[32,4,128]{2,1,0:T(4,128)S(1)} %get-tuple-element.145), channel_id=1, replica_groups=mesh['track'=8,'strip'=4] {'strip','track'}, dimensions={0} | all-to-all | bytes 131072 | tf_op jit(solution)/shard_map/all_to_all | solution.py:461
  78.0 1.5 %shard_map.99 = (f32[16,256]{1,0:T(8,128)S(1)}, f32[16,256]{1,0:T(8,128)S(1)}, f32[16,256]{1,0:T(8,128)S(1)}, f32[1,256]{1,0:T(1,128)S(1)}) custom-call(f32[32,4,128]{2,1,0:T(4,128)S(1)} %all_to_all.38.recv_ref, f32[16,256]{1,0:T(8,128)S(1)} %get-tuple-element.146.local_ref, f32[4,256]{1,0:T(4,128)S(1)} %get-tuple-element.147.begins_ref, ...), custom_call_target="tpu_custom_call" | custom-call | tf_op jit(solution)/shard_map/pallas_call | solution.py:393
  79.5 0.7 collective-permute-start.10
  80.2 0.0 collective-permute-start.11
  80.2 1.9 %shard_map.100 = (f32[16,256]{1,0:T(8,128)S(1)}, f32[3,16,256]{2,1,0:T(8,128)S(1)}, f32[1,256]{1,0:T(1,128)S(1)}) custom-call(f32[16,256]{1,0:T(8,128)S(1)} %get-tuple-element.148.value_ref, f32[1,256]{1,0:T(1,128)S(1)} %get-tuple-element.149.entry_ref, f32[32,4,128]{2,1,0:T(4,128)S(1)} %all_to_all.38.recv_ref, ...), custom_call_target="tpu_custom_call" | custom-call | tf_op jit(solution)/shard_map/pallas_call | solution.py:393
  82.1 1.3 collective-permute-done.10.first_ref
  83.3 0.0 collective-permute-done.11.second_ref
  83.3 2.2 %shard_map.101 = (f32[16,256]{1,0:T(8,128)S(1)}, f32[16,256]{1,0:T(8,128)S(1)}, f32[4,256]{1,0:T(4,128)S(1)}, f32[32,4,128]{2,1,0:T(4,128)S(1)}) custom-call(f32[16,256]{1,0:T(8,128)S(1)} %get-tuple-element.151.base_ref, f32[16,256]{1,0:T(8,128)S(1)} %collective-permute-done.10.first_ref, f32[16,256]{1,0:T(8,128)S(1)} %collective-permute-done.11.second_ref, ...), custom_call_target="tpu_custom_call" | custom-call | tf_op jit(solution)/shard_map/pallas_call | solution.py:393
  85.5 9.8 %all_to_all.39.recv_ref = f32[32,4,128]{2,1,0:T(4,128)S(1)} all-to-all(f32[32,4,128]{2,1,0:T(4,128)S(1)} %get-tuple-element.156), channel_id=1, replica_groups=mesh['track'=8,'strip'=4] {'strip','track'}, dimensions={0} | all-to-all | bytes 131072 | tf_op jit(solution)/shard_map/all_to_all | solution.py:461
  95.3 1.5 %shard_map.102 = (f32[16,256]{1,0:T(8,128)S(1)}, f32[16,256]{1,0:T(8,128)S(1)}, f32[16,256]{1,0:T(8,128)S(1)}, f32[1,256]{1,0:T(1,128)S(1)}) custom-call(f32[32,4,128]{2,1,0:T(4,128)S(1)} %all_to_all.39.recv_ref, f32[16,256]{1,0:T(8,128)S(1)} %get-tuple-element.157.local_ref, f32[4,256]{1,0:T(4,128)S(1)} %get-tuple-element.158.begins_ref, ...), custom_call_target="tpu_custom_call" | custom-call | tf_op jit(solution)/shard_map/pallas_call | solution.py:393
  96.8 0.7 collective-permute-start.12
  97.5 0.0 collective-permute-start.13
  97.5 1.9 %shard_map.103 = (f32[16,256]{1,0:T(8,128)S(1)}, f32[3,16,256]{2,1,0:T(8,128)S(1)}, f32[1,256]{1,0:T(1,128)S(1)}) custom-call(f32[16,256]{1,0:T(8,128)S(1)} %get-tuple-element.159.value_ref, f32[1,256]{1,0:T(1,128)S(1)} %get-tuple-element.160.entry_ref, f32[32,4,128]{2,1,0:T(4,128)S(1)} %all_to_all.39.recv_ref, ...), custom_call_target="tpu_custom_call" | custom-call | tf_op jit(solution)/shard_map/pallas_call | solution.py:393
  99.3 1.3 collective-permute-done.12.first_ref
  100.6 0.0 collective-permute-done.13.second_ref
  100.6 2.2 %shard_map.104 = (f32[16,256]{1,0:T(8,128)S(1)}, f32[16,256]{1,0:T(8,128)S(1)}, f32[4,256]{1,0:T(4,128)S(1)}, f32[32,4,128]{2,1,0:T(4,128)S(1)}) custom-call(f32[16,256]{1,0:T(8,128)S(1)} %get-tuple-element.162.base_ref, f32[16,256]{1,0:T(8,128)S(1)} %collective-permute-done.12.first_ref, f32[16,256]{1,0:T(8,128)S(1)} %collective-permute-done.13.second_ref, ...), custom_call_target="tpu_custom_call" | custom-call | tf_op jit(solution)/shard_map/pallas_call | solution.py:393
  102.8 9.8 %all_to_all.40.recv_ref.refs_4_ = f32[32,4,128]{2,1,0:T(4,128)S(1)} all-to-all(f32[32,4,128]{2,1,0:T(4,128)S(1)} %get-tuple-element.167), channel_id=1, replica_groups=mesh['track'=8,'strip'=4] {'strip','track'}, dimensions={0} | all-to-all | bytes 131072 | tf_op jit(solution)/shard_map/all_to_all | solution.py:461
  112.6 1.5 %shard_map.105 = (f32[16,256]{1,0:T(8,128)S(1)}, f32[16,256]{1,0:T(8,128)S(1)}, f32[16,256]{1,0:T(8,128)S(1)}, f32[1,256]{1,0:T(1,128)S(1)}) custom-call(f32[32,4,128]{2,1,0:T(4,128)S(1)} %all_to_all.40.recv_ref.refs_4_, f32[16,256]{1,0:T(8,128)S(1)} %get-tuple-element.168.local_ref, f32[4,256]{1,0:T(4,128)S(1)} %get-tuple-element.169.begins_ref, ...), custom_call_target="tpu_custom_call" | custom-call | tf_op jit(solution)/shard_map/pallas_call | solution.py:393
  114.1 0.7 collective-permute-start.14
  114.7 0.0 collective-permute-start.15
  114.7 1.9 %shard_map.106 = (f32[16,256]{1,0:T(8,128)S(1)}, f32[3,16,256]{2,1,0:T(8,128)S(1)}, f32[1,256]{1,0:T(1,128)S(1)}) custom-call(f32[16,256]{1,0:T(8,128)S(1)} %get-tuple-element.170.value_ref.refs_3_, f32[1,256]{1,0:T(1,128)S(1)} %get-tuple-element.171.entry_ref, f32[32,4,128]{2,1,0:T(4,128)S(1)} %all_to_all.40.recv_ref.refs_4_, ...), custom_call_target="tpu_custom_call" | custom-call | tf_op jit(solution)/shard_map/pallas_call | solution.py:393
  116.6 1.3 collective-permute-done.14.refs_1_
  117.9 0.0 collective-permute-done.15.refs_2_
  117.9 1.1 shard_map.107
  118.9 9.6 %all_to_all.41.recv_ref = f32[32,2,128]{2,1,0:T(2,128)S(1)} all-to-all(f32[32,2,128]{2,1,0:T(2,128)S(1)} %get-tuple-element.178), channel_id=1, replica_groups=mesh['track'=8,'strip'=4] {'strip','track'}, dimensions={0} | all-to-all | bytes 65536 | tf_op jit(solution)/shard_map/all_to_all | solution.py:498
  128.5 0.8 shard_map.108
  (3 shorter events, 0.0 us)
Async XLA Ops:
  8.1 1.7 %collective-permute-start = (f32[256,256]{1,0:T(8,128)S(1)}, f32[256,256]{1,0:T(8,128)S(1)}, u32[]{:S(2)}, u32[]{:S(2)}) collective-permute-start(f32[256,256]{1,0:T(8,128)S(1)} %get-tuple-element.92.total_ref), channel_id=1, source_target_pairs={{0,4},{4,0},{8,12},{12,8},{16,20},{20,16},{24,28},{28,24},{1,5},{5... | collective-permute-start | bytes 786440 | tf_op jit(solution)/shard_map/ppermute | solution.py:435
  10.7 10.2 %collective-permute-start.1 = (f32[256,256]{1,0:T(8,128)S(1)}, f32[256,256]{1,0:T(8,128)S(1)}, u32[]{:S(2)}, u32[]{:S(2)}) collective-permute-start(f32[256,256]{1,0:T(8,128)S(1)} %get-tuple-element.104), channel_id=1, source_target_pairs={{0,4},{4,0},{8,16},{12,28},{16,24},{20,12},{24,8},{28,20},{1,5},{5... | collective-permute-start | bytes 786440 | tf_op jit(solution)/shard_map/ppermute | solution.py:448
  21.0 2.2 %collective-permute-start.2 = (f32[256,256]{1,0:T(8,128)S(1)}, f32[256,256]{1,0:T(8,128)S(1)}, u32[]{:S(2)}, u32[]{:S(2)}) collective-permute-start(f32[256,256]{1,0:T(8,128)S(1)} %collective-permute-done.1.refs_0_), channel_id=1, source_target_pairs={{0,4},{4,0},{8,12},{12,8},{16,20},{20,16},{24,28},{28,24},{1,5},{5... | collective-permute-start | bytes 786440 | tf_op jit(solution)/shard_map/ppermute | solution.py:465
  21.0 8.7 %collective-permute-start.5 = (f32[256,256]{1,0:T(8,128)S(1)}, f32[256,256]{1,0:T(8,128)S(1)}, u32[]{:S(2)}, u32[]{:S(2)}) collective-permute-start(f32[256,256]{1,0:T(8,128)S(1)} %get-tuple-element.118), channel_id=1, source_target_pairs={{4,0},{8,4},{12,8},{16,12},{20,16},{24,20},{28,24},{0,28},{5,1},{9... | collective-permute-start | bytes 786440 | tf_op jit(solution)/shard_map/ppermute | solution.py:464
  23.2 3.4 %copy-start = (f32[1,16,256]{2,1,0:T(8,128)S(1)}, f32[1,16,256]{2,1,0:T(8,128)}, u32[]{:S(2)}) copy-start(f32[1,16,256]{2,1,0:T(8,128)} %param.7) | copy-start | bytes 49156
  23.2 3.4 %copy-start.1 = (s32[1,16]{1,0:T(1,128)S(1)}, s32[1,16]{1,0:T(1,128)}, u32[]{:S(2)}) copy-start(s32[1,16]{1,0:T(1,128)} %refs_17_.1) | copy-start | bytes 196
  24.9 4.8 %collective-permute-start.3 = (f32[16,256]{1,0:T(8,128)S(1)}, f32[16,256]{1,0:T(8,128)S(1)}, u32[]{:S(2)}, u32[]{:S(2)}) collective-permute-start(f32[16,256]{1,0:T(8,128)S(1)} %get-tuple-element.114), channel_id=1, source_target_pairs={{0,1},{1,0},{2,3},{3,2},{4,5},{5,4},{6,7},{7,6},{8,9},{9,8},{10,11... | collective-permute-start | bytes 49160 | tf_op jit(solution)/shard_map/ppermute | solution.py:479
  26.5 3.2 %collective-permute-start.4 = (f32[16,256]{1,0:T(8,128)S(1)}, f32[16,256]{1,0:T(8,128)S(1)}, u32[]{:S(2)}, u32[]{:S(2)}) collective-permute-start(f32[16,256]{1,0:T(8,128)S(1)} %get-tuple-element.115), channel_id=1, source_target_pairs={{0,4},{1,2},{2,1},{3,7},{4,0},{5,6},{6,5},{7,3},{8,12},{9,10},{10,... | collective-permute-start | bytes 49160 | tf_op jit(solution)/shard_map/ppermute | solution.py:480
  45.0 3.8 %collective-permute-start.6 = (f32[16,256]{1,0:T(8,128)S(1)}, f32[16,256]{1,0:T(8,128)S(1)}, u32[]{:S(2)}, u32[]{:S(2)}) collective-permute-start(f32[16,256]{1,0:T(8,128)S(1)} %get-tuple-element.130), channel_id=1, source_target_pairs={{0,1},{1,0},{2,3},{3,2},{4,5},{5,4},{6,7},{7,6},{8,9},{9,8},{10,11... | collective-permute-start | bytes 49160 | tf_op jit(solution)/shard_map/ppermute | solution.py:479
  45.7 3.1 %collective-permute-start.7 = (f32[16,256]{1,0:T(8,128)S(1)}, f32[16,256]{1,0:T(8,128)S(1)}, u32[]{:S(2)}, u32[]{:S(2)}) collective-permute-start(f32[16,256]{1,0:T(8,128)S(1)} %get-tuple-element.131), channel_id=1, source_target_pairs={{0,4},{1,2},{2,1},{3,7},{4,0},{5,6},{6,5},{7,3},{8,12},{9,10},{10,... | collective-permute-start | bytes 49160 | tf_op jit(solution)/shard_map/ppermute | solution.py:480
  62.3 3.8 %collective-permute-start.8 = (f32[16,256]{1,0:T(8,128)S(1)}, f32[16,256]{1,0:T(8,128)S(1)}, u32[]{:S(2)}, u32[]{:S(2)}) collective-permute-start(f32[16,256]{1,0:T(8,128)S(1)} %get-tuple-element.141), channel_id=1, source_target_pairs={{0,1},{1,0},{2,3},{3,2},{4,5},{5,4},{6,7},{7,6},{8,9},{9,8},{10,11... | collective-permute-start | bytes 49160 | tf_op jit(solution)/shard_map/ppermute | solution.py:479
  62.9 3.1 %collective-permute-start.9 = (f32[16,256]{1,0:T(8,128)S(1)}, f32[16,256]{1,0:T(8,128)S(1)}, u32[]{:S(2)}, u32[]{:S(2)}) collective-permute-start(f32[16,256]{1,0:T(8,128)S(1)} %get-tuple-element.142), channel_id=1, source_target_pairs={{0,4},{1,2},{2,1},{3,7},{4,0},{5,6},{6,5},{7,3},{8,12},{9,10},{10,... | collective-permute-start | bytes 49160 | tf_op jit(solution)/shard_map/ppermute | solution.py:480
  79.5 3.8 %collective-permute-start.10 = (f32[16,256]{1,0:T(8,128)S(1)}, f32[16,256]{1,0:T(8,128)S(1)}, u32[]{:S(2)}, u32[]{:S(2)}) collective-permute-start(f32[16,256]{1,0:T(8,128)S(1)} %get-tuple-element.152), channel_id=1, source_target_pairs={{0,1},{1,0},{2,3},{3,2},{4,5},{5,4},{6,7},{7,6},{8,9},{9,8},{10,11... | collective-permute-start | bytes 49160 | tf_op jit(solution)/shard_map/ppermute | solution.py:479
  80.2 3.1 %collective-permute-start.11 = (f32[16,256]{1,0:T(8,128)S(1)}, f32[16,256]{1,0:T(8,128)S(1)}, u32[]{:S(2)}, u32[]{:S(2)}) collective-permute-start(f32[16,256]{1,0:T(8,128)S(1)} %get-tuple-element.153), channel_id=1, source_target_pairs={{0,4},{1,2},{2,1},{3,7},{4,0},{5,6},{6,5},{7,3},{8,12},{9,10},{10,... | collective-permute-start | bytes 49160 | tf_op jit(solution)/shard_map/ppermute | solution.py:480
  96.8 3.8 %collective-permute-start.12 = (f32[16,256]{1,0:T(8,128)S(1)}, f32[16,256]{1,0:T(8,128)S(1)}, u32[]{:S(2)}, u32[]{:S(2)}) collective-permute-start(f32[16,256]{1,0:T(8,128)S(1)} %get-tuple-element.163), channel_id=1, source_target_pairs={{0,1},{1,0},{2,3},{3,2},{4,5},{5,4},{6,7},{7,6},{8,9},{9,8},{10,11... | collective-permute-start | bytes 49160 | tf_op jit(solution)/shard_map/ppermute | solution.py:479
  97.5 3.1 %collective-permute-start.13 = (f32[16,256]{1,0:T(8,128)S(1)}, f32[16,256]{1,0:T(8,128)S(1)}, u32[]{:S(2)}, u32[]{:S(2)}) collective-permute-start(f32[16,256]{1,0:T(8,128)S(1)} %get-tuple-element.164), channel_id=1, source_target_pairs={{0,4},{1,2},{2,1},{3,7},{4,0},{5,6},{6,5},{7,3},{8,12},{9,10},{10,... | collective-permute-start | bytes 49160 | tf_op jit(solution)/shard_map/ppermute | solution.py:480
  114.1 3.8 %collective-permute-start.14 = (f32[16,256]{1,0:T(8,128)S(1)}, f32[16,256]{1,0:T(8,128)S(1)}, u32[]{:S(2)}, u32[]{:S(2)}) collective-permute-start(f32[16,256]{1,0:T(8,128)S(1)} %get-tuple-element.174), channel_id=1, source_target_pairs={{0,1},{1,0},{2,3},{3,2},{4,5},{5,4},{6,7},{7,6},{8,9},{9,8},{10,11... | collective-permute-start | bytes 49160 | tf_op jit(solution)/shard_map/ppermute | solution.py:479
  114.7 3.1 %collective-permute-start.15 = (f32[16,256]{1,0:T(8,128)S(1)}, f32[16,256]{1,0:T(8,128)S(1)}, u32[]{:S(2)}, u32[]{:S(2)}) collective-permute-start(f32[16,256]{1,0:T(8,128)S(1)} %get-tuple-element.175), channel_id=1, source_target_pairs={{0,4},{1,2},{2,1},{3,7},{4,0},{5,6},{6,5},{7,3},{8,12},{9,10},{10,... | collective-permute-start | bytes 49160 | tf_op jit(solution)/shard_map/ppermute | solution.py:480

commit v8 on v7

--- a/solution.py
+++ b/solution.py
@@ -201,7 +201,7 @@
     own, other = total_ref[...], other_ref[...]
     early, late = jnp.where(first_core, own, other), jnp.where(first_core, other, own)
     chip_ref[...] = product(early, late)
-    dots = [jnp.zeros((1, 128), F32)] * 2
+    dots = []
     end = ends_ref[0:1, :]
     carried = times_f32(spread(end), other_ref[...])
     send_ends(end, carried, ends_ref[1:2, :], dots, pos_ref, n_track, send_ref)
@@ -436,7 +436,7 @@
     lower_flip, precond_flip = flip(lower, precond)
     chip, beyond, send = call(
         functools.partial(pair_kernel, n_track),
-        [square, square, (n_track,) + chunk[1:]],
+        [square, square, (n_track, width // 128, 128)],
         [VMEM] * 4 + [SMEM] + [VMEM] * 6,
         total, other, ends, last_two, pos, maps, lower, lower_flip, precond_flip, diag, coupling,
     )

time: 130 us -> 129 us (level)
  no operation moved by 1% of the time
where the time goes in v8:
time: 129 us
  blocking collectives  70 us (54%)
  Pallas kernels  43.1 us (33%)
  starting transfers between devices  8.13 us (6%)
  waiting for transfers between devices  6.34 us (5%)
  between operations  1.44 us (1%)
    all_to_all x6, blocking collectives, body(): lax.all_to_all(send, ('strip', 'track') if step_number else 'track', 0, 0)  60.4 us
    pallas_call x23, Pallas kernels, call(): pl.pallas_call(kernel, out_shape=[pltpu.VMEM(shape, dtype) if math.prod(s...  43.1 us
    all_to_all x1, blocking collectives, body(): recv = lax.all_to_all(send, ('strip', 'track'), 0, 0)  9.6 us
    ppermute x6, waiting for transfers between devices, body(): first = lax.ppermute(first, 'strip', pairs)  6.29 us
    ppermute x6, starting transfers between devices, body(): first = lax.ppermute(first, 'strip', pairs)  4.96 us
  transfers between devices with their start and end apart: 16, of which 5 were waited for; matrix products, arithmetic and copies ran while one was open for 0% of the time, Pallas kernels for 12%

profile of v8, /device:TPU:0, one launch (start us, length us, event | category | flops | bytes accessed | tf_op | source)
XLA Modules:
  0.0 129.1 jit_solution(1127798654179443865)
XLA Ops:
  1.3 0.1 pad_add_fusion.pos_ref.refs_2_.refs_18_
  1.4 6.7 %shard_map.86 = (f32[16,256,256]{2,1,0:T(8,128)S(1)}, f32[256,256]{1,0:T(8,128)S(1)}, f32[256,256]{1,0:T(8,128)S(1)}, f32[16,256]{1,0:T(8,128)S(1)}, f32[2,256]{...) custom-call(f32[16,256]{1,0:T(8,128)} %bitcast.9, ...), custom_call_target="tpu_custom_call" | custom-call | tf_op jit(solution)/shard_map/pallas_call | solution.py:393
  8.1 0.5 collective-permute-start
  8.6 1.1 shard_map.87
  9.8 0.0 collective-permute-done.other_ref.refs_16_
  9.8 0.9 shard_map.88
  10.7 0.4 collective-permute-start.1
  11.1 9.8 %all_to_all.35.recv_ref = f32[8,2,128]{2,1,0:T(2,128)S(1)} all-to-all(f32[8,2,128]{2,1,0:T(2,128)S(1)} %get-tuple-element.102), channel_id=1, replica_groups=mesh['track'=8,'strip'=4] {'track'}, dimensions={0} | all-to-all | bytes 16384 | tf_op jit(solution)/shard_map/all_to_all | solution.py:461
  20.9 0.0 collective-permute-done.1.refs_0_
  20.9 0.0 collective-permute-start.2
  20.9 2.2 %collective-permute-start.5 = (f32[256,256]{1,0:T(8,128)S(1)}, f32[256,256]{1,0:T(8,128)S(1)}, u32[]{:S(2)}, u32[]{:S(2)}) collective-permute-start(f32[256,256]{1,0:T(8,128)S(1)} %get-tuple-element.118), channel_id=1, source_target_pairs={{4,0},{8,4},{12,8},{16,12},{20,16},{24,20},{28,24},{0,28},{5,1},{9... | collective-permute-start | bytes 786440 | tf_op jit(solution)/shard_map/ppermute | solution.py:464
  23.1 0.0 collective-permute-done.2.refs_1_
  23.1 1.7 %shard_map.89 = (f32[16,256]{1,0:T(8,128)S(1)}, f32[16,256]{1,0:T(8,128)S(1)}, f32[16,256]{1,0:T(8,128)S(1)}, f32[1,256]{1,0:T(1,128)S(1)}) custom-call(f32[8,2,128]{2,1,0:T(2,128)S(1)} %all_to_all.35.recv_ref, f32[16,256]{1,0:T(8,128)S(1)} %get-tuple-element.106.local_ref, f32[4,256]{1,0:T(4,128)S(1)} %get-tuple-element.107.begins_ref, ...), custom_call_target="tpu_custom_call" | custom-call | tf_op jit(solution)/shard_map/pallas_call | solution.py:393
  24.8 1.6 %collective-permute-start.3 = (f32[16,256]{1,0:T(8,128)S(1)}, f32[16,256]{1,0:T(8,128)S(1)}, u32[]{:S(2)}, u32[]{:S(2)}) collective-permute-start(f32[16,256]{1,0:T(8,128)S(1)} %get-tuple-element.114), channel_id=1, source_target_pairs={{0,1},{1,0},{2,3},{3,2},{4,5},{5,4},{6,7},{7,6},{8,9},{9,8},{10,11... | collective-permute-start | bytes 49160 | tf_op jit(solution)/shard_map/ppermute | solution.py:479
  26.4 0.0 collective-permute-start.4
  26.4 0.0 copy-done
  26.4 1.9 %shard_map.90 = (f32[16,256]{1,0:T(8,128)S(1)}, f32[3,16,256]{2,1,0:T(8,128)S(1)}, f32[1,256]{1,0:T(1,128)S(1)}) custom-call(f32[16,256]{1,0:T(8,128)S(1)} %get-tuple-element.111.value_ref, f32[1,256]{1,0:T(1,128)S(1)} %get-tuple-element.112.entry_ref, f32[8,2,128]{2,1,0:T(2,128)S(1)} %all_to_all.35.recv_ref, f32[16,256]{1,0:T(8,128)S(1)} %bitcast.10, ...), custom_call_target="tpu_custom_call" | custom-call | tf_op jit(solution)/shard_map/pallas_call | solution.py:393
  28.3 1.2 shard_map.91
  29.5 0.0 collective-permute-done.5.edge_map_ref.refs_8_
  29.6 0.0 collective-permute-done.3.first_ref
  29.6 0.0 collective-permute-done.4.second_ref
  29.6 2.2 %shard_map.92 = (f32[16,256]{1,0:T(8,128)S(1)}, f32[16,256]{1,0:T(8,128)S(1)}, f32[4,256]{1,0:T(4,128)S(1)}, f32[32,4,128]{2,1,0:T(4,128)S(1)}) custom-call(f32[16,256]{1,0:T(8,128)S(1)} %get-tuple-element.113.base_ref, f32[16,256]{1,0:T(8,128)S(1)} %collective-permute-done.3.first_ref, f32[16,256]{1,0:T(8,128)S(1)} %collective-permute-done.4.second_ref, ...), custom_call_target="tpu_custom_call" | custom-call | tf_op jit(solution)/shard_map/pallas_call | solution.py:393
  31.8 11.6 %all_to_all.36.recv_ref = f32[32,4,128]{2,1,0:T(4,128)S(1)} all-to-all(f32[32,4,128]{2,1,0:T(4,128)S(1)} %get-tuple-element.121), channel_id=1, replica_groups=mesh['track'=8,'strip'=4] {'strip','track'}, dimensions={0} | all-to-all | bytes 131072 | tf_op jit(solution)/shard_map/all_to_all | solution.py:461
  43.4 1.5 %shard_map.93 = (f32[16,256]{1,0:T(8,128)S(1)}, f32[16,256]{1,0:T(8,128)S(1)}, f32[16,256]{1,0:T(8,128)S(1)}, f32[1,256]{1,0:T(1,128)S(1)}) custom-call(f32[32,4,128]{2,1,0:T(4,128)S(1)} %all_to_all.36.recv_ref, f32[16,256]{1,0:T(8,128)S(1)} %get-tuple-element.122.local_ref, f32[4,256]{1,0:T(4,128)S(1)} %get-tuple-element.123.begins_ref, ...), custom_call_target="tpu_custom_call" | custom-call | tf_op jit(solution)/shard_map/pallas_call | solution.py:393
  44.9 0.7 collective-permute-start.6
  45.5 0.0 collective-permute-start.7
  45.6 1.9 %shard_map.94 = (f32[16,256]{1,0:T(8,128)S(1)}, f32[3,16,256]{2,1,0:T(8,128)S(1)}, f32[1,256]{1,0:T(1,128)S(1)}) custom-call(f32[16,256]{1,0:T(8,128)S(1)} %get-tuple-element.126.value_ref, f32[1,256]{1,0:T(1,128)S(1)} %get-tuple-element.127.entry_ref, f32[32,4,128]{2,1,0:T(4,128)S(1)} %all_to_all.36.recv_ref, ...), custom_call_target="tpu_custom_call" | custom-call | tf_op jit(solution)/shard_map/pallas_call | solution.py:393
  47.4 1.3 collective-permute-done.6.first_ref
  48.7 0.0 collective-permute-done.7.second_ref
  48.7 2.2 %shard_map.95 = (f32[16,256]{1,0:T(8,128)S(1)}, f32[16,256]{1,0:T(8,128)S(1)}, f32[4,256]{1,0:T(4,128)S(1)}, f32[32,4,128]{2,1,0:T(4,128)S(1)}) custom-call(f32[16,256]{1,0:T(8,128)S(1)} %get-tuple-element.129.base_ref, f32[16,256]{1,0:T(8,128)S(1)} %collective-permute-done.6.first_ref, f32[16,256]{1,0:T(8,128)S(1)} %collective-permute-done.7.second_ref, ...), custom_call_target="tpu_custom_call" | custom-call | tf_op jit(solution)/shard_map/pallas_call | solution.py:393
  50.9 9.8 %all_to_all.37.recv_ref = f32[32,4,128]{2,1,0:T(4,128)S(1)} all-to-all(f32[32,4,128]{2,1,0:T(4,128)S(1)} %get-tuple-element.134), channel_id=1, replica_groups=mesh['track'=8,'strip'=4] {'strip','track'}, dimensions={0} | all-to-all | bytes 131072 | tf_op jit(solution)/shard_map/all_to_all | solution.py:461
  60.6 1.5 %shard_map.96 = (f32[16,256]{1,0:T(8,128)S(1)}, f32[16,256]{1,0:T(8,128)S(1)}, f32[16,256]{1,0:T(8,128)S(1)}, f32[1,256]{1,0:T(1,128)S(1)}) custom-call(f32[32,4,128]{2,1,0:T(4,128)S(1)} %all_to_all.37.recv_ref, f32[16,256]{1,0:T(8,128)S(1)} %get-tuple-element.135.local_ref, f32[4,256]{1,0:T(4,128)S(1)} %get-tuple-element.136.begins_ref, ...), custom_call_target="tpu_custom_call" | custom-call | tf_op jit(solution)/shard_map/pallas_call | solution.py:393
  62.1 0.7 collective-permute-start.8
  62.8 0.0 collective-permute-start.9
  62.8 1.9 %shard_map.97 = (f32[16,256]{1,0:T(8,128)S(1)}, f32[3,16,256]{2,1,0:T(8,128)S(1)}, f32[1,256]{1,0:T(1,128)S(1)}) custom-call(f32[16,256]{1,0:T(8,128)S(1)} %get-tuple-element.137.value_ref, f32[1,256]{1,0:T(1,128)S(1)} %get-tuple-element.138.entry_ref, f32[32,4,128]{2,1,0:T(4,128)S(1)} %all_to_all.37.recv_ref, ...), custom_call_target="tpu_custom_call" | custom-call | tf_op jit(solution)/shard_map/pallas_call | solution.py:393
  64.7 1.3 collective-permute-done.8.first_ref
  65.9 0.0 collective-permute-done.9.second_ref
  65.9 2.2 %shard_map.98 = (f32[16,256]{1,0:T(8,128)S(1)}, f32[16,256]{1,0:T(8,128)S(1)}, f32[4,256]{1,0:T(4,128)S(1)}, f32[32,4,128]{2,1,0:T(4,128)S(1)}) custom-call(f32[16,256]{1,0:T(8,128)S(1)} %get-tuple-element.140.base_ref, f32[16,256]{1,0:T(8,128)S(1)} %collective-permute-done.8.first_ref, f32[16,256]{1,0:T(8,128)S(1)} %collective-permute-done.9.second_ref, ...), custom_call_target="tpu_custom_call" | custom-call | tf_op jit(solution)/shard_map/pallas_call | solution.py:393
  68.1 9.8 %all_to_all.38.recv_ref = f32[32,4,128]{2,1,0:T(4,128)S(1)} all-to-all(f32[32,4,128]{2,1,0:T(4,128)S(1)} %get-tuple-element.145), channel_id=1, replica_groups=mesh['track'=8,'strip'=4] {'strip','track'}, dimensions={0} | all-to-all | bytes 131072 | tf_op jit(solution)/shard_map/all_to_all | solution.py:461
  77.9 1.5 %shard_map.99 = (f32[16,256]{1,0:T(8,128)S(1)}, f32[16,256]{1,0:T(8,128)S(1)}, f32[16,256]{1,0:T(8,128)S(1)}, f32[1,256]{1,0:T(1,128)S(1)}) custom-call(f32[32,4,128]{2,1,0:T(4,128)S(1)} %all_to_all.38.recv_ref, f32[16,256]{1,0:T(8,128)S(1)} %get-tuple-element.146.local_ref, f32[4,256]{1,0:T(4,128)S(1)} %get-tuple-element.147.begins_ref, ...), custom_call_target="tpu_custom_call" | custom-call | tf_op jit(solution)/shard_map/pallas_call | solution.py:393
  79.4 0.7 collective-permute-start.10
  80.0 0.0 collective-permute-start.11
  80.0 1.9 %shard_map.100 = (f32[16,256]{1,0:T(8,128)S(1)}, f32[3,16,256]{2,1,0:T(8,128)S(1)}, f32[1,256]{1,0:T(1,128)S(1)}) custom-call(f32[16,256]{1,0:T(8,128)S(1)} %get-tuple-element.148.value_ref, f32[1,256]{1,0:T(1,128)S(1)} %get-tuple-element.149.entry_ref, f32[32,4,128]{2,1,0:T(4,128)S(1)} %all_to_all.38.recv_ref, ...), custom_call_target="tpu_custom_call" | custom-call | tf_op jit(solution)/shard_map/pallas_call | solution.py:393
  81.9 1.3 collective-permute-done.10.first_ref
  83.2 0.0 collective-permute-done.11.second_ref
  83.2 2.2 %shard_map.101 = (f32[16,256]{1,0:T(8,128)S(1)}, f32[16,256]{1,0:T(8,128)S(1)}, f32[4,256]{1,0:T(4,128)S(1)}, f32[32,4,128]{2,1,0:T(4,128)S(1)}) custom-call(f32[16,256]{1,0:T(8,128)S(1)} %get-tuple-element.151.base_ref, f32[16,256]{1,0:T(8,128)S(1)} %collective-permute-done.10.first_ref, f32[16,256]{1,0:T(8,128)S(1)} %collective-permute-done.11.second_ref, ...), custom_call_target="tpu_custom_call" | custom-call | tf_op jit(solution)/shard_map/pallas_call | solution.py:393
  85.4 9.8 %all_to_all.39.recv_ref = f32[32,4,128]{2,1,0:T(4,128)S(1)} all-to-all(f32[32,4,128]{2,1,0:T(4,128)S(1)} %get-tuple-element.156), channel_id=1, replica_groups=mesh['track'=8,'strip'=4] {'strip','track'}, dimensions={0} | all-to-all | bytes 131072 | tf_op jit(solution)/shard_map/all_to_all | solution.py:461
  95.1 1.5 %shard_map.102 = (f32[16,256]{1,0:T(8,128)S(1)}, f32[16,256]{1,0:T(8,128)S(1)}, f32[16,256]{1,0:T(8,128)S(1)}, f32[1,256]{1,0:T(1,128)S(1)}) custom-call(f32[32,4,128]{2,1,0:T(4,128)S(1)} %all_to_all.39.recv_ref, f32[16,256]{1,0:T(8,128)S(1)} %get-tuple-element.157.local_ref, f32[4,256]{1,0:T(4,128)S(1)} %get-tuple-element.158.begins_ref, ...), custom_call_target="tpu_custom_call" | custom-call | tf_op jit(solution)/shard_map/pallas_call | solution.py:393
  96.6 0.7 collective-permute-start.12
  97.3 0.0 collective-permute-start.13
  97.3 1.9 %shard_map.103 = (f32[16,256]{1,0:T(8,128)S(1)}, f32[3,16,256]{2,1,0:T(8,128)S(1)}, f32[1,256]{1,0:T(1,128)S(1)}) custom-call(f32[16,256]{1,0:T(8,128)S(1)} %get-tuple-element.159.value_ref, f32[1,256]{1,0:T(1,128)S(1)} %get-tuple-element.160.entry_ref, f32[32,4,128]{2,1,0:T(4,128)S(1)} %all_to_all.39.recv_ref, ...), custom_call_target="tpu_custom_call" | custom-call | tf_op jit(solution)/shard_map/pallas_call | solution.py:393
  99.1 1.3 collective-permute-done.12.first_ref
  100.4 0.0 collective-permute-done.13.second_ref
  100.4 2.2 %shard_map.104 = (f32[16,256]{1,0:T(8,128)S(1)}, f32[16,256]{1,0:T(8,128)S(1)}, f32[4,256]{1,0:T(4,128)S(1)}, f32[32,4,128]{2,1,0:T(4,128)S(1)}) custom-call(f32[16,256]{1,0:T(8,128)S(1)} %get-tuple-element.162.base_ref, f32[16,256]{1,0:T(8,128)S(1)} %collective-permute-done.12.first_ref, f32[16,256]{1,0:T(8,128)S(1)} %collective-permute-done.13.second_ref, ...), custom_call_target="tpu_custom_call" | custom-call | tf_op jit(solution)/shard_map/pallas_call | solution.py:393
  102.6 9.8 %all_to_all.40.recv_ref.refs_4_ = f32[32,4,128]{2,1,0:T(4,128)S(1)} all-to-all(f32[32,4,128]{2,1,0:T(4,128)S(1)} %get-tuple-element.167), channel_id=1, replica_groups=mesh['track'=8,'strip'=4] {'strip','track'}, dimensions={0} | all-to-all | bytes 131072 | tf_op jit(solution)/shard_map/all_to_all | solution.py:461
  112.4 1.5 %shard_map.105 = (f32[16,256]{1,0:T(8,128)S(1)}, f32[16,256]{1,0:T(8,128)S(1)}, f32[16,256]{1,0:T(8,128)S(1)}, f32[1,256]{1,0:T(1,128)S(1)}) custom-call(f32[32,4,128]{2,1,0:T(4,128)S(1)} %all_to_all.40.recv_ref.refs_4_, f32[16,256]{1,0:T(8,128)S(1)} %get-tuple-element.168.local_ref, f32[4,256]{1,0:T(4,128)S(1)} %get-tuple-element.169.begins_ref, ...), custom_call_target="tpu_custom_call" | custom-call | tf_op jit(solution)/shard_map/pallas_call | solution.py:393
  113.8 0.7 collective-permute-start.14
  114.5 0.0 collective-permute-start.15
  114.5 1.9 %shard_map.106 = (f32[16,256]{1,0:T(8,128)S(1)}, f32[3,16,256]{2,1,0:T(8,128)S(1)}, f32[1,256]{1,0:T(1,128)S(1)}) custom-call(f32[16,256]{1,0:T(8,128)S(1)} %get-tuple-element.170.value_ref.refs_3_, f32[1,256]{1,0:T(1,128)S(1)} %get-tuple-element.171.entry_ref, f32[32,4,128]{2,1,0:T(4,128)S(1)} %all_to_all.40.recv_ref.refs_4_, ...), custom_call_target="tpu_custom_call" | custom-call | tf_op jit(solution)/shard_map/pallas_call | solution.py:393
  116.4 1.3 collective-permute-done.14.refs_1_
  117.6 0.0 collective-permute-done.15.refs_2_
  117.6 1.1 shard_map.107
  118.7 9.6 %all_to_all.41.recv_ref = f32[32,2,128]{2,1,0:T(2,128)S(1)} all-to-all(f32[32,2,128]{2,1,0:T(2,128)S(1)} %get-tuple-element.178), channel_id=1, replica_groups=mesh['track'=8,'strip'=4] {'strip','track'}, dimensions={0} | all-to-all | bytes 65536 | tf_op jit(solution)/shard_map/all_to_all | solution.py:498
  128.3 0.8 shard_map.108
  (3 shorter events, 0.0 us)
Async XLA Ops:
  8.1 1.7 %collective-permute-start = (f32[256,256]{1,0:T(8,128)S(1)}, f32[256,256]{1,0:T(8,128)S(1)}, u32[]{:S(2)}, u32[]{:S(2)}) collective-permute-start(f32[256,256]{1,0:T(8,128)S(1)} %get-tuple-element.92.total_ref), channel_id=1, source_target_pairs={{0,4},{4,0},{8,12},{12,8},{16,20},{20,16},{24,28},{28,24},{1,5},{5... | collective-permute-start | bytes 786440 | tf_op jit(solution)/shard_map/ppermute | solution.py:435
  10.7 10.2 %collective-permute-start.1 = (f32[256,256]{1,0:T(8,128)S(1)}, f32[256,256]{1,0:T(8,128)S(1)}, u32[]{:S(2)}, u32[]{:S(2)}) collective-permute-start(f32[256,256]{1,0:T(8,128)S(1)} %get-tuple-element.104), channel_id=1, source_target_pairs={{0,4},{4,0},{8,16},{12,28},{16,24},{20,12},{24,8},{28,20},{1,5},{5... | collective-permute-start | bytes 786440 | tf_op jit(solution)/shard_map/ppermute | solution.py:448
  20.9 2.2 %collective-permute-start.2 = (f32[256,256]{1,0:T(8,128)S(1)}, f32[256,256]{1,0:T(8,128)S(1)}, u32[]{:S(2)}, u32[]{:S(2)}) collective-permute-start(f32[256,256]{1,0:T(8,128)S(1)} %collective-permute-done.1.refs_0_), channel_id=1, source_target_pairs={{0,4},{4,0},{8,12},{12,8},{16,20},{20,16},{24,28},{28,24},{1,5},{5... | collective-permute-start | bytes 786440 | tf_op jit(solution)/shard_map/ppermute | solution.py:465
  20.9 8.6 %collective-permute-start.5 = (f32[256,256]{1,0:T(8,128)S(1)}, f32[256,256]{1,0:T(8,128)S(1)}, u32[]{:S(2)}, u32[]{:S(2)}) collective-permute-start(f32[256,256]{1,0:T(8,128)S(1)} %get-tuple-element.118), channel_id=1, source_target_pairs={{4,0},{8,4},{12,8},{16,12},{20,16},{24,20},{28,24},{0,28},{5,1},{9... | collective-permute-start | bytes 786440 | tf_op jit(solution)/shard_map/ppermute | solution.py:464
  23.1 3.3 %copy-start = (f32[1,16,256]{2,1,0:T(8,128)S(1)}, f32[1,16,256]{2,1,0:T(8,128)}, u32[]{:S(2)}) copy-start(f32[1,16,256]{2,1,0:T(8,128)} %param.7) | copy-start | bytes 49156
  23.1 3.3 %copy-start.1 = (s32[1,16]{1,0:T(1,128)S(1)}, s32[1,16]{1,0:T(1,128)}, u32[]{:S(2)}) copy-start(s32[1,16]{1,0:T(1,128)} %refs_17_.1) | copy-start | bytes 196
  24.8 4.8 %collective-permute-start.3 = (f32[16,256]{1,0:T(8,128)S(1)}, f32[16,256]{1,0:T(8,128)S(1)}, u32[]{:S(2)}, u32[]{:S(2)}) collective-permute-start(f32[16,256]{1,0:T(8,128)S(1)} %get-tuple-element.114), channel_id=1, source_target_pairs={{0,1},{1,0},{2,3},{3,2},{4,5},{5,4},{6,7},{7,6},{8,9},{9,8},{10,11... | collective-permute-start | bytes 49160 | tf_op jit(solution)/shard_map/ppermute | solution.py:479
  26.4 3.1 %collective-permute-start.4 = (f32[16,256]{1,0:T(8,128)S(1)}, f32[16,256]{1,0:T(8,128)S(1)}, u32[]{:S(2)}, u32[]{:S(2)}) collective-permute-start(f32[16,256]{1,0:T(8,128)S(1)} %get-tuple-element.115), channel_id=1, source_target_pairs={{0,4},{1,2},{2,1},{3,7},{4,0},{5,6},{6,5},{7,3},{8,12},{9,10},{10,... | collective-permute-start | bytes 49160 | tf_op jit(solution)/shard_map/ppermute | solution.py:480
  44.9 3.8 %collective-permute-start.6 = (f32[16,256]{1,0:T(8,128)S(1)}, f32[16,256]{1,0:T(8,128)S(1)}, u32[]{:S(2)}, u32[]{:S(2)}) collective-permute-start(f32[16,256]{1,0:T(8,128)S(1)} %get-tuple-element.130), channel_id=1, source_target_pairs={{0,1},{1,0},{2,3},{3,2},{4,5},{5,4},{6,7},{7,6},{8,9},{9,8},{10,11... | collective-permute-start | bytes 49160 | tf_op jit(solution)/shard_map/ppermute | solution.py:479
  45.5 3.1 %collective-permute-start.7 = (f32[16,256]{1,0:T(8,128)S(1)}, f32[16,256]{1,0:T(8,128)S(1)}, u32[]{:S(2)}, u32[]{:S(2)}) collective-permute-start(f32[16,256]{1,0:T(8,128)S(1)} %get-tuple-element.131), channel_id=1, source_target_pairs={{0,4},{1,2},{2,1},{3,7},{4,0},{5,6},{6,5},{7,3},{8,12},{9,10},{10,... | collective-permute-start | bytes 49160 | tf_op jit(solution)/shard_map/ppermute | solution.py:480
  62.1 3.8 %collective-permute-start.8 = (f32[16,256]{1,0:T(8,128)S(1)}, f32[16,256]{1,0:T(8,128)S(1)}, u32[]{:S(2)}, u32[]{:S(2)}) collective-permute-start(f32[16,256]{1,0:T(8,128)S(1)} %get-tuple-element.141), channel_id=1, source_target_pairs={{0,1},{1,0},{2,3},{3,2},{4,5},{5,4},{6,7},{7,6},{8,9},{9,8},{10,11... | collective-permute-start | bytes 49160 | tf_op jit(solution)/shard_map/ppermute | solution.py:479
  62.8 3.1 %collective-permute-start.9 = (f32[16,256]{1,0:T(8,128)S(1)}, f32[16,256]{1,0:T(8,128)S(1)}, u32[]{:S(2)}, u32[]{:S(2)}) collective-permute-start(f32[16,256]{1,0:T(8,128)S(1)} %get-tuple-element.142), channel_id=1, source_target_pairs={{0,4},{1,2},{2,1},{3,7},{4,0},{5,6},{6,5},{7,3},{8,12},{9,10},{10,... | collective-permute-start | bytes 49160 | tf_op jit(solution)/shard_map/ppermute | solution.py:480
  79.4 3.8 %collective-permute-start.10 = (f32[16,256]{1,0:T(8,128)S(1)}, f32[16,256]{1,0:T(8,128)S(1)}, u32[]{:S(2)}, u32[]{:S(2)}) collective-permute-start(f32[16,256]{1,0:T(8,128)S(1)} %get-tuple-element.152), channel_id=1, source_target_pairs={{0,1},{1,0},{2,3},{3,2},{4,5},{5,4},{6,7},{7,6},{8,9},{9,8},{10,11... | collective-permute-start | bytes 49160 | tf_op jit(solution)/shard_map/ppermute | solution.py:479
  80.0 3.1 %collective-permute-start.11 = (f32[16,256]{1,0:T(8,128)S(1)}, f32[16,256]{1,0:T(8,128)S(1)}, u32[]{:S(2)}, u32[]{:S(2)}) collective-permute-start(f32[16,256]{1,0:T(8,128)S(1)} %get-tuple-element.153), channel_id=1, source_target_pairs={{0,4},{1,2},{2,1},{3,7},{4,0},{5,6},{6,5},{7,3},{8,12},{9,10},{10,... | collective-permute-start | bytes 49160 | tf_op jit(solution)/shard_map/ppermute | solution.py:480
  96.6 3.8 %collective-permute-start.12 = (f32[16,256]{1,0:T(8,128)S(1)}, f32[16,256]{1,0:T(8,128)S(1)}, u32[]{:S(2)}, u32[]{:S(2)}) collective-permute-start(f32[16,256]{1,0:T(8,128)S(1)} %get-tuple-element.163), channel_id=1, source_target_pairs={{0,1},{1,0},{2,3},{3,2},{4,5},{5,4},{6,7},{7,6},{8,9},{9,8},{10,11... | collective-permute-start | bytes 49160 | tf_op jit(solution)/shard_map/ppermute | solution.py:479
  97.3 3.1 %collective-permute-start.13 = (f32[16,256]{1,0:T(8,128)S(1)}, f32[16,256]{1,0:T(8,128)S(1)}, u32[]{:S(2)}, u32[]{:S(2)}) collective-permute-start(f32[16,256]{1,0:T(8,128)S(1)} %get-tuple-element.164), channel_id=1, source_target_pairs={{0,4},{1,2},{2,1},{3,7},{4,0},{5,6},{6,5},{7,3},{8,12},{9,10},{10,... | collective-permute-start | bytes 49160 | tf_op jit(solution)/shard_map/ppermute | solution.py:480
  113.8 3.8 %collective-permute-start.14 = (f32[16,256]{1,0:T(8,128)S(1)}, f32[16,256]{1,0:T(8,128)S(1)}, u32[]{:S(2)}, u32[]{:S(2)}) collective-permute-start(f32[16,256]{1,0:T(8,128)S(1)} %get-tuple-element.174), channel_id=1, source_target_pairs={{0,1},{1,0},{2,3},{3,2},{4,5},{5,4},{6,7},{7,6},{8,9},{9,8},{10,11... | collective-permute-start | bytes 49160 | tf_op jit(solution)/shard_map/ppermute | solution.py:479
  114.5 3.1 %collective-permute-start.15 = (f32[16,256]{1,0:T(8,128)S(1)}, f32[16,256]{1,0:T(8,128)S(1)}, u32[]{:S(2)}, u32[]{:S(2)}) collective-permute-start(f32[16,256]{1,0:T(8,128)S(1)} %get-tuple-element.175), channel_id=1, source_target_pairs={{0,4},{1,2},{2,1},{3,7},{4,0},{5,6},{6,5},{7,3},{8,12},{9,10},{10,... | collective-permute-start | bytes 49160 | tf_op jit(solution)/shard_map/ppermute | solution.py:480
